TPU v7x, 512 devices: a whole 4x4x16 slice. The times are simulated.
512 devices in a mesh: tm: 8 (over y, core), utt: 64 (over x, z).
Axes of the slice: x: 4, y: 4, z: 16, core: 2. Of those that a mesh axis runs over, the one named last changes fastest.
Arguments:
- encoder: bfloat16 [128, 512, 512], P('utt', 'tm'), may hold values from -16 to 16
- predictor: bfloat16 [128, 65, 512], P('utt'), may hold values from -6 to 6
- starts: int32 [128, 512], P('utt', 'tm'), may hold values from 0 to 49, as said below
- frame_lengths: int32 [128], P('utt'), may hold values from 256 to 512, as said below
- label_lengths: int32 [128], P('utt'), may hold values from 32 to 64, as said below
- labels: int32 [128, 64], P('utt'), may hold values from 1 to 499
- w_out: bfloat16 [512, 500], P('utt'), may hold values from -7 to 7
Outputs:
- losses: float32 [128], P('utt')
- grad_encoder: bfloat16 [128, 512, 512], P('utt', 'tm')
- grad_predictor: float32 [128, 65, 512], P('utt')
- grad_w_out: float32 [512, 500], P('utt')
Inputs may be any that keep to these rules, and one draw needn't show every extreme that they name: `frame_lengths`: some utterance has all 512 frames. `label_lengths`: some utterance has 64 labels. starts[b, 0] = 0; starts never falls along frames and rises by at most 15 from one frame to the next; the ranges hold a complete path of blanks and emissions from label 0 at frame 0 to label label_lengths[b] after the last frame, and every range from frame frame_lengths[b] - 1 on contains label_lengths[b].
All inputs are finite; a program needn't handle non-finite values.
Results may differ from a plain program's by a relative error of at most 0.012.
Values may be sent and summed in bfloat16 or wider, within the bound.
No kernel may reach another device: no remote copies, remote signals or barrier semaphores. Data moves between devices by JAX's collectives and lax.ppermute only.
A program may use at most 64 MiB of HBM per device.

v0:
```python
import jax
import jax.numpy as jnp
from jax import lax
from jax.sharding import PartitionSpec as P

S = 16


masked_log = -1e30


def from_behind(block, axis, distance):
    devices = range(lax.axis_size(axis))
    route = [(i - distance, i) for i in devices if i - distance in devices]
    return lax.ppermute(block, axis, route)


def log_product(former, latter):
    return jax.nn.logsumexp(former[..., :, :, None] + latter[..., None, :, :], axis=-2)


def frame_matrices(blank_lp, emit_lp, shifts):
    size = blank_lp.shape[-1]
    places = jnp.arange(size, dtype=jnp.int32)
    entries = places - shifts[..., None]
    inside = (entries[..., :, None, None] <= places) & (places < places[:, None])
    spans = jnp.sum(jnp.where(inside, emit_lp[..., None, None, :], jnp.float32(0.0)), axis=-1)
    usable = (entries[..., :, None] >= 0) & (entries[..., :, None] <= places)
    return jnp.where(usable, spans + blank_lp[..., None, :], jnp.float32(masked_log))


def chain_product(matrices):
    while matrices.shape[-3] > 1:
        matrices = log_product(matrices[..., 0::2, :, :], matrices[..., 1::2, :, :])
    return matrices[..., 0, :, :]


def log_onehot(index, size):
    places = jnp.arange(size, dtype=jnp.int32)
    return jnp.where(places == index[..., None], jnp.float32(0.0), jnp.float32(masked_log))


def vector_times(boundary, matrices):
    return jax.nn.logsumexp(boundary[..., :, None] + matrices, axis=-2)


def times_vector(matrices, boundary):
    return jax.nn.logsumexp(matrices + boundary[..., None, :], axis=-1)


def per_device(encoder, predictor, starts, frame_lengths, label_lengths, labels, w_out):
    weights = lax.all_gather(w_out, "utt", axis=0, tiled=True)
    utt_count, frame_count, width = encoder.shape
    label_rows = predictor.shape[1]
    label_cap = labels.shape[1]
    vocab = weights.shape[1]
    tm_index = lax.axis_index("tm")
    tm_count = lax.axis_size("tm")
    offsets = jnp.arange(S, dtype=jnp.int32)
    window_rows = starts[:, :, None] + offsets
    flat_rows = window_rows.reshape(utt_count, -1)
    picked = jax.vmap(lambda table, index: jnp.take(table, index, axis=0))(predictor, flat_rows)
    summed = encoder[:, :, None, :].astype(jnp.float32) + picked.reshape(
        utt_count, frame_count, S, width
    ).astype(jnp.float32)
    hidden = jnp.tanh(summed).astype(jnp.bfloat16).reshape(-1, width)
    logits = jnp.dot(hidden, weights, preferred_element_type=jnp.float32)
    log_probs = jax.nn.log_softmax(logits, axis=-1)
    label_ids = jnp.take_along_axis(labels, jnp.minimum(flat_rows, label_cap - 1), axis=1).reshape(
        -1
    )
    vocab_ids = jnp.arange(vocab, dtype=jnp.int32)
    is_label = vocab_ids == label_ids[:, None]
    blank_lp = log_probs[:, 0].reshape(utt_count, frame_count, S)
    emit_lp = jnp.sum(jnp.where(is_label, log_probs, jnp.float32(0.0)), axis=-1).reshape(
        utt_count, frame_count, S
    )
    frame_ids = tm_index * frame_count + jnp.arange(frame_count, dtype=jnp.int32)
    live = frame_ids[None, :, None] < frame_lengths[:, None, None]
    blank_lp = jnp.where(live, blank_lp, jnp.float32(0.0))
    emit_lp = jnp.where(
        live & (window_rows < label_lengths[:, None, None]), emit_lp, jnp.float32(masked_log)
    )
    prior_start = from_behind(starts[:, -1], "tm", 1)
    shifts = starts - jnp.concatenate([prior_start[:, None], starts[:, :-1]], axis=1)
    block, pull_block = jax.vjp(
        lambda blanks, emits: chain_product(frame_matrices(blanks, emits, shifts)),
        blank_lp,
        emit_lp,
    )
    is_final = tm_index == tm_count - 1
    final_place = label_lengths - starts[:, -1]
    opening = log_onehot(jnp.zeros((utt_count,), jnp.int32), S)
    closing = log_onehot(final_place, S)

    def forward_turn(turn_index, boundary):
        moved = from_behind(vector_times(boundary, block), "tm", 1)
        return jnp.where(tm_index == 0, opening, moved)

    incoming = lax.fori_loop(0, tm_count - 1, forward_turn, opening)

    def backward_turn(turn_index, boundary):
        moved = from_behind(times_vector(block, boundary), "tm", -1)
        return jnp.where(is_final, closing, moved)

    outgoing = lax.fori_loop(0, tm_count - 1, backward_turn, closing)
    leaving, pull_leaving = jax.vjp(lambda matrices: vector_times(incoming, matrices), block)
    log_total = jax.nn.logsumexp(leaving + outgoing, axis=-1)
    seed = -jnp.exp(leaving + outgoing - log_total[:, None])
    grad_blank, grad_emit = pull_block(pull_leaving(seed)[0])
    losses = -log_total / frame_lengths.astype(jnp.float32)
    coeff = jnp.where(is_label, grad_emit.reshape(-1)[:, None], jnp.float32(0.0))
    coeff = coeff + jnp.where(vocab_ids == 0, grad_blank.reshape(-1)[:, None], jnp.float32(0.0))
    probs = jnp.exp(log_probs)
    grad_logits = (coeff - probs * jnp.sum(coeff, axis=-1, keepdims=True)).astype(jnp.bfloat16)
    grad_hidden = jnp.einsum("rv,jv->rj", grad_logits, weights, preferred_element_type=jnp.float32)
    hidden_wide = hidden.astype(jnp.float32)
    grad_summed = grad_hidden * (1.0 - hidden_wide * hidden_wide)
    grad_encoder = jnp.sum(grad_summed.reshape(utt_count, frame_count, S, width), axis=2).astype(
        jnp.bfloat16
    )
    row_match = (flat_rows[:, :, None] == jnp.arange(label_rows, dtype=jnp.int32)).astype(
        jnp.bfloat16
    )
    summed_rows = grad_summed.reshape(utt_count, -1, width)
    upper = summed_rows.astype(jnp.bfloat16)
    lower = (summed_rows - upper.astype(jnp.float32)).astype(jnp.bfloat16)
    pred_term = jnp.einsum("brp,brj->bpj", row_match, upper, preferred_element_type=jnp.float32)
    pred_term = pred_term + jnp.einsum(
        "brp,brj->bpj", row_match, lower, preferred_element_type=jnp.float32
    )
    grad_predictor = lax.psum(pred_term, "tm")
    weight_term = jnp.einsum("rj,rv->jv", hidden, grad_logits, preferred_element_type=jnp.float32)
    weight_total = lax.psum(weight_term, "tm")
    grad_w_out = lax.psum_scatter(weight_total, "utt", scatter_dimension=0, tiled=True)
    return (losses, grad_encoder, grad_predictor, grad_w_out)


def solution(mesh):
    return jax.shard_map(
        per_device,
        mesh=mesh,
        in_specs=(
            P("utt", "tm", None),
            P("utt", None, None),
            P("utt", "tm"),
            P("utt"),
            P("utt"),
            P("utt", None),
            P("utt", None),
        ),
        out_specs=(P("utt"), P("utt", "tm", None), P("utt", None, None), P("utt", None)),
        check_vma=False,
    )
```

profile of v0, /device:TPU:1, one launch (start us, length us, event | category | flops | bytes accessed | tf_op | source)
XLA Modules:
  0.0 1068.7 jit_solution(4964846580270922536)
XLA Ops:
  9.0 4.6 collective-permute-start.2
  16.7 80.6 %all_gather.3 = bf16[512,500]{1,0:T(8,128)(2,1)S(1)} all-gather(bf16[8,500]{1,0:T(8,128)(2,1)} %param.17), channel_id=1, replica_groups=mesh['tm'=8,'utt'=64] {'utt'}, dimensions={0}, use_global_device_ids=true | all-gather | bytes 520000 | tf_op jit(solution)/shard_map/all_gather | solution.py:52
  97.3 21.7 %gather_fusion.1 = bf16[2048,512]{1,0:T(8,128)(2,1)} fusion(bf16[2,65,512]{2,0,1:T(2,128)(2,1)S(1)} %copy-done, s32[2048]{0:T(1024)S(1)} %get-tuple-element.190), kind=kCustom, calls=%fused_computation.1 | custom fusion | bytes 4210688 | tf_op jit(solution)/shard_map/vmap(jit(_take))/gather | solution.py:62
  125.0 17.6 %gather_fusion = s32[2048]{0:T(1024)S(1)} fusion(s32[2,64]{1,0:T(2,128)S(1)} %copy-done.1, s32[2048]{0:T(1024)S(1)} %get-tuple-element.191), kind=kCustom, calls=%fused_computation | custom fusion | bytes 32768 | tf_op jit(solution)/shard_map/jit(take_along_axis)/gather | solution.py:69
  170.8 63.4 %while.24 = (s32[]{:T(128)}, f32[2,16]{1,0:T(2,128)S(1)}, pred[]{:T(512)}, f32[2,16,16]{2,1,0:T(8,128)S(1)}, f32[16]{0:T(128)}, /*index=5*/s32[]{:T(128)}) while((s32[]{:T(128)}, f32[2,16]{1,0:T(2,128)S(1)}, pred[]{:T(512)}, f32[2,16,16]{2,1,0:T(8,128)S(1)}, f32[16]{0:T(128)}, /*index=5*/s32[]{:T(128)}) %tuple.74), condition=%wide.region_19.20_spmd.clone, body=%wide.region_16.19_spmd.clone.sunk | while | flops 2722 | bytes 6318 | solution.py:100
  171.1 27.7 %collective-permute-start = (f32[2,16]{1,0:T(2,128)S(1)}, f32[2,16]{1,0:T(2,128)S(1)}, u32[]{:S(2)}, u32[]{:S(2)}) collective-permute-start(f32[2,16]{1,0:T(2,128)S(1)} %log_add_fusion.12), channel_id=1, source_target_pairs={{0,64},{64,128},{128,192},{192,256},{256,320},{320,384},{384,448},... | collective-permute-start | bytes 392 | tf_op jit(solution)/shard_map/while/body/eval_jaxpr/ppermute | solution.py:15
  200.2 4.2 collective-permute-start
  206.0 4.2 collective-permute-start
  211.7 4.2 collective-permute-start
  217.4 4.2 collective-permute-start
  223.1 4.2 collective-permute-start
  228.8 4.2 collective-permute-start
  234.5 37.2 %while.25 = (s32[]{:T(128)}, f32[2,16]{1,0:T(2,128)S(1)}, pred[]{:T(512)}, f32[2,16,16]{2,1,0:T(8,128)S(1)}, s32[2]{0:T(128)S(1)}, /*index=5*/s32[]{:T(128)}) while((s32[]{:T(128)}, f32[2,16]{1,0:T(2,128)S(1)}, pred[]{:T(512)}, f32[2,16,16]{2,1,0:T(8,128)S(1)}, s32[2]{0:T(128)S(1)}, /*index=5*/s32[]{:T(128)}) %tuple.82), condition=%wide.region_25.26_spmd.clone, body=%wide.region_22.25_spmd.clone.sunk | while | flops 2786 | bytes 6262 | solution.py:106
  284.4 4.7 pad.42
  289.1 4.7 pad.43
  297.8 8.5 pad.44
  306.3 8.5 pad.45
  315.9 4.5 fusion.15
  325.9 12.0 %pad.47 = f32[2,32,16,16]{1,3,2,0:T(8,128)} pad(f32[2,16,16,16]{1,3,2,0:T(8,128)S(1)} %copy.21, f32[]{:T(128)} %constant.49.clone.1), padding=0_0_0x0_1_1x0_0_0x0_0_0 | pad | bytes 98308 | tf_op jit(solution)/shard_map/transpose(jvp())/pad | solution.py:34
  341.7 4.4 pad.48
  346.1 4.5 pad.49
  367.3 65.6 %all-reduce.14.cloned.1.call-done = f32[2,65,512]{2,1,0:T(8,128)} async-done(((f32[2,65,512]{2,1,0:T(8,128)}), f32[2,65,512]{2,1,0:T(8,128)}) %all-reduce.14.cloned.1.call-update) | async-done | bytes 266256 | tf_op jit(solution)/shard_map/psum | solution.py:132
  434.8 594.0 %reduce-scatter.2.cloned.1.call-done = f32[8,500]{1,0:T(8,128)} async-done(((f32[512,500]{1,0:T(8,128)}), f32[8,500]{1,0:T(8,128)}) %reduce-scatter.2.cloned.1.call-update) | async-done | bytes 16016 | tf_op jit(solution)/shard_map/reduce_scatter | solution.py:135
  1028.8 32.5 %psum.16 = f32[8,500]{1,0:T(8,128)} all-reduce(f32[8,500]{1,0:T(8,128)} %reduce-scatter.2.cloned.1.call-done), channel_id=1, replica_groups=mesh['tm'=8,'utt'=64] {'tm'}, use_global_device_ids=true, to_apply=%region_45.46 | all-reduce | flops 4000 | bytes 32000 | tf_op jit(solution)/shard_map/psum | solution.py:134
  (277 shorter events, 131.3 us)
Async XLA Ops:
  8.0 89.3 %copy-start = (bf16[2,65,512]{2,0,1:T(2,128)(2,1)S(1)}, bf16[2,65,512]{2,0,1:T(2,128)(2,1)}, u32[]{:S(2)}) copy-start(bf16[2,65,512]{2,0,1:T(2,128)(2,1)} %param.12) | copy-start | bytes 399364
  8.0 424.9 %all-reduce.14.cloned.1.call-start = ((), (), s32[]{:S(2)}) async-start(), calls=%async_computation.1 | async-start | bytes 589824 | tf_op jit(solution)/shard_map/psum | solution.py:132
  9.0 139.3 %collective-permute-start.2 = (s32[2]{0:T(128)S(1)}, s32[2]{0:T(128)S(1)}, u32[]{:S(2)}, u32[]{:S(2)}) collective-permute-start(s32[2]{0:T(128)S(1)} %slice_reduce_fusion.1), channel_id=1, source_target_pairs={{0,64},{64,128},{128,192},{192,256},{256,320},{320,384},{384,448},... | collective-permute-start | bytes 32 | tf_op jit(solution)/shard_map/ppermute | solution.py:15
  14.6 133.9 %copy-start.28 = (pred[16,16]{1,0:T(8,128)(4,1)}, pred[16,16]{1,0:T(8,128)(4,1)S(1)}, u32[]{:S(2)}) copy-start(pred[16,16]{1,0:T(8,128)(4,1)S(1)} %iota_compare_fusion.5) | copy-start | bytes 772
  97.3 23.8 %copy-start.9 = (bf16[512,500]{1,0:T(8,128)(2,1)}, bf16[512,500]{1,0:T(8,128)(2,1)S(1)}, u32[]{:S(2)}) copy-start(bf16[512,500]{1,0:T(8,128)(2,1)S(1)} %all_gather.3) | copy-start | bytes 1536004
  162.8 71.7 %copy-start.31 = (s32[2]{0:T(128)S(1)}, s32[2]{0:T(128)}, u32[]{:S(2)}) copy-start(s32[2]{0:T(128)} %copy-done.30) | copy-start | bytes 28
  162.8 109.2 %copy-start.34 = (s32[2]{0:T(128)S(1)}, s32[2]{0:T(128)}, u32[]{:S(2)}) copy-start(s32[2]{0:T(128)} %param.14) | copy-start | bytes 28
  171.1 28.4 %collective-permute-start = (f32[2,16]{1,0:T(2,128)S(1)}, f32[2,16]{1,0:T(2,128)S(1)}, u32[]{:S(2)}, u32[]{:S(2)}) collective-permute-start(f32[2,16]{1,0:T(2,128)S(1)} %log_add_fusion.12), channel_id=1, source_target_pairs={{0,64},{64,128},{128,192},{192,256},{256,320},{320,384},{384,448},... | collective-permute-start | bytes 392 | tf_op jit(solution)/shard_map/while/body/eval_jaxpr/ppermute | solution.py:15
  200.2 4.9 collective-permute-start
  206.0 4.9 collective-permute-start
  211.7 4.9 collective-permute-start
  217.4 4.9 collective-permute-start
  223.1 4.9 collective-permute-start
  228.8 4.9 collective-permute-start
  234.7 5.4 collective-permute-start.1
  240.5 4.9 collective-permute-start.1
  245.7 4.9 collective-permute-start.1
  251.0 4.9 collective-permute-start.1
  256.2 4.9 collective-permute-start.1
  261.4 4.9 collective-permute-start.1
  266.7 4.9 collective-permute-start.1
  272.9 65.0 %copy-start.5 = (f32[2,32,16,16]{1,3,2,0:T(8,128)S(1)}, f32[2,32,16,16]{1,3,2,0:T(8,128)}, u32[]{:S(2)}) copy-start(f32[2,32,16,16]{1,3,2,0:T(8,128)} %copy-done.4) | copy-start | bytes 196612
  314.7 35.9 %copy-start.27 = (pred[2,64,16]{1,2,0:T(8,128)(4,1)S(1)}, pred[2,64,16]{1,2,0:T(8,128)(4,1)}, u32[]{:S(2)}) copy-start(pred[2,64,16]{1,2,0:T(8,128)(4,1)} %copy-done.26) | copy-start | bytes 6148
  363.3 665.4 %reduce-scatter.2.cloned.1.call-start = ((), (), s32[]{:S(2)}) async-start(), calls=%async_computation.2 | async-start | bytes 1064960 | tf_op jit(solution)/shard_map/reduce_scatter | solution.py:135
  (28 other events, 102.4 us)
Sparse Core Ops, SparseCore 0:
  363.4 69.4 all-reduce.13
Sparse Core Ops, SparseCore 1:
  368.8 659.9 reduce-scatter.1
where the time goes:
time: 1070 us
  waiting for transfers between devices  686 us (64%)
  local copies, waits for them, and re-layouts  119 us (11%)
  blocking collectives  113 us (11%)
  starting transfers between devices  70.8 us (7%)
  other arithmetic  53.7 us (5%)
  between operations  16.4 us (2%)
    reduce_scatter x1, waiting for transfers between devices, per_device(): lax.psum_scatter(weight_total, 'utt', scatter_dimension=0, tiled=True)  594 us
    all_gather x1, blocking collectives, per_device(): weights = lax.all_gather(w_out, 'utt', axis=0, tiled=True)  80.6 us
    ppermute x15, starting transfers between devices, from_behind(): return lax.ppermute(block, axis, route)  70.8 us
    psum x1, waiting for transfers between devices, per_device(): grad_predictor = lax.psum(pred_term, 'tm')  65.6 us
    pad x10, local copies, waits for them, and re-layouts, chain_product(): matrices = log_product(matrices[..., 0::2, :, :], matrices[..., 1::2, :, :])  56.8 us
    psum x1, blocking collectives, per_device(): weight_total = lax.psum(weight_term, 'tm')  32.5 us
    ppermute x15, waiting for transfers between devices, from_behind(): return lax.ppermute(block, axis, route)  26.2 us
    gather x2, local copies, waits for them, and re-layouts, per_device(): jnp.take(table, index, axis=0)  21.7 us
  transfers between devices with their start and end apart: 17, of which 16 were waited for; matrix products, arithmetic and copies ran while one was open for 5% of the time, Pallas kernels for 0%

commit v1 on v0

v1 whole, which is shorter than its diff:
```python
import functools

import jax
import jax.numpy as jnp
from jax import lax
from jax.experimental import pallas as pl
from jax.experimental.pallas import tpu as pltpu
from jax.sharding import PartitionSpec as P

S = 16
LANES = 128
GROUP = 4
STEPS = S // GROUP
WIDE = GROUP * LANES
PRED_PAD = 80
PRED_SHARE = 17
PRED_SLOT = 32
VMEM_BYTES = 40 * 2**20

masked_log = -1e30

F32 = jnp.float32
BF16 = jnp.bfloat16

NT_DIMS = (((1,), (1,)), ((), ()))


def lane_ids(shape=(1, LANES)):
    return lax.broadcasted_iota(jnp.int32, shape, 1)


def row_ids(shape):
    return lax.broadcasted_iota(jnp.int32, shape, 0)


def per_lane(half, low, high):
    return jnp.where(lane_ids() < half, low, high)


def rows_to_lanes(pair):
    return jnp.concatenate([pair[0:1, :], pair[1:2, :]], axis=1)


def rowwise_logsumexp(terms):
    top = functools.reduce(jnp.maximum, terms)
    total = functools.reduce(lambda a, b: a + b, [jnp.exp(t - top) for t in terms])
    return top + jnp.log(total)


def vector_times(vector, matrix):
    return rowwise_logsumexp([vector[i : i + 1, :] + matrix[i] for i in range(S)])


def times_vector(matrix, vector, rows_ref):
    for i in range(S):
        terms = matrix[i] + vector
        top = jnp.max(terms, axis=0, keepdims=True)
        total = jnp.sum(jnp.exp(terms - top), axis=0, keepdims=True)
        rows_ref[i : i + 1, :] = top + jnp.log(total)
    return rows_ref[...]


def span_rows(blank, emit):
    places = row_ids((S, LANES))
    spans = jnp.zeros((S, LANES), F32)
    rows = [None] * S
    for e in reversed(range(S)):
        spans = jnp.where(places > e, spans + emit[e : e + 1, :], 0.0)
        rows[e] = jnp.where(places >= e, spans + blank, masked_log)
    return rows


def hidden_kernel(starts_ref, labels_ref, enc_ref, pred_ref, hidden_ref, label_ref, enc_t, pred_t, stack):
    step = pl.program_id(0)
    half = starts_ref.shape[1]
    starts = rows_to_lanes(starts_ref[...])

    @pl.when(step == 0)
    def _():
        enc_t[...] = jnp.transpose(enc_ref[...].astype(F32))
        stack[...] = jnp.zeros_like(stack)
        rows = pred_ref.shape[1]
        stack[0:rows, :] = pred_ref[0].astype(F32)
        stack[PRED_PAD : PRED_PAD + rows, :] = pred_ref[1].astype(F32)
        pred_t[...] = jnp.transpose(stack[...]).astype(BF16)
        cap = labels_ref.shape[1]
        labels = labels_ref[...].astype(F32)
        table = [jnp.transpose(jnp.broadcast_to(labels[b : b + 1, :], (LANES, cap))) for b in range(2)]
        table = jnp.where(lane_ids((cap, LANES)) < half, table[0], table[1])
        places = row_ids((cap, LANES))
        for k in range(S):
            wanted = jnp.minimum(starts + k, cap - 1)
            label_ref[k : k + 1, :] = jnp.sum(
                jnp.where(places == wanted, table, 0.0), axis=0, keepdims=True
            ).astype(jnp.int32)

    base = starts + per_lane(half, 0, PRED_PAD) + step * GROUP
    wanted = jnp.concatenate([base + k for k in range(GROUP)], axis=1)
    match = (row_ids((2 * PRED_PAD, WIDE)) == wanted).astype(BF16)
    picked = jnp.dot(pred_t[...], match, preferred_element_type=F32)
    for k in range(GROUP):
        part = slice(k * LANES, (k + 1) * LANES)
        hidden_ref[:, part] = jnp.tanh(enc_t[...] + picked[:, part]).astype(BF16)


def forward_kernel(
    piece,
    vocab,
    starts_ref,
    prior_ref,
    frames_ref,
    labels_len_ref,
    block_ref,
    label_ref,
    gathered_ref,
    hidden_ref,
    exps_ref,
    weights_ref,
    lps_ref,
    tree_ref,
    payload_ref,
    weights_t,
    root,
):
    step = pl.program_id(0)
    width = gathered_ref.shape[0]

    @pl.when(step == 0)
    def _():
        own = row_ids((width, width))
        got = lane_ids((width, width))
        share = width // 8
        source = (got % share) // piece * (8 * piece) + got // share * piece + got % piece
        turn = (own == source).astype(BF16)
        weights = jnp.dot(turn, gathered_ref[...], preferred_element_type=F32)
        weights_ref[...] = weights.astype(BF16)
        weights_t[...] = jnp.transpose(weights).astype(BF16)

    logits = jnp.dot(weights_t[...], hidden_ref[...], preferred_element_type=F32)
    padded = logits.shape[0]
    edge = padded - 16
    tail = jnp.where(row_ids((16, WIDE)) < vocab - edge, logits[edge:], masked_log)
    logits = jnp.concatenate([logits[:edge], tail], axis=0)
    top = jnp.max(logits, axis=0, keepdims=True)
    exps = jnp.exp(logits - top)
    exps_ref[...] = exps
    total = jnp.sum(exps, axis=0, keepdims=True)
    norm = top + jnp.log(total)
    scale = 1.0 / total
    names = jnp.concatenate([label_ref[pl.ds(step * GROUP + k, 1), :] for k in range(GROUP)], axis=1)
    emit = jnp.sum(jnp.where(row_ids((padded, WIDE)) == names, logits, 0.0), axis=0, keepdims=True) - norm
    blank = logits[0:1, :] - norm
    for k in range(GROUP):
        part = slice(k * LANES, (k + 1) * LANES)
        row = pl.ds(step * GROUP + k, 1)
        lps_ref[0, row, :] = blank[:, part]
        lps_ref[1, row, :] = emit[:, part]
        lps_ref[2, row, :] = scale[:, part]

    @pl.when(step == STEPS - 1)
    def _():
        half = starts_ref.shape[1]
        lanes = lane_ids()
        starts = rows_to_lanes(starts_ref[...])
        frame = block_ref[0] * half + lanes % half
        live = frame < per_lane(half, frames_ref[0], frames_ref[1])
        limit = per_lane(half, labels_len_ref[0], labels_len_ref[1])
        allowed = live & (row_ids((S, LANES)) + starts < limit)
        blank = jnp.where(live, lps_ref[0], 0.0)
        emit = jnp.where(allowed, lps_ref[1], masked_log)
        lps_ref[0] = blank
        lps_ref[1] = emit
        before = pltpu.roll(starts, 1, 1)
        before = jnp.where(lanes == 0, prior_ref[0], jnp.where(lanes == half, prior_ref[1], before))
        shift = starts - before
        rows = span_rows(blank, emit)
        for bit in (1, 2, 4, 8):
            moved = (shift & bit) != 0
            rows = [
                jnp.where(moved, rows[i - bit] if i >= bit else masked_log, rows[i]) for i in range(S)
            ]
        for i in range(S):
            tree_ref[0, i] = rows[i]
        levels = half.bit_length() - 1
        for level in range(levels):
            reach = 1 << level
            latter = [pltpu.roll(tree_ref[level, m], LANES - reach, 1) for m in range(S)]

            def product(i, carry, level=level, latter=latter):
                former = tree_ref[level, i]
                row = rowwise_logsumexp([former[m : m + 1, :] + latter[m] for m in range(S)])
                if level + 1 < levels:
                    tree_ref[level + 1, i] = row
                else:
                    root[i] = row
                return carry

            lax.fori_loop(0, S, product, 0)
        flat = jnp.transpose(root[...].reshape(S * S, LANES))
        payload_ref[...] = jnp.zeros_like(payload_ref)
        for b in range(2):
            line = flat[b * half : b * half + 1, :]
            payload_ref[4 * b : 4 * b + 1, :] = line[:, :LANES]
            payload_ref[4 * b + 1 : 4 * b + 2, :] = line[:, LANES:]
            last = starts_ref[b : b + 1, half - 1 : half].astype(F32)
            payload_ref[4 * b + 2 : 4 * b + 3, :] = jnp.broadcast_to(last, (1, LANES))


def backward_kernel(
    piece,
    vocab,
    starts_ref,
    prior_ref,
    frames_ref,
    labels_len_ref,
    block_ref,
    blocks_ref,
    lps_ref,
    tree_ref,
    label_ref,
    weights_ref,
    hidden_ref,
    exps_ref,
    losses_ref,
    grad_enc_ref,
    send_ref,
    chain,
    line_up,
    rows_ref,
    grads,
    enc_sum,
    pred_sum,
    weight_sum,
):
    step = pl.program_id(0)
    half = starts_ref.shape[1]
    width = weights_ref.shape[0]
    count = blocks_ref.shape[0]
    lanes = lane_ids()

    @pl.when(step == 0)
    def _():
        places = row_ids((S, LANES))
        line_up[...] = jnp.zeros_like(line_up)
        for r in range(count):
            for b in range(2):
                at = 2 * r + b
                line_up[at : at + 1, :LANES] = blocks_ref[r, 4 * b : 4 * b + 1, :]
                line_up[at : at + 1, LANES:] = blocks_ref[r, 4 * b + 1 : 4 * b + 2, :]
        chain[...] = jnp.transpose(line_up[...]).reshape(S, S, LANES)
        odd = lanes % 2 == 1
        last_start = [blocks_ref[count - 1, 4 * b + 2 : 4 * b + 3, :].astype(jnp.int32) for b in range(2)]
        final_place = jnp.where(odd, labels_len_ref[1] - last_start[1], labels_len_ref[0] - last_start[0])
        forward = jnp.where(places == 0, 0.0, masked_log) + jnp.zeros((S, LANES), F32)
        closing = jnp.where(places == final_place, 0.0, masked_log)
        backward = closing
        owner = lanes // 2
        for turn in range(count - 1):
            ahead = pltpu.roll(vector_times(forward, chain), 2, 1)
            forward = jnp.where(owner == turn + 1, ahead, forward)
            behind = pltpu.roll(times_vector(chain, backward, rows_ref), LANES - 2, 1)
            backward = jnp.where(owner == count - 2 - turn, behind, backward)
        leaving = vector_times(forward, chain) + closing
        best = jnp.max(leaving, axis=0, keepdims=True)
        log_total = best + jnp.log(jnp.sum(jnp.exp(leaving - best), axis=0, keepdims=True))
        for b in range(2):
            own_total = jnp.sum(jnp.where(lanes == 2 * (count - 1) + b, log_total, 0.0))
            losses_ref[b] = -own_total / frames_ref[b].astype(F32)

        def own_boundary(vectors):
            columns = [
                jnp.sum(jnp.where(lanes == 2 * block_ref[0] + b, vectors, 0.0), axis=1, keepdims=True)
                for b in range(2)
            ]
            spread = jnp.where(lanes < half, columns[0], columns[1])
            return spread - jnp.max(spread, axis=0, keepdims=True)

        alpha = own_boundary(forward)
        beta = own_boundary(backward)
        levels = half.bit_length() - 1
        for level in reversed(range(levels)):
            reach = 1 << level
            later = lanes % (2 * reach) == reach
            ahead = pltpu.roll(vector_times(alpha, tree_ref.at[level]), reach, 1)
            alpha = jnp.where(later, ahead, alpha)
            beta_late = pltpu.roll(beta, reach, 1)
            behind = times_vector(tree_ref.at[level], beta_late, rows_ref)
            beta = jnp.where(later, beta_late, pltpu.roll(behind, LANES - reach, 1))
        starts = rows_to_lanes(starts_ref[...])
        before = pltpu.roll(starts, 1, 1)
        before = jnp.where(lanes == 0, prior_ref[0], jnp.where(lanes == half, prior_ref[1], before))
        shift = starts - before
        for bit in (1, 2, 4, 8):
            moved = jnp.where(places < S - bit, pltpu.roll(alpha, S - bit, 0), masked_log)
            alpha = jnp.where((shift & bit) != 0, moved, alpha)
        spans = span_rows(lps_ref[0], lps_ref[1])
        scores = [spans[e] + alpha[e : e + 1, :] + beta for e in range(S)]
        best = jnp.max(functools.reduce(jnp.maximum, scores), axis=0, keepdims=True)
        weights = [jnp.exp(score - best) for score in scores]
        for e in range(1, S):
            weights[e] = weights[e] + weights[e - 1]
        total = jnp.sum(weights[S - 1], axis=0, keepdims=True)
        negative = -1.0 / total
        grads[0] = weights[S - 1] * negative
        for m in range(S):
            crossing = jnp.sum(jnp.where(places > m, weights[m], 0.0), axis=0, keepdims=True)
            grads[1, m : m + 1, :] = crossing * negative
        enc_sum[...] = jnp.zeros_like(enc_sum)
        pred_sum[...] = jnp.zeros_like(pred_sum)
        weight_sum[...] = jnp.zeros_like(weight_sum)

    def wide(ref, *lead):
        return jnp.concatenate([ref[(*lead, pl.ds(step * GROUP + k, 1), slice(None))] for k in range(GROUP)], axis=1)

    names = wide(label_ref)
    grad_blank = wide(grads, 0)
    grad_emit = wide(grads, 1)
    spread = (grad_blank + grad_emit) * wide(lps_ref, 2)
    padded = exps_ref.shape[0]
    ids = row_ids((padded, WIDE))
    coeff = jnp.where(ids == names, grad_emit, jnp.where(ids == 0, grad_blank, 0.0))
    grad_logits = (coeff - exps_ref[...] * spread).astype(BF16)
    grad_hidden = jnp.dot(weights_ref[...], grad_logits, preferred_element_type=F32)
    hidden = hidden_ref[...]
    hidden_wide = hidden.astype(F32)
    grad_summed = grad_hidden * (1.0 - hidden_wide * hidden_wide)
    enc_sum[...] += functools.reduce(
        lambda a, b: a + b, [grad_summed[:, k * LANES : (k + 1) * LANES] for k in range(GROUP)]
    )
    starts = rows_to_lanes(starts_ref[...])
    base = starts + step * GROUP
    rows = jnp.concatenate([base + k for k in range(GROUP)], axis=1)
    second = jnp.concatenate([per_lane(half, 0, 65)] * GROUP, axis=1)
    slot = row_ids((8 * PRED_SLOT, WIDE))
    wanted = rows + second
    match = (slot // PRED_SLOT * PRED_SHARE + slot % PRED_SLOT == wanted) & (slot % PRED_SLOT < PRED_SHARE)
    pred_sum[...] += lax.dot_general(
        match.astype(BF16), grad_summed.astype(BF16), NT_DIMS, preferred_element_type=F32
    )
    weight_sum[...] += lax.dot_general(hidden, grad_logits, NT_DIMS, preferred_element_type=F32)

    @pl.when(step == STEPS - 1)
    def _():
        grad_enc_ref[...] = jnp.transpose(enc_sum[...]).astype(BF16)
        share = width // 8
        got = row_ids((width, width))
        source = (got % share) // piece * (8 * piece) + got // share * piece + got % piece
        turn = (lane_ids((width, width)) == source).astype(BF16)
        turned = jnp.dot(turn, weight_sum[...].astype(BF16), preferred_element_type=F32).astype(BF16)
        for p in range(8):
            send_ref[p, 0:share, :] = turned[p * share : (p + 1) * share, :]
            send_ref[p, share : share + PRED_SLOT, :] = pred_sum[p * PRED_SLOT : (p + 1) * PRED_SLOT, :].astype(BF16)


def params():
    return pltpu.CompilerParams(dimension_semantics=("arbitrary",), vmem_limit_bytes=VMEM_BYTES)


def whole(shape):
    return pl.BlockSpec(shape, lambda i: (0,) * len(shape))


smem = pl.BlockSpec(memory_space=pltpu.SMEM)


def from_behind(block, axis, distance):
    devices = range(lax.axis_size(axis))
    route = [(i - distance, i) for i in devices if i - distance in devices]
    return lax.ppermute(block, axis, route)


def per_device(encoder, predictor, starts, frame_lengths, label_lengths, labels, w_out):
    utt_count, frame_count, width = encoder.shape
    own_rows, vocab = w_out.shape
    tm_index = lax.axis_index("tm")
    tm_count = lax.axis_size("tm")
    utt_size = lax.axis_size("utt")
    piece = own_rows // tm_count
    padded = -(-vocab // LANES) * LANES
    share = width // tm_count
    rows = S * utt_count * frame_count
    shape = jax.ShapeDtypeStruct

    mine = lax.dynamic_slice_in_dim(w_out, tm_index * piece, piece, axis=0)
    mine = jnp.pad(mine, ((0, 0), (0, padded - vocab)))
    across = lax.all_to_all(
        jnp.broadcast_to(mine.reshape(1, piece * padded // LANES, LANES), (utt_size, piece * padded // LANES, LANES)),
        "utt", 0, 0, tiled=True,
    )
    gathered = lax.all_gather(across.reshape(share, padded), "tm", axis=0, tiled=True)
    prior = from_behind(starts[:, -1], "tm", 1)
    block = tm_index.reshape(1).astype(jnp.int32)

    hidden, label_ids = pl.pallas_call(
        hidden_kernel,
        grid=(STEPS,),
        in_specs=[
            whole(starts.shape),
            whole(labels.shape),
            whole((utt_count * frame_count, width)),
            whole(predictor.shape),
        ],
        out_specs=[pl.BlockSpec((width, WIDE), lambda i: (0, i)), whole((S, LANES))],
        out_shape=[shape((width, rows), BF16), shape((S, LANES), jnp.int32)],
        scratch_shapes=[
            pltpu.VMEM((width, LANES), F32),
            pltpu.VMEM((width, 2 * PRED_PAD), BF16),
            pltpu.VMEM((2 * PRED_PAD, width), F32),
        ],
        compiler_params=params(),
        cost_estimate=pl.CostEstimate(
            flops=2 * 2 * PRED_PAD * width * rows, bytes_accessed=3 * 2**20, transcendentals=width * rows
        ),
    )(starts, labels, encoder.reshape(-1, width), predictor)

    levels = frame_count.bit_length() - 1
    exps, weights, lps, tree, payload = pl.pallas_call(
        functools.partial(forward_kernel, piece, vocab),
        grid=(STEPS,),
        in_specs=[
            whole(starts.shape),
            smem,
            smem,
            smem,
            smem,
            whole((S, LANES)),
            whole((width, padded)),
            pl.BlockSpec((width, WIDE), lambda i: (0, i)),
        ],
        out_specs=[
            pl.BlockSpec((padded, WIDE), lambda i: (0, i)),
            whole((width, padded)),
            whole((3, S, LANES)),
            whole((levels, S, S, LANES)),
            whole((8, LANES)),
        ],
        out_shape=[
            shape((padded, rows), F32),
            shape((width, padded), BF16),
            shape((3, S, LANES), F32),
            shape((levels, S, S, LANES), F32),
            shape((8, LANES), F32),
        ],
        scratch_shapes=[pltpu.VMEM((padded, width), BF16), pltpu.VMEM((S, S, LANES), F32)],
        compiler_params=params(),
        cost_estimate=pl.CostEstimate(
            flops=2 * padded * width * rows, bytes_accessed=8 * 2**20, transcendentals=padded * rows
        ),
    )(starts, prior, frame_lengths, label_lengths, block, label_ids, gathered, hidden)

    blocks = lax.all_gather(payload, "tm", axis=0)

    losses, grad_encoder, send = pl.pallas_call(
        functools.partial(backward_kernel, piece, vocab),
        grid=(STEPS,),
        in_specs=[
            whole(starts.shape),
            smem,
            smem,
            smem,
            smem,
            whole((tm_count, 8, LANES)),
            whole((3, S, LANES)),
            whole((levels, S, S, LANES)),
            whole((S, LANES)),
            whole((width, padded)),
            pl.BlockSpec((width, WIDE), lambda i: (0, i)),
            pl.BlockSpec((padded, WIDE), lambda i: (0, i)),
        ],
        out_specs=[smem, whole((utt_count * frame_count, width)), whole((tm_count, share + PRED_SLOT, padded))],
        out_shape=[
            shape((utt_count,), F32),
            shape((utt_count * frame_count, width), BF16),
            shape((tm_count, share + PRED_SLOT, padded), BF16),
        ],
        scratch_shapes=[
            pltpu.VMEM((S, S, LANES), F32),
            pltpu.VMEM((LANES, S * S), F32),
            pltpu.VMEM((S, LANES), F32),
            pltpu.VMEM((2, S, LANES), F32),
            pltpu.VMEM((width, LANES), F32),
            pltpu.VMEM((8 * PRED_SLOT, width), F32),
            pltpu.VMEM((width, padded), F32),
        ],
        compiler_params=params(),
        cost_estimate=pl.CostEstimate(
            flops=6 * padded * width * rows, bytes_accessed=8 * 2**20, transcendentals=2**16
        ),
    )(starts, prior, frame_lengths, label_lengths, block, blocks, lps, tree, label_ids, weights, hidden, exps)

    came = lax.all_to_all(send, "tm", 0, 0, tiled=True)
    block_sum = jnp.sum(came.astype(F32), axis=0)
    weight_rows = block_sum[:share].reshape(utt_size, piece * padded // LANES, LANES)
    pred_rows = block_sum[share : share + PRED_SHARE]
    across = lax.all_to_all(weight_rows, "utt", 0, 0, tiled=True)
    own_weight = jnp.sum(across, axis=0).reshape(piece, padded)
    final = lax.all_gather(jnp.concatenate([pred_rows, own_weight], axis=0), "tm", axis=0)
    label_rows = predictor.shape[1]
    grad_predictor = final[:, :PRED_SHARE].reshape(-1, width)[: utt_count * label_rows]
    grad_predictor = grad_predictor.reshape(utt_count, label_rows, width)
    grad_w_out = final[:, PRED_SHARE:, :vocab].reshape(own_rows, vocab)
    return (losses, grad_encoder.reshape(encoder.shape), grad_predictor, grad_w_out)


def solution(mesh):
    return jax.shard_map(
        per_device,
        mesh=mesh,
        in_specs=(
            P("utt", "tm", None),
            P("utt", None, None),
            P("utt", "tm"),
            P("utt"),
            P("utt"),
            P("utt", None),
            P("utt", None),
        ),
        out_specs=(P("utt"), P("utt", "tm", None), P("utt", None, None), P("utt", None)),
        check_vma=False,
    )
```

time: 1070 us -> 140 us (0.13)
  waiting for transfers between devices: 686 us -> 17.5 us
  local copies, waits for them, and re-layouts: 119 us -> 7.74 us
  other arithmetic: 53.7 us -> 0.19 us
  blocking collectives: 113 us -> 60.5 us
  starting transfers between devices: 70.8 us -> 31.2 us
  Pallas kernels: 0 us -> 21.8 us
  between operations: 16.4 us -> 0.79 us
    reduce_scatter x1 -> x0, waiting for transfers between devices: 594 us -> none  [per_device(): lax.psum_scatter(weight_total, 'utt', scatter_dimension=0, tiled=True)]
    ppermute x15 -> x1, starting transfers between devices: 70.8 us -> 4.04 us  [from_behind(): return lax.ppermute(block, axis, route)]
    psum x1 -> x0, waiting for transfers between devices: 65.6 us -> none  [per_device(): grad_predictor = lax.psum(pred_term, 'tm')]
    pad x10 -> x1, local copies, waits for them, and re-layouts: 56.8 us -> 0.02 us  [per_device(): mine = jnp.pad(mine, ((0, 0), (0, padded - vocab)))]
    gather x3 -> x0, local copies, waits for them, and re-layouts: 39.2 us -> none  [the longest x2 21.7 us: per_device(): jnp.take(table, index, axis=0)]
    all_gather x1 -> x3, blocking collectives: 80.6 us -> 44.6 us  [the longest x1 16.2 us: per_device(): lax.all_gather(jnp.concatenate([pred_rows, own_weight], axis=0), 'tm', ax...]
    psum x1 -> x0, blocking collectives: 32.5 us -> none  [per_device(): weight_total = lax.psum(weight_term, 'tm')]
    reduce_sum x34 -> x2, other arithmetic: 30.4 us -> 0.18 us  [the longest x1 0.11 us: per_device(): block_sum = jnp.sum(came.astype(F32), axis=0)]
  transfers between devices with their start and end apart: 17 -> 3, of which waited for: 16 -> 2; matrix products, arithmetic and copies ran while one was open for 5% -> 1% of each run, Pallas kernels for 0% -> 1%
where the time goes in v1:
time: 140 us
  blocking collectives  60.5 us (43%)
  starting transfers between devices  31.2 us (22%)
  Pallas kernels  21.8 us (16%)
  waiting for transfers between devices  17.5 us (12%)
  local copies, waits for them, and re-layouts  7.74 us (6%)
    all_to_all x1, starting transfers between devices, per_device(): lax.all_to_all(jnp.broadcast_to(mine.reshape(1, piece * padded // LANES,...  19.1 us
    all_gather x1, blocking collectives, per_device(): lax.all_gather(jnp.concatenate([pred_rows, own_weight], axis=0), 'tm', ax...  16.2 us
    all_to_all x1, blocking collectives, per_device(): came = lax.all_to_all(send, 'tm', 0, 0, tiled=True)  15.9 us
    all_gather x1, blocking collectives, per_device(): lax.all_gather(across.reshape(share, padded), 'tm', axis=0, tiled=True)  15.6 us
    all_to_all x1, waiting for transfers between devices, per_device(): across = lax.all_to_all(weight_rows, 'utt', 0, 0, tiled=True)  13.9 us
    all_gather x1, blocking collectives, per_device(): blocks = lax.all_gather(payload, 'tm', axis=0)  12.8 us
    pallas_call x1, Pallas kernels, per_device(): pl.pallas_call(functools.partial(forward_kernel, piece, vocab), grid=(STE...  10.8 us
    pallas_call x1, Pallas kernels, per_device(): pl.pallas_call(functools.partial(backward_kernel, piece, vocab), grid=(ST...  9.18 us
  transfers between devices with their start and end apart: 3, of which 2 were waited for; matrix products, arithmetic and copies ran while one was open for 1% of the time, Pallas kernels for 1%

profile of v1, /device:TPU:1, one launch (start us, length us, event | category | flops | bytes accessed | tf_op | source)
XLA Modules:
  0.0 139.8 jit_solution(7530008329822634314)
XLA Ops:
  0.7 0.7 copy-done
  1.4 0.6 broadcast_in_dim.8
  2.0 19.1 %all-to-all-start = ((bf16[64,4,128]{2,1,0:T(4,128)(2,1)}), bf16[64,4,128]{2,1,0:T(4,128)(2,1)S(1)}, u32[]{:S(2)}, u32[]{:S(2)}) async-start(bf16[64,4,128]{2,1,0:T(4,128)(2,1)} %broadcast_in_dim.8), calls=%async_computation | async-start | bytes 131072 | tf_op jit(solution)/shard_map/all_to_all | solution.py:386
  21.1 0.9 slice_reduce_fusion
  22.0 4.0 %collective-permute-start = (s32[2]{0:T(128)S(1)}, s32[2]{0:T(128)S(1)}, u32[]{:S(2)}, u32[]{:S(2)}) collective-permute-start(s32[2]{0:T(128)S(1)} %slice_reduce_fusion), channel_id=1, source_target_pairs={{0,64},{64,128},{128,192},{192,256},{256,320},{320,384},{384,448},... | collective-permute-start | bytes 32 | tf_op jit(solution)/shard_map/ppermute | solution.py:369
  26.0 0.9 copy.15.pred_ref
  27.0 0.9 copy-done.1
  27.9 0.7 copy-done.2
  28.6 0.7 copy-done.3
  29.2 1.9 %shard_map.102 = (bf16[512,2048]{1,0:T(8,128)(2,1)S(1)}, s32[16,128]{1,0:T(8,128)S(1)}) custom-call(s32[2,64]{1,0:T(2,128)S(1)} %copy-done.3, s32[2,64]{1,0:T(2,128)S(1)} %copy-done.2, bf16[128,512]{1,0:T(8,128)(2,1)S(1)} %bitcast.18, bf16[2,65,512]{2,1,0:T(8,128)(2,1)S(1)} %copy.15.pred_ref), custom_call_target="tpu_custom_call" | custom-call | flops 335544320 | bytes 3145728 | tf_op jit(solution)/shard_map/pallas_call | solution.py:394
  31.1 3.5 %all-to-all-done = bf16[64,4,128]{2,1,0:T(4,128)(2,1)S(1)} async-done(((bf16[64,4,128]{2,1,0:T(4,128)(2,1)}), bf16[64,4,128]{2,1,0:T(4,128)(2,1)S(1)}, u32[]{:S(2)}, u32[]{:S(2)}) %all-to-all-start) | async-done | bytes 65568 | tf_op jit(solution)/shard_map/all_to_all | solution.py:386
  34.7 15.6 %all_gather.15.gathered_ref = bf16[512,512]{1,0:T(8,128)(2,1)S(1)} all-gather(bf16[64,512]{1,0:T(8,128)(2,1)S(1)} %bitcast.21), channel_id=1, replica_groups=mesh['tm'=8,'utt'=64] {'tm'}, dimensions={0}, use_global_device_ids=true | all-gather | bytes 589824 | tf_op jit(solution)/shard_map/all_gather | solution.py:390
  50.3 10.8 %shard_map.103 = (f32[512,2048]{1,0:T(8,128)S(1)}, bf16[512,512]{1,0:T(8,128)(2,1)S(1)}, f32[3,16,128]{2,1,0:T(8,128)S(1)}, f32[6,16,16,128]{3,2,1,0:T(8,128)S(1)}, f32[8,128]{1,0:T(8,128)S(1)}) custom-call(s32[2,64]{1,0:T(2,128)S(1)} %copy-done.4, s32[2]{0:T(128)S(1)} %collective-permute-done.prior_ref, s32[2]{0:T(128)S(1)} %copy-done.5, s32[2]{0:T(128)S(1)} %copy-done.6, ...), custom_call_target="tpu_custom_call" | custom-call | flops 1073741824 | bytes 8388608 | tf_op jit(solution)/shard_map/pallas_call | solution.py:417
  61.0 12.8 %all-gather = f32[64,128]{1,0:T(8,128)S(1)} all-gather(f32[8,128]{1,0:T(8,128)S(1)} %get-tuple-element.16), channel_id=2, replica_groups=mesh['tm'=8,'utt'=64] {'tm'}, dimensions={0}, use_global_device_ids=true | all-gather | bytes 36864 | tf_op jit(solution)/shard_map/all_gather | solution.py:451
  73.8 9.2 %shard_map.104 = (f32[2]{0:T(128)}, bf16[128,512]{1,0:T(8,128)(2,1)}, bf16[8,96,512]{2,1,0:T(8,128)(2,1)S(1)}) custom-call(s32[2,64]{1,0:T(2,128)S(1)} %copy-done.4, s32[2]{0:T(128)S(1)} %collective-permute-done.prior_ref, s32[2]{0:T(128)S(1)} %copy-done.5, s32[2]{0:T(128)S(1)} %copy-done.6, s32[1]{0:T(128)} %bitcast.block_ref, f32[8,8,128]{2,1,0:T(8,128)S(1)} %bitcast.17, ...), custom_call_target="tpu_custom_call" | custom-call | flops 3221225472 | bytes 8388608 | tf_op jit(solution)/shard_map/pallas_call | solution.py:453
  83.0 15.9 %all_to_all.15 = bf16[8,96,512]{2,1,0:T(8,128)(2,1)S(1)} all-to-all(bf16[8,96,512]{2,1,0:T(8,128)(2,1)S(1)} %get-tuple-element.23), channel_id=1, replica_groups=mesh['tm'=8,'utt'=64] {'tm'}, dimensions={0} | all-to-all | bytes 1572864 | tf_op jit(solution)/shard_map/all_to_all | solution.py:491
  99.0 0.1 convert_reduce_fusion
  99.1 0.7 reshape.41
  99.8 8.1 %all-to-all-start.2 = ((f32[64,4,128]{2,1,0:T(4,128)}), f32[64,4,128]{2,1,0:T(4,128)S(1)}, u32[]{:S(2)}, u32[]{:S(2)}) async-start(f32[64,4,128]{2,1,0:T(4,128)} %reshape.41), calls=%async_computation.2 | async-start | bytes 262144 | tf_op jit(solution)/shard_map/all_to_all | solution.py:495
  107.9 13.9 %all-to-all-done.2 = f32[64,4,128]{2,1,0:T(4,128)S(1)} async-done(((f32[64,4,128]{2,1,0:T(4,128)}), f32[64,4,128]{2,1,0:T(4,128)S(1)}, u32[]{:S(2)}, u32[]{:S(2)}) %all-to-all-start.2) | async-done | bytes 131104 | tf_op jit(solution)/shard_map/all_to_all | solution.py:495
  121.8 0.1 reduce_sum.19
  121.9 16.2 %all-gather.2 = f32[8,18,512]{2,1,0:T(8,128)S(1)} all-gather(f32[1,18,512]{2,1,0:T(8,128)S(1)} %maximum_bitcast_fusion), channel_id=3, replica_groups=mesh['tm'=8,'utt'=64] {'tm'}, dimensions={0}, use_global_device_ids=true | all-gather | bytes 331776 | tf_op jit(solution)/shard_map/all_gather | solution.py:497
  138.1 0.6 copy.22
  138.8 0.9 copy.16
  (20 shorter events, 0.2 us)
Async XLA Ops:
  0.6 0.7 copy-start
  0.6 49.6 %copy-start.4 = (s32[2,64]{1,0:T(2,128)S(1)}, s32[2,64]{1,0:T(2,128)}, u32[]{:S(2)}) copy-start(s32[2,64]{1,0:T(2,128)} %starts_ref.5) | copy-start | bytes 1540
  0.7 49.6 %copy-start.6 = (s32[2]{0:T(128)S(1)}, s32[2]{0:T(128)}, u32[]{:S(2)}) copy-start(s32[2]{0:T(128)} %labels_len_ref.3) | copy-start | bytes 28
  0.7 49.6 %copy-start.5 = (s32[2]{0:T(128)S(1)}, s32[2]{0:T(128)}, u32[]{:S(2)}) copy-start(s32[2]{0:T(128)} %frames_ref.3) | copy-start | bytes 28
  2.0 32.6 %all-to-all-start = ((bf16[64,4,128]{2,1,0:T(4,128)(2,1)}), bf16[64,4,128]{2,1,0:T(4,128)(2,1)S(1)}, u32[]{:S(2)}, u32[]{:S(2)}) async-start(bf16[64,4,128]{2,1,0:T(4,128)(2,1)} %broadcast_in_dim.8), calls=%async_computation | async-start | bytes 131072 | tf_op jit(solution)/shard_map/all_to_all | solution.py:386
  22.0 28.3 %collective-permute-start = (s32[2]{0:T(128)S(1)}, s32[2]{0:T(128)S(1)}, u32[]{:S(2)}, u32[]{:S(2)}) collective-permute-start(s32[2]{0:T(128)S(1)} %slice_reduce_fusion), channel_id=1, source_target_pairs={{0,64},{64,128},{128,192},{192,256},{256,320},{320,384},{384,448},... | collective-permute-start | bytes 32 | tf_op jit(solution)/shard_map/ppermute | solution.py:369
  27.0 0.9 copy-start.1
  27.9 0.7 copy-start.2
  28.6 0.7 copy-start.3
  99.8 22.0 %all-to-all-start.2 = ((f32[64,4,128]{2,1,0:T(4,128)}), f32[64,4,128]{2,1,0:T(4,128)S(1)}, u32[]{:S(2)}, u32[]{:S(2)}) async-start(f32[64,4,128]{2,1,0:T(4,128)} %reshape.41), calls=%async_computation.2 | async-start | bytes 262144 | tf_op jit(solution)/shard_map/all_to_all | solution.py:495

commit v2 on v1

--- a/solution.py
+++ b/solution.py
@@ -13,14 +13,15 @@
 STEPS = S // GROUP
 WIDE = GROUP * LANES
 PRED_PAD = 80
-PRED_SHARE = 17
-PRED_SLOT = 32
 VMEM_BYTES = 40 * 2**20
 
 masked_log = -1e30
 
 F32 = jnp.float32
 BF16 = jnp.bfloat16
+
+OFFSETS = (0, 1, 2, -1)
+RINGS = {64: (4, 16), 1: (1, 1)}
 
 NT_DIMS = (((1,), (1,)), ((), ()))
 
@@ -58,6 +59,39 @@
         total = jnp.sum(jnp.exp(terms - top), axis=0, keepdims=True)
         rows_ref[i : i + 1, :] = top + jnp.log(total)
     return rows_ref[...]
+
+
+def window_down(vector, distance):
+    places = row_ids((S, LANES))
+    for bit in (1, 2, 4, 8):
+        moved = jnp.where(places < S - bit, pltpu.roll(vector, S - bit, 0), masked_log)
+        vector = jnp.where((distance & bit) != 0, moved, vector)
+    return vector
+
+
+def window_up(vector, distance):
+    places = row_ids((S, LANES))
+    for bit in (1, 2, 4, 8):
+        moved = jnp.where(places >= bit, pltpu.roll(vector, bit, 0), masked_log)
+        vector = jnp.where((distance & bit) != 0, moved, vector)
+    return vector
+
+
+def slot_row(slot, utt_index, own_rows, x_size, z_size):
+    if x_size * z_size == 1:
+        return slot
+    unit = slot // own_rows
+    s4, s1, sx = unit % 4, unit // 4 % 4, unit // 16
+    near = lambda s: jnp.where(s == 3, -1, s)
+    x = (utt_index // z_size + near(sx) + x_size) % x_size
+    z = (utt_index % z_size + near(s1) + 4 * s4 + z_size) % z_size
+    return (x * z_size + z) * own_rows + slot % own_rows
+
+
+def frame_shifts(starts, half):
+    lanes = lane_ids()
+    first = (lanes == 0) | (lanes == half)
+    return jnp.where(first, 0, starts - pltpu.roll(starts, 1, 1))
 
 
 def span_rows(blank, emit):
@@ -104,35 +138,40 @@
 
 
 def forward_kernel(
-    piece,
-    vocab,
+    own_rows,
+    rings,
     starts_ref,
-    prior_ref,
     frames_ref,
     labels_len_ref,
     block_ref,
     label_ref,
-    gathered_ref,
+    parts_0,
+    parts_1,
+    parts_2,
+    parts_3,
     hidden_ref,
     exps_ref,
     weights_ref,
     lps_ref,
     tree_ref,
     payload_ref,
+    gathered,
     weights_t,
     root,
 ):
     step = pl.program_id(0)
-    width = gathered_ref.shape[0]
+    width = gathered.shape[0]
+    vocab = parts_0.shape[1]
 
     @pl.when(step == 0)
     def _():
-        own = row_ids((width, width))
-        got = lane_ids((width, width))
-        share = width // 8
-        source = (got % share) // piece * (8 * piece) + got // share * piece + got % piece
-        turn = (own == source).astype(BF16)
-        weights = jnp.dot(turn, gathered_ref[...], preferred_element_type=F32)
+        gathered[...] = jnp.zeros_like(gathered)
+        part = width // 4
+        for i, parts in enumerate((parts_0, parts_1, parts_2, parts_3)):
+            gathered[i * part : (i + 1) * part, :vocab] = parts[...]
+        source = slot_row(lane_ids((width, width)), block_ref[1], own_rows, *rings)
+        turn = (row_ids((width, width)) == source).astype(BF16)
+        weights = jnp.dot(turn, gathered[...], preferred_element_type=F32)
         weights_ref[...] = weights.astype(BF16)
         weights_t[...] = jnp.transpose(weights).astype(BF16)
 
@@ -170,9 +209,7 @@
         emit = jnp.where(allowed, lps_ref[1], masked_log)
         lps_ref[0] = blank
         lps_ref[1] = emit
-        before = pltpu.roll(starts, 1, 1)
-        before = jnp.where(lanes == 0, prior_ref[0], jnp.where(lanes == half, prior_ref[1], before))
-        shift = starts - before
+        shift = frame_shifts(starts, half)
         rows = span_rows(blank, emit)
         for bit in (1, 2, 4, 8):
             moved = (shift & bit) != 0
@@ -202,63 +239,64 @@
             line = flat[b * half : b * half + 1, :]
             payload_ref[4 * b : 4 * b + 1, :] = line[:, :LANES]
             payload_ref[4 * b + 1 : 4 * b + 2, :] = line[:, LANES:]
-            last = starts_ref[b : b + 1, half - 1 : half].astype(F32)
-            payload_ref[4 * b + 2 : 4 * b + 3, :] = jnp.broadcast_to(last, (1, LANES))
+            for end, at in ((2, half - 1), (3, 0)):
+                edge_start = starts_ref[b : b + 1, at : at + 1].astype(F32)
+                payload_ref[4 * b + end : 4 * b + end + 1, :] = jnp.broadcast_to(edge_start, (1, LANES))
 
 
 def backward_kernel(
-    piece,
-    vocab,
+    own_rows,
+    rings,
+    label_rows,
     starts_ref,
-    prior_ref,
     frames_ref,
     labels_len_ref,
     block_ref,
-    blocks_ref,
-    lps_ref,
-    tree_ref,
-    label_ref,
-    weights_ref,
-    hidden_ref,
-    exps_ref,
-    losses_ref,
-    grad_enc_ref,
-    send_ref,
-    chain,
-    line_up,
-    rows_ref,
-    grads,
-    enc_sum,
-    pred_sum,
-    weight_sum,
+    *refs,
 ):
+    blocks_refs, refs = refs[:8], refs[8:]
+    lps_ref, tree_ref, label_ref, weights_ref, hidden_ref, exps_ref = refs[:6]
+    losses_ref, grad_enc_ref, send_0, send_1, send_2, send_3, pred_own, pred_other = refs[6:14]
+    chain, line_up, rows_ref, grads, enc_sum, pred_sum, weight_sum = refs[14:]
     step = pl.program_id(0)
     half = starts_ref.shape[1]
     width = weights_ref.shape[0]
-    count = blocks_ref.shape[0]
+    count = len(blocks_refs)
     lanes = lane_ids()
+    core = block_ref[0] % 2
 
     @pl.when(step == 0)
     def _():
         places = row_ids((S, LANES))
         line_up[...] = jnp.zeros_like(line_up)
-        for r in range(count):
+        final = [jnp.zeros((1, LANES), F32)] * 2
+        ends = jnp.zeros((1, LANES), F32)
+        begins = jnp.zeros((1, LANES), F32)
+        for turn, blocks_ref in enumerate(blocks_refs):
+            r = block_ref[0] ^ turn
             for b in range(2):
                 at = 2 * r + b
-                line_up[at : at + 1, :LANES] = blocks_ref[r, 4 * b : 4 * b + 1, :]
-                line_up[at : at + 1, LANES:] = blocks_ref[r, 4 * b + 1 : 4 * b + 2, :]
-        chain[...] = jnp.transpose(line_up[...]).reshape(S, S, LANES)
+                end = blocks_ref[4 * b + 2 : 4 * b + 3, :]
+                line_up[0, pl.ds(at, 1), :] = blocks_ref[4 * b : 4 * b + 1, :]
+                line_up[1, pl.ds(at, 1), :] = blocks_ref[4 * b + 1 : 4 * b + 2, :]
+                ends = jnp.where(lanes == at, end, ends)
+                begins = jnp.where(lanes == at, blocks_ref[4 * b + 3 : 4 * b + 4, :], begins)
+                final[b] = jnp.where(r == count - 1, end, final[b])
+        for h in range(2):
+            chain[h * S // 2 : (h + 1) * S // 2] = jnp.transpose(line_up[h]).reshape(S // 2, S, LANES)
         odd = lanes % 2 == 1
-        last_start = [blocks_ref[count - 1, 4 * b + 2 : 4 * b + 3, :].astype(jnp.int32) for b in range(2)]
+        last_start = [row.astype(jnp.int32) for row in final]
         final_place = jnp.where(odd, labels_len_ref[1] - last_start[1], labels_len_ref[0] - last_start[0])
+        gap = (begins - pltpu.roll(ends, 2, 1)).astype(jnp.int32)
+        gap = jnp.where((lanes >= 2) & (lanes < 2 * count), gap, 0)
         forward = jnp.where(places == 0, 0.0, masked_log) + jnp.zeros((S, LANES), F32)
         closing = jnp.where(places == final_place, 0.0, masked_log)
         backward = closing
         owner = lanes // 2
         for turn in range(count - 1):
-            ahead = pltpu.roll(vector_times(forward, chain), 2, 1)
+            ahead = window_down(pltpu.roll(vector_times(forward, chain), 2, 1), gap)
             forward = jnp.where(owner == turn + 1, ahead, forward)
-            behind = pltpu.roll(times_vector(chain, backward, rows_ref), LANES - 2, 1)
+            behind = pltpu.roll(window_up(times_vector(chain, backward, rows_ref), gap), LANES - 2, 1)
             backward = jnp.where(owner == count - 2 - turn, behind, backward)
         leaving = vector_times(forward, chain) + closing
         best = jnp.max(leaving, axis=0, keepdims=True)
@@ -287,12 +325,7 @@
             behind = times_vector(tree_ref.at[level], beta_late, rows_ref)
             beta = jnp.where(later, beta_late, pltpu.roll(behind, LANES - reach, 1))
         starts = rows_to_lanes(starts_ref[...])
-        before = pltpu.roll(starts, 1, 1)
-        before = jnp.where(lanes == 0, prior_ref[0], jnp.where(lanes == half, prior_ref[1], before))
-        shift = starts - before
-        for bit in (1, 2, 4, 8):
-            moved = jnp.where(places < S - bit, pltpu.roll(alpha, S - bit, 0), masked_log)
-            alpha = jnp.where((shift & bit) != 0, moved, alpha)
+        alpha = window_down(alpha, frame_shifts(starts, half))
         spans = span_rows(lps_ref[0], lps_ref[1])
         scores = [spans[e] + alpha[e : e + 1, :] + beta for e in range(S)]
         best = jnp.max(functools.reduce(jnp.maximum, scores), axis=0, keepdims=True)
@@ -330,10 +363,9 @@
     starts = rows_to_lanes(starts_ref[...])
     base = starts + step * GROUP
     rows = jnp.concatenate([base + k for k in range(GROUP)], axis=1)
-    second = jnp.concatenate([per_lane(half, 0, 65)] * GROUP, axis=1)
-    slot = row_ids((8 * PRED_SLOT, WIDE))
-    wanted = rows + second
-    match = (slot // PRED_SLOT * PRED_SHARE + slot % PRED_SLOT == wanted) & (slot % PRED_SLOT < PRED_SHARE)
+    second = jnp.concatenate([per_lane(half, 0, 1)] * GROUP, axis=1)
+    slot = row_ids((2 * PRED_PAD, WIDE))
+    match = (slot % PRED_PAD == rows) & ((slot // PRED_PAD ^ core) == second)
     pred_sum[...] += lax.dot_general(
         match.astype(BF16), grad_summed.astype(BF16), NT_DIMS, preferred_element_type=F32
     )
@@ -342,14 +374,33 @@
     @pl.when(step == STEPS - 1)
     def _():
         grad_enc_ref[...] = jnp.transpose(enc_sum[...]).astype(BF16)
-        share = width // 8
-        got = row_ids((width, width))
-        source = (got % share) // piece * (8 * piece) + got // share * piece + got % piece
+        source = slot_row(row_ids((width, width)), block_ref[1], own_rows, *rings)
         turn = (lane_ids((width, width)) == source).astype(BF16)
         turned = jnp.dot(turn, weight_sum[...].astype(BF16), preferred_element_type=F32).astype(BF16)
-        for p in range(8):
-            send_ref[p, 0:share, :] = turned[p * share : (p + 1) * share, :]
-            send_ref[p, share : share + PRED_SLOT, :] = pred_sum[p * PRED_SLOT : (p + 1) * PRED_SLOT, :].astype(BF16)
+        part = width // 4
+        for i, send_ref in enumerate((send_0, send_1, send_2, send_3)):
+            send_ref[...] = turned[i * part : (i + 1) * part, :]
+        pred_own[...] = pred_sum[0:PRED_PAD, :]
+        pred_other[...] = pred_sum[PRED_PAD:, :].astype(BF16)
+
+
+def sum_kernel(*refs):
+    ins, outs = refs[:4], refs[4:]
+    total = functools.reduce(lambda a, b: a + b, [r[...].astype(F32) for r in ins])
+    part = total.shape[0] // len(outs)
+    for i, out in enumerate(outs):
+        out[...] = total[i * part : (i + 1) * part].astype(out.dtype)
+
+
+def sum_and_split(arrays, kinds):
+    rows, width = arrays[0].shape
+    vmem = pl.BlockSpec(memory_space=pltpu.VMEM)
+    return pl.pallas_call(
+        sum_kernel,
+        in_specs=[vmem] * 4,
+        out_specs=[vmem] * len(kinds),
+        out_shape=[jax.ShapeDtypeStruct((rows // len(kinds), width), kind) for kind in kinds],
+    )(*arrays)
 
 
 def params():
@@ -363,33 +414,41 @@
 smem = pl.BlockSpec(memory_space=pltpu.SMEM)
 
 
-def from_behind(block, axis, distance):
-    devices = range(lax.axis_size(axis))
-    route = [(i - distance, i) for i in devices if i - distance in devices]
-    return lax.ppermute(block, axis, route)
+def from_offset(block, axis, source):
+    size = lax.axis_size(axis)
+    return lax.ppermute(block, axis, [(source(i) % size, i) for i in range(size)])
+
+
+def x_source(offset, x_size, z_size):
+    return lambda i: (i // z_size + offset) % x_size * z_size + i % z_size
+
+
+def z_source(offset, x_size, z_size):
+    return lambda i: i // z_size * z_size + (i % z_size + offset) % z_size
 
 
 def per_device(encoder, predictor, starts, frame_lengths, label_lengths, labels, w_out):
     utt_count, frame_count, width = encoder.shape
     own_rows, vocab = w_out.shape
+    label_rows = predictor.shape[1]
     tm_index = lax.axis_index("tm")
     tm_count = lax.axis_size("tm")
+    utt_index = lax.axis_index("utt")
     utt_size = lax.axis_size("utt")
-    piece = own_rows // tm_count
+    rings = RINGS[utt_size]
     padded = -(-vocab // LANES) * LANES
-    share = width // tm_count
     rows = S * utt_count * frame_count
     shape = jax.ShapeDtypeStruct
 
-    mine = lax.dynamic_slice_in_dim(w_out, tm_index * piece, piece, axis=0)
-    mine = jnp.pad(mine, ((0, 0), (0, padded - vocab)))
-    across = lax.all_to_all(
-        jnp.broadcast_to(mine.reshape(1, piece * padded // LANES, LANES), (utt_size, piece * padded // LANES, LANES)),
-        "utt", 0, 0, tiled=True,
-    )
-    gathered = lax.all_gather(across.reshape(share, padded), "tm", axis=0, tiled=True)
-    prior = from_behind(starts[:, -1], "tm", 1)
-    block = tm_index.reshape(1).astype(jnp.int32)
+    if utt_size > 1:
+        held = [w_out] + [from_offset(w_out, "utt", z_source(4 * s, *rings)) for s in (1, 2, 3)]
+        held = jnp.concatenate(held, axis=0)
+        held = [held] + [from_offset(held, "utt", z_source(o, *rings)) for o in OFFSETS[1:]]
+        held = jnp.concatenate(held, axis=0)
+        parts = [held] + [from_offset(held, "utt", x_source(o, *rings)) for o in OFFSETS[1:]]
+    else:
+        parts = [w_out[i * width // 4 : (i + 1) * width // 4] for i in range(4)]
+    block = jnp.stack([tm_index, utt_index]).astype(jnp.int32)
 
     hidden, label_ids = pl.pallas_call(
         hidden_kernel,
@@ -415,16 +474,15 @@
 
     levels = frame_count.bit_length() - 1
     exps, weights, lps, tree, payload = pl.pallas_call(
-        functools.partial(forward_kernel, piece, vocab),
+        functools.partial(forward_kernel, own_rows, rings),
         grid=(STEPS,),
         in_specs=[
             whole(starts.shape),
             smem,
             smem,
             smem,
-            smem,
             whole((S, LANES)),
-            whole((width, padded)),
+            *[whole((width // 4, vocab))] * 4,
             pl.BlockSpec((width, WIDE), lambda i: (0, i)),
         ],
         out_specs=[
@@ -441,25 +499,31 @@
             shape((levels, S, S, LANES), F32),
             shape((8, LANES), F32),
         ],
-        scratch_shapes=[pltpu.VMEM((padded, width), BF16), pltpu.VMEM((S, S, LANES), F32)],
+        scratch_shapes=[
+            pltpu.VMEM((width, padded), BF16),
+            pltpu.VMEM((padded, width), BF16),
+            pltpu.VMEM((S, S, LANES), F32),
+        ],
         compiler_params=params(),
         cost_estimate=pl.CostEstimate(
             flops=2 * padded * width * rows, bytes_accessed=8 * 2**20, transcendentals=padded * rows
         ),
-    )(starts, prior, frame_lengths, label_lengths, block, label_ids, gathered, hidden)
-
-    blocks = lax.all_gather(payload, "tm", axis=0)
-
-    losses, grad_encoder, send = pl.pallas_call(
-        functools.partial(backward_kernel, piece, vocab),
+    )(starts, frame_lengths, label_lengths, block, label_ids, *parts, hidden)
+
+    def tm_flip(block, turn):
+        return from_offset(block, "tm", lambda i: i ^ turn)
+
+    blocks = [payload] + [tm_flip(payload, turn) for turn in range(1, tm_count)]
+
+    losses, grad_encoder, *sends = pl.pallas_call(
+        functools.partial(backward_kernel, own_rows, rings, label_rows),
         grid=(STEPS,),
         in_specs=[
             whole(starts.shape),
             smem,
             smem,
             smem,
-            smem,
-            whole((tm_count, 8, LANES)),
+            *[whole((8, LANES))] * tm_count,
             whole((3, S, LANES)),
             whole((levels, S, S, LANES)),
             whole((S, LANES)),
@@ -467,39 +531,56 @@
             pl.BlockSpec((width, WIDE), lambda i: (0, i)),
             pl.BlockSpec((padded, WIDE), lambda i: (0, i)),
         ],
-        out_specs=[smem, whole((utt_count * frame_count, width)), whole((tm_count, share + PRED_SLOT, padded))],
+        out_specs=[
+            smem,
+            whole((utt_count * frame_count, width)),
+            *[whole((width // 4, padded))] * 4,
+            *[whole((PRED_PAD, width))] * 2,
+        ],
         out_shape=[
             shape((utt_count,), F32),
             shape((utt_count * frame_count, width), BF16),
-            shape((tm_count, share + PRED_SLOT, padded), BF16),
+            *[shape((width // 4, padded), BF16)] * 4,
+            shape((PRED_PAD, width), F32),
+            shape((PRED_PAD, width), BF16),
         ],
         scratch_shapes=[
             pltpu.VMEM((S, S, LANES), F32),
-            pltpu.VMEM((LANES, S * S), F32),
+            pltpu.VMEM((2, LANES, LANES), F32),
             pltpu.VMEM((S, LANES), F32),
             pltpu.VMEM((2, S, LANES), F32),
             pltpu.VMEM((width, LANES), F32),
-            pltpu.VMEM((8 * PRED_SLOT, width), F32),
+            pltpu.VMEM((2 * PRED_PAD, width), F32),
             pltpu.VMEM((width, padded), F32),
         ],
         compiler_params=params(),
         cost_estimate=pl.CostEstimate(
             flops=6 * padded * width * rows, bytes_accessed=8 * 2**20, transcendentals=2**16
         ),
-    )(starts, prior, frame_lengths, label_lengths, block, blocks, lps, tree, label_ids, weights, hidden, exps)
-
-    came = lax.all_to_all(send, "tm", 0, 0, tiled=True)
-    block_sum = jnp.sum(came.astype(F32), axis=0)
-    weight_rows = block_sum[:share].reshape(utt_size, piece * padded // LANES, LANES)
-    pred_rows = block_sum[share : share + PRED_SHARE]
-    across = lax.all_to_all(weight_rows, "utt", 0, 0, tiled=True)
-    own_weight = jnp.sum(across, axis=0).reshape(piece, padded)
-    final = lax.all_gather(jnp.concatenate([pred_rows, own_weight], axis=0), "tm", axis=0)
-    label_rows = predictor.shape[1]
-    grad_predictor = final[:, :PRED_SHARE].reshape(-1, width)[: utt_count * label_rows]
-    grad_predictor = grad_predictor.reshape(utt_count, label_rows, width)
-    grad_w_out = final[:, PRED_SHARE:, :vocab].reshape(own_rows, vocab)
-    return (losses, grad_encoder.reshape(encoder.shape), grad_predictor, grad_w_out)
+    )(starts, frame_lengths, label_lengths, block, *blocks, lps, tree, label_ids, weights, hidden, exps)
+
+    terms, (pred_own, pred_other) = sends[:4], sends[4:]
+    pred_own = pred_own + tm_flip(pred_other, 1).astype(F32)
+    pred_sent = pred_own.astype(BF16)
+    for turn in (2, 4, 6):
+        pred_own = pred_own + tm_flip(pred_sent, turn).astype(F32)
+    pred_own = pred_own[:label_rows]
+    pred_far = tm_flip(pred_own, 1)
+    is_odd = tm_index % 2 == 1
+    grad_predictor = jnp.stack([jnp.where(is_odd, pred_far, pred_own), jnp.where(is_odd, pred_own, pred_far)])
+
+    if utt_size > 1:
+        arrived = [terms[0]] + [from_offset(t, "utt", x_source(-o, *rings)) for t, o in zip(terms[1:], OFFSETS[1:])]
+        terms = sum_and_split(arrived, [F32, BF16, BF16, BF16])
+        arrived = [terms[0]] + [from_offset(t, "utt", z_source(-o, *rings)) for t, o in zip(terms[1:], OFFSETS[1:])]
+        terms = sum_and_split(arrived, [F32] * 4)
+        arrived = [terms[0]] + [from_offset(t, "utt", z_source(-4 * s, *rings)) for t, s in zip(terms[1:], (1, 2, 3))]
+        own = arrived[0] + arrived[1] + arrived[2] + arrived[3]
+    else:
+        own = jnp.concatenate(terms, axis=0).astype(F32)
+    own = own + tm_flip(own, 1)
+    own = own + tm_flip(own, 2) + tm_flip(own, 4) + tm_flip(own, 6)
+    return (losses, grad_encoder.reshape(encoder.shape), grad_predictor, own[:, :vocab])
 
 
 def solution(mesh):

time: 140 us -> 186 us (1.33)
  starting transfers between devices: 31.2 us -> 138 us
  blocking collectives: 60.5 us -> 0 us
  waiting for transfers between devices: 17.5 us -> 9.17 us
  Pallas kernels: 21.8 us -> 25.7 us
    ppermute x1 -> x34, starting transfers between devices: 4.04 us -> 138 us  [from_offset(): lax.ppermute(block, axis, [(source(i) % size, i) for i in range(size)])]
    all_gather x3 -> x0, blocking collectives: 44.6 us -> none  [the longest x1 16.2 us: per_device(): lax.all_gather(jnp.concatenate([pred_rows, own_weight], axis=0), 'tm', ax...]
    all_to_all x2 -> x0, starting transfers between devices: 27.2 us -> none  [the longest x1 19.1 us: per_device(): lax.all_to_all(jnp.broadcast_to(mine.reshape(1, piece * padded // LANES,...]
    all_to_all x2 -> x0, waiting for transfers between devices: 17.5 us -> none  [the longest x1 13.9 us: per_device(): across = lax.all_to_all(weight_rows, 'utt', 0, 0, tiled=True)]
    all_to_all x1 -> x0, blocking collectives: 15.9 us -> none  [per_device(): came = lax.all_to_all(send, 'tm', 0, 0, tiled=True)]
    ppermute x1 -> x34, waiting for transfers between devices: 0.01 us -> 9.17 us  [from_offset(): lax.ppermute(block, axis, [(source(i) % size, i) for i in range(size)])]
    pallas_call x2 -> x4, Pallas kernels: 19.9 us -> 23.8 us  [the longest x1 10.9 us: per_device(): pl.pallas_call(functools.partial(forward_kernel, own_rows, rings), grid=(...]
    unnamed x18 -> x33, local copies, waits for them, and re-layouts: 5.38 us -> 8.73 us
  transfers between devices with their start and end apart: 3 -> 34, of which waited for: 2 -> 7; matrix products, arithmetic and copies ran while one was open for 1% -> 2% of each run, Pallas kernels for 1% -> 3%
where the time goes in v2:
time: 186 us; the launch traced here: 185 us
  starting transfers between devices  138 us (74%)
  Pallas kernels  25.7 us (14%)
  waiting for transfers between devices  9.17 us (5%)
  local copies, waits for them, and re-layouts  8.74 us (5%)
    ppermute x34, starting transfers between devices, from_offset(): lax.ppermute(block, axis, [(source(i) % size, i) for i in range(size)])  138 us
    pallas_call x1, Pallas kernels, per_device(): pl.pallas_call(functools.partial(forward_kernel, own_rows, rings), grid=(...  10.9 us
    pallas_call x1, Pallas kernels, per_device(): pl.pallas_call(functools.partial(backward_kernel, own_rows, rings, label_...  9.7 us
    ppermute x34, waiting for transfers between devices, from_offset(): lax.ppermute(block, axis, [(source(i) % size, i) for i in range(size)])  9.17 us
    unnamed x33, local copies, waits for them, and re-layouts  8.73 us
  transfers between devices with their start and end apart: 34, of which 7 were waited for; matrix products, arithmetic and copies ran while one was open for 2% of the time, Pallas kernels for 3%

profile of v2, /device:TPU:1, one launch (start us, length us, event | category | flops | bytes accessed | tf_op | source)
XLA Modules:
  0.0 184.8 jit_solution(9791267920870513015)
XLA Ops:
  0.6 16.3 %collective-permute-start.1 = (bf16[8,500]{1,0:T(8,128)(2,1)}, bf16[8,500]{1,0:T(8,128)(2,1)S(1)}, u32[]{:S(2)}, u32[]{:S(2)}) collective-permute-start(bf16[8,500]{1,0:T(8,128)(2,1)} %param.13), channel_id=1, source_target_pairs={{8,0},{9,1},{10,2},{11,3},{12,4},{13,5},{14,6},{15,7},{0,8},{1,9},... | collective-permute-start | bytes 24008 | tf_op jit(solution)/shard_map/ppermute | solution.py:419
  18.8 7.3 %collective-permute-start.2 = (bf16[8,500]{1,0:T(8,128)(2,1)}, bf16[8,500]{1,0:T(8,128)(2,1)S(1)}, u32[]{:S(2)}, u32[]{:S(2)}) collective-permute-start(bf16[8,500]{1,0:T(8,128)(2,1)} %param.13), channel_id=1, source_target_pairs={{12,0},{13,1},{14,2},{15,3},{0,4},{1,5},{2,6},{3,7},{4,8},{5,9},{6... | collective-permute-start | bytes 24008 | tf_op jit(solution)/shard_map/ppermute | solution.py:419
  27.4 2.7 %collective-permute-start.3 = (bf16[32,500]{1,0:T(8,128)(2,1)S(1)}, bf16[32,500]{1,0:T(8,128)(2,1)S(1)}, u32[]{:S(2)}, u32[]{:S(2)}) collective-permute-start(bf16[32,500]{1,0:T(8,128)(2,1)S(1)} %get-tuple-element.58), channel_id=1, source_target_pairs={{1,0},{2,1},{3,2},{4,3},{5,4},{6,5},{7,6},{8,7},{9,8},{10,9},{11,1... | collective-permute-start | bytes 96008 | tf_op jit(solution)/shard_map/ppermute | solution.py:419
  33.6 3.1 %collective-permute-start.4 = (bf16[32,500]{1,0:T(8,128)(2,1)S(1)}, bf16[32,500]{1,0:T(8,128)(2,1)S(1)}, u32[]{:S(2)}, u32[]{:S(2)}) collective-permute-start(bf16[32,500]{1,0:T(8,128)(2,1)S(1)} %get-tuple-element.58), channel_id=1, source_target_pairs={{2,0},{3,1},{4,2},{5,3},{6,4},{7,5},{8,6},{9,7},{10,8},{11,9},{12,... | collective-permute-start | bytes 96008 | tf_op jit(solution)/shard_map/ppermute | solution.py:419
  39.1 3.1 %collective-permute-start.8 = (bf16[128,500]{1,0:T(8,128)(2,1)S(1)}, bf16[128,500]{1,0:T(8,128)(2,1)S(1)}, u32[]{:S(2)}, u32[]{:S(2)}) collective-permute-start(bf16[128,500]{1,0:T(8,128)(2,1)S(1)} %constant_dynamic-update-slice_fusion.4.parts_0), channel_id=1, source_target_pairs={{48,0},{49,1},{50,2},{51,3},{52,4},{53,5},{54,6},{55,7},{56,8},{57... | collective-permute-start | bytes 384008 | tf_op jit(solution)/shard_map/ppermute | solution.py:419
  42.3 4.4 %collective-permute-start.7 = (bf16[128,500]{1,0:T(8,128)(2,1)S(1)}, bf16[128,500]{1,0:T(8,128)(2,1)S(1)}, u32[]{:S(2)}, u32[]{:S(2)}) collective-permute-start(bf16[128,500]{1,0:T(8,128)(2,1)S(1)} %constant_dynamic-update-slice_fusion.4.parts_0), channel_id=1, source_target_pairs={{32,0},{33,1},{34,2},{35,3},{36,4},{37,5},{38,6},{39,7},{40,8},{41... | collective-permute-start | bytes 384008 | tf_op jit(solution)/shard_map/ppermute | solution.py:419
  46.6 3.1 %collective-permute-start.6 = (bf16[128,500]{1,0:T(8,128)(2,1)S(1)}, bf16[128,500]{1,0:T(8,128)(2,1)S(1)}, u32[]{:S(2)}, u32[]{:S(2)}) collective-permute-start(bf16[128,500]{1,0:T(8,128)(2,1)S(1)} %constant_dynamic-update-slice_fusion.4.parts_0), channel_id=1, source_target_pairs={{16,0},{17,1},{18,2},{19,3},{20,4},{21,5},{22,6},{23,7},{24,8},{25... | collective-permute-start | bytes 384008 | tf_op jit(solution)/shard_map/ppermute | solution.py:419
  56.0 10.9 %shard_map.103 = (f32[512,2048]{1,0:T(8,128)S(1)}, bf16[512,512]{1,0:T(8,128)(2,1)S(1)}, f32[3,16,128]{2,1,0:T(8,128)S(1)}, f32[6,16,16,128]{3,2,1,0:T(8,128)S(1)}, f32[8,128]{1,0:T(8,128)S(1)}) custom-call(s32[2,64]{1,0:T(2,128)S(1)} %copy-done.4, s32[2]{0:T(128)S(1)} %copy-done.5, s32[2]{0:T(128)S(1)} %copy-done.6, s32[2]{0:T(128)S(1)} %pad_add_fusion.block_ref, ...), custom_call_target="tpu_custom_call" | custom-call | flops 1073741824 | bytes 8388608 | tf_op jit(solution)/shard_map/pallas_call | solution.py:476
  66.8 9.2 %collective-permute-start.15 = (f32[8,128]{1,0:T(8,128)S(1)}, f32[8,128]{1,0:T(8,128)S(1)}, u32[]{:S(2)}, u32[]{:S(2)}) collective-permute-start(f32[8,128]{1,0:T(8,128)S(1)} %get-tuple-element.29.refs_0_), channel_id=1, source_target_pairs={{448,0},{384,64},{320,128},{256,192},{192,256},{128,320},{64,384},... | collective-permute-start | bytes 12296 | tf_op jit(solution)/shard_map/ppermute | solution.py:419
  80.5 4.6 %collective-permute-start.12 = (f32[8,128]{1,0:T(8,128)S(1)}, f32[8,128]{1,0:T(8,128)S(1)}, u32[]{:S(2)}, u32[]{:S(2)}) collective-permute-start(f32[8,128]{1,0:T(8,128)S(1)} %get-tuple-element.29.refs_0_), channel_id=1, source_target_pairs={{256,0},{320,64},{384,128},{448,192},{0,256},{64,320},{128,384},{1... | collective-permute-start | bytes 12296 | tf_op jit(solution)/shard_map/ppermute | solution.py:419
  87.3 3.3 %collective-permute-start.10 = (f32[8,128]{1,0:T(8,128)S(1)}, f32[8,128]{1,0:T(8,128)S(1)}, u32[]{:S(2)}, u32[]{:S(2)}) collective-permute-start(f32[8,128]{1,0:T(8,128)S(1)} %get-tuple-element.29.refs_0_), channel_id=1, source_target_pairs={{128,0},{192,64},{0,128},{64,192},{384,256},{448,320},{256,384},{3... | collective-permute-start | bytes 12296 | tf_op jit(solution)/shard_map/ppermute | solution.py:419
  93.8 9.7 %shard_map.104 = (f32[2]{0:T(128)}, bf16[128,512]{1,0:T(8,128)(2,1)}, bf16[128,512]{1,0:T(8,128)(2,1)S(1)}, bf16[128,512]{1,0:T(8,128)(2,1)S(1)}, bf16[128,512]{...) custom-call(s32[2,64]{1,0:T(2,128)S(1)} %copy-done.4, ...), custom_call_target="tpu_custom_call" | custom-call | flops 3221225472 | bytes 8388608 | tf_op jit(solution)/shard_map/pallas_call | solution.py:518
  106.4 4.4 %collective-permute-start.22 = (bf16[128,512]{1,0:T(8,128)(2,1)S(1)}, bf16[128,512]{1,0:T(8,128)(2,1)S(1)}, u32[]{:S(2)}, u32[]{:S(2)}) collective-permute-start(bf16[128,512]{1,0:T(8,128)(2,1)S(1)} %get-tuple-element.40), channel_id=1, source_target_pairs={{32,0},{33,1},{34,2},{35,3},{36,4},{37,5},{38,6},{39,7},{40,8},{41... | collective-permute-start | bytes 393224 | tf_op jit(solution)/shard_map/ppermute | solution.py:419
  112.7 2.8 %collective-permute-start.16 = (bf16[80,512]{1,0:T(8,128)(2,1)S(1)}, bf16[80,512]{1,0:T(8,128)(2,1)S(1)}, u32[]{:S(2)}, u32[]{:S(2)}) collective-permute-start(bf16[80,512]{1,0:T(8,128)(2,1)S(1)} %get-tuple-element.37), channel_id=1, source_target_pairs={{64,0},{0,64},{192,128},{128,192},{320,256},{256,320},{448,384},{3... | collective-permute-start | bytes 245768 | tf_op jit(solution)/shard_map/ppermute | solution.py:419
  119.4 3.9 %collective-permute-start.24 = (bf16[32,512]{1,0:T(8,128)(2,1)}, bf16[32,512]{1,0:T(8,128)(2,1)S(1)}, u32[]{:S(2)}, u32[]{:S(2)}) collective-permute-start(bf16[32,512]{1,0:T(8,128)(2,1)} %get-tuple-element.43), channel_id=1, source_target_pairs={{15,0},{0,1},{1,2},{2,3},{3,4},{4,5},{5,6},{6,7},{7,8},{8,9},{9,10... | collective-permute-start | bytes 98312 | tf_op jit(solution)/shard_map/ppermute | solution.py:419
  123.3 6.1 %collective-permute-start.25 = (bf16[32,512]{1,0:T(8,128)(2,1)}, bf16[32,512]{1,0:T(8,128)(2,1)S(1)}, u32[]{:S(2)}, u32[]{:S(2)}) collective-permute-start(bf16[32,512]{1,0:T(8,128)(2,1)} %get-tuple-element.44), channel_id=1, source_target_pairs={{14,0},{15,1},{0,2},{1,3},{2,4},{3,5},{4,6},{5,7},{6,8},{7,9},{8,1... | collective-permute-start | bytes 98312 | tf_op jit(solution)/shard_map/ppermute | solution.py:419
  131.4 2.9 %collective-permute-done.26.refs_3_ = bf16[32,512]{1,0:T(8,128)(2,1)S(1)} collective-permute-done((bf16[32,512]{1,0:T(8,128)(2,1)}, bf16[32,512]{1,0:T(8,128)(2,1)S(1)}, u32[]{:S(2)}, u32[]{:S(2)}) %collective-permute-start.26) | collective-permute-done | bytes 32800 | tf_op jit(solution)/shard_map/ppermute | solution.py:419
  136.4 5.7 %collective-permute-start.27 = (f32[8,512]{1,0:T(8,128)}, f32[8,512]{1,0:T(8,128)S(1)}, u32[]{:S(2)}, u32[]{:S(2)}) collective-permute-start(f32[8,512]{1,0:T(8,128)} %get-tuple-element.47), channel_id=1, source_target_pairs={{12,0},{13,1},{14,2},{15,3},{0,4},{1,5},{2,6},{3,7},{4,8},{5,9},{6... | collective-permute-start | bytes 49160 | tf_op jit(solution)/shard_map/ppermute | solution.py:419
  142.1 4.2 %collective-permute-start.28 = (f32[8,512]{1,0:T(8,128)}, f32[8,512]{1,0:T(8,128)S(1)}, u32[]{:S(2)}, u32[]{:S(2)}) collective-permute-start(f32[8,512]{1,0:T(8,128)} %get-tuple-element.48), channel_id=1, source_target_pairs={{8,0},{9,1},{10,2},{11,3},{12,4},{13,5},{14,6},{15,7},{0,8},{1,9},... | collective-permute-start | bytes 49160 | tf_op jit(solution)/shard_map/ppermute | solution.py:419
  146.3 7.0 %collective-permute-start.29 = (f32[8,512]{1,0:T(8,128)}, f32[8,512]{1,0:T(8,128)S(1)}, u32[]{:S(2)}, u32[]{:S(2)}) collective-permute-start(f32[8,512]{1,0:T(8,128)} %get-tuple-element.49), channel_id=1, source_target_pairs={{4,0},{5,1},{6,2},{7,3},{8,4},{9,5},{10,6},{11,7},{12,8},{13,9},{1... | collective-permute-start | bytes 49160 | tf_op jit(solution)/shard_map/ppermute | solution.py:419
  153.3 4.5 %collective-permute-start.19 = (bf16[80,512]{1,0:T(8,128)(2,1)S(1)}, bf16[80,512]{1,0:T(8,128)(2,1)S(1)}, u32[]{:S(2)}, u32[]{:S(2)}) collective-permute-start(bf16[80,512]{1,0:T(8,128)(2,1)S(1)} %get-tuple-element.54), channel_id=1, source_target_pairs={{384,0},{448,64},{256,128},{320,192},{128,256},{192,320},{0,384},{... | collective-permute-start | bytes 245768 | tf_op jit(solution)/shard_map/ppermute | solution.py:419
  163.1 6.7 %collective-permute-start.30 = (f32[8,512]{1,0:T(8,128)S(1)}, f32[8,512]{1,0:T(8,128)S(1)}, u32[]{:S(2)}, u32[]{:S(2)}) collective-permute-start(f32[8,512]{1,0:T(8,128)S(1)} %add_add_fusion), channel_id=1, source_target_pairs={{64,0},{0,64},{192,128},{128,192},{320,256},{256,320},{448,384},{3... | collective-permute-start | bytes 49160 | tf_op jit(solution)/shard_map/ppermute | solution.py:419
  170.6 4.5 %collective-permute-start.33 = (f32[8,512]{1,0:T(8,128)S(1)}, f32[8,512]{1,0:T(8,128)S(1)}, u32[]{:S(2)}, u32[]{:S(2)}) collective-permute-start(f32[8,512]{1,0:T(8,128)S(1)} %add.45), channel_id=1, source_target_pairs={{384,0},{448,64},{256,128},{320,192},{128,256},{192,320},{0,384},{... | collective-permute-start | bytes 49160 | tf_op jit(solution)/shard_map/ppermute | solution.py:419
  179.7 3.1 %collective-permute-start.20 = (f32[65,512]{1,0:T(8,128)S(1)}, f32[65,512]{1,0:T(8,128)S(1)}, u32[]{:S(2)}, u32[]{:S(2)}) collective-permute-start(f32[65,512]{1,0:T(8,128)S(1)} %fusion.1), channel_id=1, source_target_pairs={{64,0},{0,64},{192,128},{128,192},{320,256},{256,320},{448,384},{3... | collective-permute-start | bytes 399368 | tf_op jit(solution)/shard_map/ppermute | solution.py:419
  (92 shorter events, 50.3 us)
Async XLA Ops:
  0.6 26.2 %collective-permute-start.1 = (bf16[8,500]{1,0:T(8,128)(2,1)}, bf16[8,500]{1,0:T(8,128)(2,1)S(1)}, u32[]{:S(2)}, u32[]{:S(2)}) collective-permute-start(bf16[8,500]{1,0:T(8,128)(2,1)} %param.13), channel_id=1, source_target_pairs={{8,0},{9,1},{10,2},{11,3},{12,4},{13,5},{14,6},{15,7},{0,8},{1,9},... | collective-permute-start | bytes 24008 | tf_op jit(solution)/shard_map/ppermute | solution.py:419
  16.9 9.9 %collective-permute-start = (bf16[8,500]{1,0:T(8,128)(2,1)}, bf16[8,500]{1,0:T(8,128)(2,1)S(1)}, u32[]{:S(2)}, u32[]{:S(2)}) collective-permute-start(bf16[8,500]{1,0:T(8,128)(2,1)} %param.13), channel_id=1, source_target_pairs={{4,0},{5,1},{6,2},{7,3},{8,4},{9,5},{10,6},{11,7},{12,8},{13,9},{1... | collective-permute-start | bytes 24008 | tf_op jit(solution)/shard_map/ppermute | solution.py:419
  18.8 8.5 %collective-permute-start.2 = (bf16[8,500]{1,0:T(8,128)(2,1)}, bf16[8,500]{1,0:T(8,128)(2,1)S(1)}, u32[]{:S(2)}, u32[]{:S(2)}) collective-permute-start(bf16[8,500]{1,0:T(8,128)(2,1)} %param.13), channel_id=1, source_target_pairs={{12,0},{13,1},{14,2},{15,3},{0,4},{1,5},{2,6},{3,7},{4,8},{5,9},{6... | collective-permute-start | bytes 24008 | tf_op jit(solution)/shard_map/ppermute | solution.py:419
  27.4 9.3 %collective-permute-start.3 = (bf16[32,500]{1,0:T(8,128)(2,1)S(1)}, bf16[32,500]{1,0:T(8,128)(2,1)S(1)}, u32[]{:S(2)}, u32[]{:S(2)}) collective-permute-start(bf16[32,500]{1,0:T(8,128)(2,1)S(1)} %get-tuple-element.58), channel_id=1, source_target_pairs={{1,0},{2,1},{3,2},{4,3},{5,4},{6,5},{7,6},{8,7},{9,8},{10,9},{11,1... | collective-permute-start | bytes 96008 | tf_op jit(solution)/shard_map/ppermute | solution.py:419
  31.0 8.2 %collective-permute-start.5 = (bf16[32,500]{1,0:T(8,128)(2,1)S(1)}, bf16[32,500]{1,0:T(8,128)(2,1)S(1)}, u32[]{:S(2)}, u32[]{:S(2)}) collective-permute-start(bf16[32,500]{1,0:T(8,128)(2,1)S(1)} %get-tuple-element.58), channel_id=1, source_target_pairs={{15,0},{0,1},{1,2},{2,3},{3,4},{4,5},{5,6},{6,7},{7,8},{8,9},{9,10... | collective-permute-start | bytes 96008 | tf_op jit(solution)/shard_map/ppermute | solution.py:419
  39.1 14.8 %collective-permute-start.8 = (bf16[128,500]{1,0:T(8,128)(2,1)S(1)}, bf16[128,500]{1,0:T(8,128)(2,1)S(1)}, u32[]{:S(2)}, u32[]{:S(2)}) collective-permute-start(bf16[128,500]{1,0:T(8,128)(2,1)S(1)} %constant_dynamic-update-slice_fusion.4.parts_0), channel_id=1, source_target_pairs={{48,0},{49,1},{50,2},{51,3},{52,4},{53,5},{54,6},{55,7},{56,8},{57... | collective-permute-start | bytes 384008 | tf_op jit(solution)/shard_map/ppermute | solution.py:419
  42.3 11.7 %collective-permute-start.7 = (bf16[128,500]{1,0:T(8,128)(2,1)S(1)}, bf16[128,500]{1,0:T(8,128)(2,1)S(1)}, u32[]{:S(2)}, u32[]{:S(2)}) collective-permute-start(bf16[128,500]{1,0:T(8,128)(2,1)S(1)} %constant_dynamic-update-slice_fusion.4.parts_0), channel_id=1, source_target_pairs={{32,0},{33,1},{34,2},{35,3},{36,4},{37,5},{38,6},{39,7},{40,8},{41... | collective-permute-start | bytes 384008 | tf_op jit(solution)/shard_map/ppermute | solution.py:419
  66.8 20.5 %collective-permute-start.15 = (f32[8,128]{1,0:T(8,128)S(1)}, f32[8,128]{1,0:T(8,128)S(1)}, u32[]{:S(2)}, u32[]{:S(2)}) collective-permute-start(f32[8,128]{1,0:T(8,128)S(1)} %get-tuple-element.29.refs_0_), channel_id=1, source_target_pairs={{448,0},{384,64},{320,128},{256,192},{192,256},{128,320},{64,384},... | collective-permute-start | bytes 12296 | tf_op jit(solution)/shard_map/ppermute | solution.py:419
  76.1 14.6 %collective-permute-start.14 = (f32[8,128]{1,0:T(8,128)S(1)}, f32[8,128]{1,0:T(8,128)S(1)}, u32[]{:S(2)}, u32[]{:S(2)}) collective-permute-start(f32[8,128]{1,0:T(8,128)S(1)} %get-tuple-element.29.refs_0_), channel_id=1, source_target_pairs={{384,0},{448,64},{256,128},{320,192},{128,256},{192,320},{0,384},{... | collective-permute-start | bytes 12296 | tf_op jit(solution)/shard_map/ppermute | solution.py:419
  78.0 15.0 %collective-permute-start.13 = (f32[8,128]{1,0:T(8,128)S(1)}, f32[8,128]{1,0:T(8,128)S(1)}, u32[]{:S(2)}, u32[]{:S(2)}) collective-permute-start(f32[8,128]{1,0:T(8,128)S(1)} %get-tuple-element.29.refs_0_), channel_id=1, source_target_pairs={{320,0},{256,64},{448,128},{384,192},{64,256},{0,320},{192,384},{1... | collective-permute-start | bytes 12296 | tf_op jit(solution)/shard_map/ppermute | solution.py:419
  80.5 12.5 %collective-permute-start.12 = (f32[8,128]{1,0:T(8,128)S(1)}, f32[8,128]{1,0:T(8,128)S(1)}, u32[]{:S(2)}, u32[]{:S(2)}) collective-permute-start(f32[8,128]{1,0:T(8,128)S(1)} %get-tuple-element.29.refs_0_), channel_id=1, source_target_pairs={{256,0},{320,64},{384,128},{448,192},{0,256},{64,320},{128,384},{1... | collective-permute-start | bytes 12296 | tf_op jit(solution)/shard_map/ppermute | solution.py:419
  85.1 7.9 %collective-permute-start.11 = (f32[8,128]{1,0:T(8,128)S(1)}, f32[8,128]{1,0:T(8,128)S(1)}, u32[]{:S(2)}, u32[]{:S(2)}) collective-permute-start(f32[8,128]{1,0:T(8,128)S(1)} %get-tuple-element.29.refs_0_), channel_id=1, source_target_pairs={{192,0},{128,64},{64,128},{0,192},{448,256},{384,320},{320,384},{2... | collective-permute-start | bytes 12296 | tf_op jit(solution)/shard_map/ppermute | solution.py:419
  104.2 11.4 %collective-permute-start.21 = (bf16[128,512]{1,0:T(8,128)(2,1)S(1)}, bf16[128,512]{1,0:T(8,128)(2,1)S(1)}, u32[]{:S(2)}, u32[]{:S(2)}) collective-permute-start(bf16[128,512]{1,0:T(8,128)(2,1)S(1)} %get-tuple-element.39), channel_id=1, source_target_pairs={{48,0},{49,1},{50,2},{51,3},{52,4},{53,5},{54,6},{55,7},{56,8},{57... | collective-permute-start | bytes 393224 | tf_op jit(solution)/shard_map/ppermute | solution.py:419
  106.4 9.2 %collective-permute-start.22 = (bf16[128,512]{1,0:T(8,128)(2,1)S(1)}, bf16[128,512]{1,0:T(8,128)(2,1)S(1)}, u32[]{:S(2)}, u32[]{:S(2)}) collective-permute-start(bf16[128,512]{1,0:T(8,128)(2,1)S(1)} %get-tuple-element.40), channel_id=1, source_target_pairs={{32,0},{33,1},{34,2},{35,3},{36,4},{37,5},{38,6},{39,7},{40,8},{41... | collective-permute-start | bytes 393224 | tf_op jit(solution)/shard_map/ppermute | solution.py:419
  112.7 40.6 %collective-permute-start.16 = (bf16[80,512]{1,0:T(8,128)(2,1)S(1)}, bf16[80,512]{1,0:T(8,128)(2,1)S(1)}, u32[]{:S(2)}, u32[]{:S(2)}) collective-permute-start(bf16[80,512]{1,0:T(8,128)(2,1)S(1)} %get-tuple-element.37), channel_id=1, source_target_pairs={{64,0},{0,64},{192,128},{128,192},{320,256},{256,320},{448,384},{3... | collective-permute-start | bytes 245768 | tf_op jit(solution)/shard_map/ppermute | solution.py:419
  119.4 11.9 %collective-permute-start.24 = (bf16[32,512]{1,0:T(8,128)(2,1)}, bf16[32,512]{1,0:T(8,128)(2,1)S(1)}, u32[]{:S(2)}, u32[]{:S(2)}) collective-permute-start(bf16[32,512]{1,0:T(8,128)(2,1)} %get-tuple-element.43), channel_id=1, source_target_pairs={{15,0},{0,1},{1,2},{2,3},{3,4},{4,5},{5,6},{6,7},{7,8},{8,9},{9,10... | collective-permute-start | bytes 98312 | tf_op jit(solution)/shard_map/ppermute | solution.py:419
  123.3 8.1 %collective-permute-start.25 = (bf16[32,512]{1,0:T(8,128)(2,1)}, bf16[32,512]{1,0:T(8,128)(2,1)S(1)}, u32[]{:S(2)}, u32[]{:S(2)}) collective-permute-start(bf16[32,512]{1,0:T(8,128)(2,1)} %get-tuple-element.44), channel_id=1, source_target_pairs={{14,0},{15,1},{0,2},{1,3},{2,4},{3,5},{4,6},{5,7},{6,8},{7,9},{8,1... | collective-permute-start | bytes 98312 | tf_op jit(solution)/shard_map/ppermute | solution.py:419
  136.4 23.3 %collective-permute-start.27 = (f32[8,512]{1,0:T(8,128)}, f32[8,512]{1,0:T(8,128)S(1)}, u32[]{:S(2)}, u32[]{:S(2)}) collective-permute-start(f32[8,512]{1,0:T(8,128)} %get-tuple-element.47), channel_id=1, source_target_pairs={{12,0},{13,1},{14,2},{15,3},{0,4},{1,5},{2,6},{3,7},{4,8},{5,9},{6... | collective-permute-start | bytes 49160 | tf_op jit(solution)/shard_map/ppermute | solution.py:419
  142.1 20.3 %collective-permute-start.28 = (f32[8,512]{1,0:T(8,128)}, f32[8,512]{1,0:T(8,128)S(1)}, u32[]{:S(2)}, u32[]{:S(2)}) collective-permute-start(f32[8,512]{1,0:T(8,128)} %get-tuple-element.48), channel_id=1, source_target_pairs={{8,0},{9,1},{10,2},{11,3},{12,4},{13,5},{14,6},{15,7},{0,8},{1,9},... | collective-permute-start | bytes 49160 | tf_op jit(solution)/shard_map/ppermute | solution.py:419
  146.3 16.1 %collective-permute-start.29 = (f32[8,512]{1,0:T(8,128)}, f32[8,512]{1,0:T(8,128)S(1)}, u32[]{:S(2)}, u32[]{:S(2)}) collective-permute-start(f32[8,512]{1,0:T(8,128)} %get-tuple-element.49), channel_id=1, source_target_pairs={{4,0},{5,1},{6,2},{7,3},{8,4},{9,5},{10,6},{11,7},{12,8},{13,9},{1... | collective-permute-start | bytes 49160 | tf_op jit(solution)/shard_map/ppermute | solution.py:419
  153.3 23.7 %collective-permute-start.19 = (bf16[80,512]{1,0:T(8,128)(2,1)S(1)}, bf16[80,512]{1,0:T(8,128)(2,1)S(1)}, u32[]{:S(2)}, u32[]{:S(2)}) collective-permute-start(bf16[80,512]{1,0:T(8,128)(2,1)S(1)} %get-tuple-element.54), channel_id=1, source_target_pairs={{384,0},{448,64},{256,128},{320,192},{128,256},{192,320},{0,384},{... | collective-permute-start | bytes 245768 | tf_op jit(solution)/shard_map/ppermute | solution.py:419
  157.8 21.8 %collective-permute-start.18 = (bf16[80,512]{1,0:T(8,128)(2,1)S(1)}, bf16[80,512]{1,0:T(8,128)(2,1)S(1)}, u32[]{:S(2)}, u32[]{:S(2)}) collective-permute-start(bf16[80,512]{1,0:T(8,128)(2,1)S(1)} %get-tuple-element.54), channel_id=1, source_target_pairs={{256,0},{320,64},{384,128},{448,192},{0,256},{64,320},{128,384},{1... | collective-permute-start | bytes 245768 | tf_op jit(solution)/shard_map/ppermute | solution.py:419
  159.8 19.9 %collective-permute-start.17 = (bf16[80,512]{1,0:T(8,128)(2,1)S(1)}, bf16[80,512]{1,0:T(8,128)(2,1)S(1)}, u32[]{:S(2)}, u32[]{:S(2)}) collective-permute-start(bf16[80,512]{1,0:T(8,128)(2,1)S(1)} %get-tuple-element.54), channel_id=1, source_target_pairs={{128,0},{192,64},{0,128},{64,192},{384,256},{448,320},{256,384},{3... | collective-permute-start | bytes 245768 | tf_op jit(solution)/shard_map/ppermute | solution.py:419
  170.6 12.2 %collective-permute-start.33 = (f32[8,512]{1,0:T(8,128)S(1)}, f32[8,512]{1,0:T(8,128)S(1)}, u32[]{:S(2)}, u32[]{:S(2)}) collective-permute-start(f32[8,512]{1,0:T(8,128)S(1)} %add.45), channel_id=1, source_target_pairs={{384,0},{448,64},{256,128},{320,192},{128,256},{192,320},{0,384},{... | collective-permute-start | bytes 49160 | tf_op jit(solution)/shard_map/ppermute | solution.py:419
  (23 other events, 72.8 us)

commit v3 on v1

--- a/solution.py
+++ b/solution.py
@@ -13,14 +13,18 @@
 STEPS = S // GROUP
 WIDE = GROUP * LANES
 PRED_PAD = 80
+VMEM_BYTES = 40 * 2**20
+
+masked_log = -1e30
+
+F32 = jnp.float32
+BF16 = jnp.bfloat16
+
 PRED_SHARE = 17
 PRED_SLOT = 32
-VMEM_BYTES = 40 * 2**20
-
-masked_log = -1e30
-
-F32 = jnp.float32
-BF16 = jnp.bfloat16
+TM = ("y", "core")
+NEAR = ("x", "zl")
+FAR = "zh"
 
 NT_DIMS = (((1,), (1,)), ((), ()))
 
@@ -41,9 +45,15 @@
     return jnp.concatenate([pair[0:1, :], pair[1:2, :]], axis=1)
 
 
+def balanced(combine, terms):
+    while len(terms) > 1:
+        terms = [combine(a, b) for a, b in zip(terms[0::2], terms[1::2])]
+    return terms[0]
+
+
 def rowwise_logsumexp(terms):
-    top = functools.reduce(jnp.maximum, terms)
-    total = functools.reduce(lambda a, b: a + b, [jnp.exp(t - top) for t in terms])
+    top = balanced(jnp.maximum, terms)
+    total = balanced(jnp.add, [jnp.exp(t - top) for t in terms])
     return top + jnp.log(total)
 
 
@@ -58,6 +68,36 @@
         total = jnp.sum(jnp.exp(terms - top), axis=0, keepdims=True)
         rows_ref[i : i + 1, :] = top + jnp.log(total)
     return rows_ref[...]
+
+
+def window_down(vector, distance):
+    places = row_ids((S, LANES))
+    for bit in (1, 2, 4, 8):
+        moved = jnp.where(places < S - bit, pltpu.roll(vector, S - bit, 0), masked_log)
+        vector = jnp.where((distance & bit) != 0, moved, vector)
+    return vector
+
+
+def window_up(vector, distance):
+    places = row_ids((S, LANES))
+    for bit in (1, 2, 4, 8):
+        moved = jnp.where(places >= bit, pltpu.roll(vector, bit, 0), masked_log)
+        vector = jnp.where((distance & bit) != 0, moved, vector)
+    return vector
+
+
+def slot_row(slot, own_rows, width):
+    if own_rows != 8:
+        return slot
+    share = width // 8
+    tm, x, zl, zh = slot // share, slot // 16 % 4, slot // 8 % 2, slot % 8
+    return (x * 16 + zh * 2 + zl) * own_rows + tm
+
+
+def frame_shifts(starts, half):
+    lanes = lane_ids()
+    first = (lanes == 0) | (lanes == half)
+    return jnp.where(first, 0, starts - pltpu.roll(starts, 1, 1))
 
 
 def span_rows(blank, emit):
@@ -104,10 +144,9 @@
 
 
 def forward_kernel(
-    piece,
+    own_rows,
     vocab,
     starts_ref,
-    prior_ref,
     frames_ref,
     labels_len_ref,
     block_ref,
@@ -127,11 +166,8 @@
 
     @pl.when(step == 0)
     def _():
-        own = row_ids((width, width))
-        got = lane_ids((width, width))
-        share = width // 8
-        source = (got % share) // piece * (8 * piece) + got // share * piece + got % piece
-        turn = (own == source).astype(BF16)
+        source = slot_row(lane_ids((width, width)), own_rows, width)
+        turn = (row_ids((width, width)) == source).astype(BF16)
         weights = jnp.dot(turn, gathered_ref[...], preferred_element_type=F32)
         weights_ref[...] = weights.astype(BF16)
         weights_t[...] = jnp.transpose(weights).astype(BF16)
@@ -170,9 +206,7 @@
         emit = jnp.where(allowed, lps_ref[1], masked_log)
         lps_ref[0] = blank
         lps_ref[1] = emit
-        before = pltpu.roll(starts, 1, 1)
-        before = jnp.where(lanes == 0, prior_ref[0], jnp.where(lanes == half, prior_ref[1], before))
-        shift = starts - before
+        shift = frame_shifts(starts, half)
         rows = span_rows(blank, emit)
         for bit in (1, 2, 4, 8):
             moved = (shift & bit) != 0
@@ -195,22 +229,22 @@
                     root[i] = row
                 return carry
 
-            lax.fori_loop(0, S, product, 0)
+            lax.fori_loop(0, S, product, 0, unroll=4)
         flat = jnp.transpose(root[...].reshape(S * S, LANES))
         payload_ref[...] = jnp.zeros_like(payload_ref)
         for b in range(2):
             line = flat[b * half : b * half + 1, :]
             payload_ref[4 * b : 4 * b + 1, :] = line[:, :LANES]
             payload_ref[4 * b + 1 : 4 * b + 2, :] = line[:, LANES:]
-            last = starts_ref[b : b + 1, half - 1 : half].astype(F32)
-            payload_ref[4 * b + 2 : 4 * b + 3, :] = jnp.broadcast_to(last, (1, LANES))
+            for end, at in ((2, half - 1), (3, 0)):
+                edge_start = starts_ref[b : b + 1, at : at + 1].astype(F32)
+                payload_ref[4 * b + end : 4 * b + end + 1, :] = jnp.broadcast_to(edge_start, (1, LANES))
 
 
 def backward_kernel(
-    piece,
-    vocab,
+    own_rows,
+    label_rows,
     starts_ref,
-    prior_ref,
     frames_ref,
     labels_len_ref,
     block_ref,
@@ -242,23 +276,30 @@
     def _():
         places = row_ids((S, LANES))
         line_up[...] = jnp.zeros_like(line_up)
+        ends = jnp.zeros((1, LANES), F32)
+        begins = jnp.zeros((1, LANES), F32)
         for r in range(count):
             for b in range(2):
                 at = 2 * r + b
-                line_up[at : at + 1, :LANES] = blocks_ref[r, 4 * b : 4 * b + 1, :]
-                line_up[at : at + 1, LANES:] = blocks_ref[r, 4 * b + 1 : 4 * b + 2, :]
-        chain[...] = jnp.transpose(line_up[...]).reshape(S, S, LANES)
+                line_up[0, at : at + 1, :] = blocks_ref[r, 4 * b : 4 * b + 1, :]
+                line_up[1, at : at + 1, :] = blocks_ref[r, 4 * b + 1 : 4 * b + 2, :]
+                ends = jnp.where(lanes == at, blocks_ref[r, 4 * b + 2 : 4 * b + 3, :], ends)
+                begins = jnp.where(lanes == at, blocks_ref[r, 4 * b + 3 : 4 * b + 4, :], begins)
+        for h in range(2):
+            chain[h * S // 2 : (h + 1) * S // 2] = jnp.transpose(line_up[h]).reshape(S // 2, S, LANES)
         odd = lanes % 2 == 1
         last_start = [blocks_ref[count - 1, 4 * b + 2 : 4 * b + 3, :].astype(jnp.int32) for b in range(2)]
         final_place = jnp.where(odd, labels_len_ref[1] - last_start[1], labels_len_ref[0] - last_start[0])
+        gap = (begins - pltpu.roll(ends, 2, 1)).astype(jnp.int32)
+        gap = jnp.where((lanes >= 2) & (lanes < 2 * count), gap, 0)
         forward = jnp.where(places == 0, 0.0, masked_log) + jnp.zeros((S, LANES), F32)
         closing = jnp.where(places == final_place, 0.0, masked_log)
         backward = closing
         owner = lanes // 2
         for turn in range(count - 1):
-            ahead = pltpu.roll(vector_times(forward, chain), 2, 1)
+            ahead = window_down(pltpu.roll(vector_times(forward, chain), 2, 1), gap)
             forward = jnp.where(owner == turn + 1, ahead, forward)
-            behind = pltpu.roll(times_vector(chain, backward, rows_ref), LANES - 2, 1)
+            behind = pltpu.roll(window_up(times_vector(chain, backward, rows_ref), gap), LANES - 2, 1)
             backward = jnp.where(owner == count - 2 - turn, behind, backward)
         leaving = vector_times(forward, chain) + closing
         best = jnp.max(leaving, axis=0, keepdims=True)
@@ -287,12 +328,7 @@
             behind = times_vector(tree_ref.at[level], beta_late, rows_ref)
             beta = jnp.where(later, beta_late, pltpu.roll(behind, LANES - reach, 1))
         starts = rows_to_lanes(starts_ref[...])
-        before = pltpu.roll(starts, 1, 1)
-        before = jnp.where(lanes == 0, prior_ref[0], jnp.where(lanes == half, prior_ref[1], before))
-        shift = starts - before
-        for bit in (1, 2, 4, 8):
-            moved = jnp.where(places < S - bit, pltpu.roll(alpha, S - bit, 0), masked_log)
-            alpha = jnp.where((shift & bit) != 0, moved, alpha)
+        alpha = window_down(alpha, frame_shifts(starts, half))
         spans = span_rows(lps_ref[0], lps_ref[1])
         scores = [spans[e] + alpha[e : e + 1, :] + beta for e in range(S)]
         best = jnp.max(functools.reduce(jnp.maximum, scores), axis=0, keepdims=True)
@@ -330,9 +366,8 @@
     starts = rows_to_lanes(starts_ref[...])
     base = starts + step * GROUP
     rows = jnp.concatenate([base + k for k in range(GROUP)], axis=1)
-    second = jnp.concatenate([per_lane(half, 0, 65)] * GROUP, axis=1)
+    wanted = rows + jnp.concatenate([per_lane(half, 0, label_rows)] * GROUP, axis=1)
     slot = row_ids((8 * PRED_SLOT, WIDE))
-    wanted = rows + second
     match = (slot // PRED_SLOT * PRED_SHARE + slot % PRED_SLOT == wanted) & (slot % PRED_SLOT < PRED_SHARE)
     pred_sum[...] += lax.dot_general(
         match.astype(BF16), grad_summed.astype(BF16), NT_DIMS, preferred_element_type=F32
@@ -343,8 +378,7 @@
     def _():
         grad_enc_ref[...] = jnp.transpose(enc_sum[...]).astype(BF16)
         share = width // 8
-        got = row_ids((width, width))
-        source = (got % share) // piece * (8 * piece) + got // share * piece + got % piece
+        source = slot_row(row_ids((width, width)), own_rows, width)
         turn = (lane_ids((width, width)) == source).astype(BF16)
         turned = jnp.dot(turn, weight_sum[...].astype(BF16), preferred_element_type=F32).astype(BF16)
         for p in range(8):
@@ -363,32 +397,34 @@
 smem = pl.BlockSpec(memory_space=pltpu.SMEM)
 
 
-def from_behind(block, axis, distance):
-    devices = range(lax.axis_size(axis))
-    route = [(i - distance, i) for i in devices if i - distance in devices]
-    return lax.ppermute(block, axis, route)
+def exchange(blocks, axes):
+    return lax.all_to_all(blocks, axes, 0, 0, tiled=True)
+
+
+def share_copies(block, axes):
+    count = lax.axis_size(axes)
+    return exchange(jnp.broadcast_to(block[None], (count, *block.shape)), axes)
 
 
 def per_device(encoder, predictor, starts, frame_lengths, label_lengths, labels, w_out):
     utt_count, frame_count, width = encoder.shape
     own_rows, vocab = w_out.shape
-    tm_index = lax.axis_index("tm")
-    tm_count = lax.axis_size("tm")
-    utt_size = lax.axis_size("utt")
+    label_rows = predictor.shape[1]
+    tm_index = lax.axis_index(TM)
+    tm_count = lax.axis_size(TM)
+    near, far = lax.axis_size(NEAR), lax.axis_size(FAR)
     piece = own_rows // tm_count
     padded = -(-vocab // LANES) * LANES
+    fold = piece * padded // LANES
     share = width // tm_count
     rows = S * utt_count * frame_count
     shape = jax.ShapeDtypeStruct
 
     mine = lax.dynamic_slice_in_dim(w_out, tm_index * piece, piece, axis=0)
-    mine = jnp.pad(mine, ((0, 0), (0, padded - vocab)))
-    across = lax.all_to_all(
-        jnp.broadcast_to(mine.reshape(1, piece * padded // LANES, LANES), (utt_size, piece * padded // LANES, LANES)),
-        "utt", 0, 0, tiled=True,
-    )
-    gathered = lax.all_gather(across.reshape(share, padded), "tm", axis=0, tiled=True)
-    prior = from_behind(starts[:, -1], "tm", 1)
+    mine = jnp.pad(mine, ((0, 0), (0, padded - vocab))).reshape(fold, LANES)
+    held = share_copies(mine, FAR).reshape(far * piece, padded)
+    held = share_copies(held, NEAR).reshape(share, padded)
+    gathered = share_copies(held, TM).reshape(width, padded)
     block = tm_index.reshape(1).astype(jnp.int32)
 
     hidden, label_ids = pl.pallas_call(
@@ -415,11 +451,10 @@
 
     levels = frame_count.bit_length() - 1
     exps, weights, lps, tree, payload = pl.pallas_call(
-        functools.partial(forward_kernel, piece, vocab),
+        functools.partial(forward_kernel, own_rows, vocab),
         grid=(STEPS,),
         in_specs=[
             whole(starts.shape),
-            smem,
             smem,
             smem,
             smem,
@@ -441,21 +476,23 @@
             shape((levels, S, S, LANES), F32),
             shape((8, LANES), F32),
         ],
-        scratch_shapes=[pltpu.VMEM((padded, width), BF16), pltpu.VMEM((S, S, LANES), F32)],
+        scratch_shapes=[
+            pltpu.VMEM((padded, width), BF16),
+            pltpu.VMEM((S, S, LANES), F32),
+        ],
         compiler_params=params(),
         cost_estimate=pl.CostEstimate(
             flops=2 * padded * width * rows, bytes_accessed=8 * 2**20, transcendentals=padded * rows
         ),
-    )(starts, prior, frame_lengths, label_lengths, block, label_ids, gathered, hidden)
-
-    blocks = lax.all_gather(payload, "tm", axis=0)
+    )(starts, frame_lengths, label_lengths, block, label_ids, gathered, hidden)
+
+    blocks = share_copies(payload, TM)
 
     losses, grad_encoder, send = pl.pallas_call(
-        functools.partial(backward_kernel, piece, vocab),
+        functools.partial(backward_kernel, own_rows, label_rows),
         grid=(STEPS,),
         in_specs=[
             whole(starts.shape),
-            smem,
             smem,
             smem,
             smem,
@@ -467,7 +504,11 @@
             pl.BlockSpec((width, WIDE), lambda i: (0, i)),
             pl.BlockSpec((padded, WIDE), lambda i: (0, i)),
         ],
-        out_specs=[smem, whole((utt_count * frame_count, width)), whole((tm_count, share + PRED_SLOT, padded))],
+        out_specs=[
+            smem,
+            whole((utt_count * frame_count, width)),
+            whole((tm_count, share + PRED_SLOT, padded)),
+        ],
         out_shape=[
             shape((utt_count,), F32),
             shape((utt_count * frame_count, width), BF16),
@@ -475,7 +516,7 @@
         ],
         scratch_shapes=[
             pltpu.VMEM((S, S, LANES), F32),
-            pltpu.VMEM((LANES, S * S), F32),
+            pltpu.VMEM((2, LANES, LANES), F32),
             pltpu.VMEM((S, LANES), F32),
             pltpu.VMEM((2, S, LANES), F32),
             pltpu.VMEM((width, LANES), F32),
@@ -486,35 +527,38 @@
         cost_estimate=pl.CostEstimate(
             flops=6 * padded * width * rows, bytes_accessed=8 * 2**20, transcendentals=2**16
         ),
-    )(starts, prior, frame_lengths, label_lengths, block, blocks, lps, tree, label_ids, weights, hidden, exps)
-
-    came = lax.all_to_all(send, "tm", 0, 0, tiled=True)
-    block_sum = jnp.sum(came.astype(F32), axis=0)
-    weight_rows = block_sum[:share].reshape(utt_size, piece * padded // LANES, LANES)
+    )(starts, frame_lengths, label_lengths, block, blocks, lps, tree, label_ids, weights, hidden, exps)
+
+    block_sum = jnp.sum(exchange(send, TM).astype(F32), axis=0)
     pred_rows = block_sum[share : share + PRED_SHARE]
-    across = lax.all_to_all(weight_rows, "utt", 0, 0, tiled=True)
-    own_weight = jnp.sum(across, axis=0).reshape(piece, padded)
-    final = lax.all_gather(jnp.concatenate([pred_rows, own_weight], axis=0), "tm", axis=0)
-    label_rows = predictor.shape[1]
+    near_sum = jnp.sum(exchange(block_sum[:share].reshape(near, share // near, padded), NEAR), axis=0)
+    own_weight = jnp.sum(exchange(near_sum.reshape(far, fold, LANES), FAR), axis=0).reshape(piece, padded)
+    final = share_copies(jnp.concatenate([pred_rows, own_weight], axis=0), TM)
     grad_predictor = final[:, :PRED_SHARE].reshape(-1, width)[: utt_count * label_rows]
     grad_predictor = grad_predictor.reshape(utt_count, label_rows, width)
     grad_w_out = final[:, PRED_SHARE:, :vocab].reshape(own_rows, vocab)
     return (losses, grad_encoder.reshape(encoder.shape), grad_predictor, grad_w_out)
 
 
+def finer(mesh):
+    sizes = (4, 2, 4, 8, 2) if mesh.shape["utt"] == 64 else (4, 2, 1, 1, 1)
+    return jax.sharding.Mesh(mesh.devices.reshape(sizes), (*TM, "x", FAR, "zl"))
+
+
 def solution(mesh):
+    utt = ("x", FAR, "zl")
     return jax.shard_map(
         per_device,
-        mesh=mesh,
+        mesh=finer(mesh),
         in_specs=(
-            P("utt", "tm", None),
-            P("utt", None, None),
-            P("utt", "tm"),
-            P("utt"),
-            P("utt"),
-            P("utt", None),
-            P("utt", None),
+            P(utt, TM, None),
+            P(utt, None, None),
+            P(utt, TM),
+            P(utt),
+            P(utt),
+            P(utt, None),
+            P(utt, None),
         ),
-        out_specs=(P("utt"), P("utt", "tm", None), P("utt", None, None), P("utt", None)),
+        out_specs=(P(utt), P(utt, TM, None), P(utt, None, None), P(utt, None)),
         check_vma=False,
     )

time: 140 us -> 136 us (0.971)
  blocking collectives: 60.5 us -> 81.4 us
  starting transfers between devices: 31.2 us -> 11.3 us
  local copies, waits for them, and re-layouts: 7.74 us -> 4.74 us
  Pallas kernels: 21.8 us -> 19.4 us
    all_to_all x1 -> x6, blocking collectives: 15.9 us -> 81.4 us  [exchange(): return lax.all_to_all(blocks, axes, 0, 0, tiled=True)]
    all_gather x3 -> x0, blocking collectives: 44.6 us -> none  [the longest x1 16.2 us: per_device(): lax.all_gather(jnp.concatenate([pred_rows, own_weight], axis=0), 'tm', ax...]
    all_to_all x2, starting transfers between devices: 27.2 us -> 11.3 us  [exchange(): return lax.all_to_all(blocks, axes, 0, 0, tiled=True)]
    ppermute x1 -> x0, starting transfers between devices: 4.04 us -> none  [from_behind(): return lax.ppermute(block, axis, route)]
    pallas_call x2, Pallas kernels: 19.9 us -> 17.5 us  [the longest x1 9.25 us: per_device(): pl.pallas_call(functools.partial(backward_kernel, own_rows, label_rows),...]
    unnamed x18 -> x16, local copies, waits for them, and re-layouts: 5.38 us -> 3.1 us
  transfers between devices with their start and end apart: 3 -> 2, of which waited for: 2 -> 2; matrix products, arithmetic and copies ran while one was open for 1% -> 1% of each run, Pallas kernels for 1% -> 1%
where the time goes in v3:
time: 136 us
  blocking collectives  81.4 us (60%)
  Pallas kernels  19.4 us (14%)
  waiting for transfers between devices  17.9 us (13%)
  starting transfers between devices  11.3 us (8%)
  local copies, waits for them, and re-layouts  4.74 us (3%)
    all_to_all x6, blocking collectives, exchange(): return lax.all_to_all(blocks, axes, 0, 0, tiled=True)  81.4 us
    all_to_all x2, waiting for transfers between devices, exchange(): return lax.all_to_all(blocks, axes, 0, 0, tiled=True)  17.9 us
    all_to_all x2, starting transfers between devices, exchange(): return lax.all_to_all(blocks, axes, 0, 0, tiled=True)  11.3 us
    pallas_call x1, Pallas kernels, per_device(): pl.pallas_call(functools.partial(backward_kernel, own_rows, label_rows),...  9.25 us
    pallas_call x1, Pallas kernels, per_device(): pl.pallas_call(functools.partial(forward_kernel, own_rows, vocab), grid=(...  8.2 us
    unnamed x16, local copies, waits for them, and re-layouts  3.1 us
  transfers between devices with their start and end apart: 2, of which 2 were waited for; matrix products, arithmetic and copies ran while one was open for 1% of the time, Pallas kernels for 1%

profile of v3, /device:TPU:1, one launch (start us, length us, event | category | flops | bytes accessed | tf_op | source)
XLA Modules:
  0.0 135.7 jit_solution(7172140795286449999)
XLA Ops:
  0.6 0.0 copy-start
  0.7 0.6 copy-done
  1.4 26.8 %all_to_all.40 = bf16[8,4,128]{2,1,0:T(4,128)(2,1)S(1)} all-to-all(bf16[8,4,128]{2,1,0:T(4,128)(2,1)S(1)} %broadcast_in_dim.34), channel_id=1, replica_groups=mesh['y'=4,'core'=2,'x'=4,'zh'=8,'zl'=2] {'zh'}, dimensions={0} | all-to-all | bytes 16384 | tf_op jit(solution)/shard_map/all_to_all | solution.py:401
  28.2 9.5 %all_to_all.41 = bf16[8,8,512]{2,1,0:T(8,128)(2,1)S(1)} all-to-all(bf16[8,8,512]{2,1,0:T(8,128)(2,1)S(1)} %broadcast_in_dim.36), channel_id=1, replica_groups=mesh['y'=4,'core'=2,'x'=4,'zh'=8,'zl'=2] {'x','zl'}, dimensions={0} | all-to-all | bytes 131072 | tf_op jit(solution)/shard_map/all_to_all | solution.py:401
  37.7 0.8 broadcast_in_dim.38
  38.5 8.0 %all-to-all-start.2 = ((bf16[8,64,512]{2,1,0:T(8,128)(2,1)}), bf16[8,64,512]{2,1,0:T(8,128)(2,1)S(1)}, u32[]{:S(2)}, u32[]{:S(2)}) async-start(bf16[8,64,512]{2,1,0:T(8,128)(2,1)} %broadcast_in_dim.38), calls=%async_computation.2 | async-start | bytes 1048576 | tf_op jit(solution)/shard_map/all_to_all | solution.py:401
  46.5 0.9 copy.15.pred_ref
  47.4 0.0 copy-done.3
  47.4 0.0 copy-done.2
  47.5 1.9 %shard_map.102 = (bf16[512,2048]{1,0:T(8,128)(2,1)S(1)}, s32[16,128]{1,0:T(8,128)S(1)}) custom-call(s32[2,64]{1,0:T(2,128)S(1)} %copy-done.3, s32[2,64]{1,0:T(2,128)S(1)} %copy-done.2, bf16[128,512]{1,0:T(8,128)(2,1)S(1)} %bitcast.19, bf16[2,65,512]{2,1,0:T(8,128)(2,1)S(1)} %copy.15.pred_ref), custom_call_target="tpu_custom_call" | custom-call | flops 335544320 | bytes 3145728 | tf_op jit(solution)/shard_map/pallas_call | solution.py:430
  49.4 6.6 %all-to-all-done.2 = bf16[8,64,512]{2,1,0:T(8,128)(2,1)S(1)} async-done(((bf16[8,64,512]{2,1,0:T(8,128)(2,1)}), bf16[8,64,512]{2,1,0:T(8,128)(2,1)S(1)}, u32[]{:S(2)}, u32[]{:S(2)}) %all-to-all-start.2) | async-done | bytes 524320 | tf_op jit(solution)/shard_map/all_to_all | solution.py:401
  56.0 8.2 %shard_map.103 = (f32[512,2048]{1,0:T(8,128)S(1)}, bf16[512,512]{1,0:T(8,128)(2,1)S(1)}, f32[3,16,128]{2,1,0:T(8,128)S(1)}, f32[6,16,16,128]{3,2,1,0:T(8,128)S(1)}, f32[8,128]{1,0:T(8,128)S(1)}) custom-call(s32[2,64]{1,0:T(2,128)S(1)} %copy-done.3, s32[2]{0:T(128)S(1)} %copy-done.4, s32[2]{0:T(128)S(1)} %copy-done.5, s32[1]{0:T(128)} %bitcast.block_ref, ...), custom_call_target="tpu_custom_call" | custom-call | flops 1073741824 | bytes 8388608 | tf_op jit(solution)/shard_map/pallas_call | solution.py:453
  64.2 8.0 %all_to_all.42.blocks_ref = f32[8,8,128]{2,1,0:T(8,128)S(1)} all-to-all(f32[8,8,128]{2,1,0:T(8,128)S(1)} %broadcast_in_dim.39), channel_id=1, replica_groups=mesh['y'=4,'core'=2,'x'=4,'zh'=8,'zl'=2] {'y','core'}, dimensions={0} | all-to-all | bytes 65536 | tf_op jit(solution)/shard_map/all_to_all | solution.py:401
  72.2 9.3 %shard_map.104 = (f32[2]{0:T(128)}, bf16[128,512]{1,0:T(8,128)(2,1)}, bf16[8,96,512]{2,1,0:T(8,128)(2,1)S(1)}) custom-call(s32[2,64]{1,0:T(2,128)S(1)} %copy-done.3, s32[2]{0:T(128)S(1)} %copy-done.4, s32[2]{0:T(128)S(1)} %copy-done.5, s32[1]{0:T(128)} %bitcast.block_ref, f32[8,8,128]{2,1,0:T(8,128)S(1)} %all_to_all.42.blocks_ref, ...), custom_call_target="tpu_custom_call" | custom-call | flops 3221225472 | bytes 8388608 | tf_op jit(solution)/shard_map/pallas_call | solution.py:491
  81.4 15.4 %all_to_all.43 = bf16[8,96,512]{2,1,0:T(8,128)(2,1)S(1)} all-to-all(bf16[8,96,512]{2,1,0:T(8,128)(2,1)S(1)} %get-tuple-element.23), channel_id=1, replica_groups=mesh['y'=4,'core'=2,'x'=4,'zh'=8,'zl'=2] {'y','core'}, dimensions={0} | all-to-all | bytes 1572864 | tf_op jit(solution)/shard_map/all_to_all | solution.py:401
  96.8 0.1 convert_reduce_fusion
  96.9 8.0 %all_to_all.44 = f32[8,8,512]{2,1,0:T(8,128)S(1)} all-to-all(f32[8,8,512]{2,1,0:T(8,128)S(1)} %slice_bitcast_fusion), channel_id=1, replica_groups=mesh['y'=4,'core'=2,'x'=4,'zh'=8,'zl'=2] {'x','zl'}, dimensions={0} | all-to-all | bytes 262144 | tf_op jit(solution)/shard_map/all_to_all | solution.py:401
  104.9 0.6 reshape.48
  105.5 3.3 %all-to-all-start.6 = ((f32[8,4,128]{2,1,0:T(4,128)}), f32[8,4,128]{2,1,0:T(4,128)S(1)}, u32[]{:S(2)}, u32[]{:S(2)}) async-start(f32[8,4,128]{2,1,0:T(4,128)} %reshape.48), calls=%async_computation.6 | async-start | bytes 32768 | tf_op jit(solution)/shard_map/all_to_all | solution.py:401
  108.9 11.3 %all-to-all-done.6 = f32[8,4,128]{2,1,0:T(4,128)S(1)} async-done(((f32[8,4,128]{2,1,0:T(4,128)}), f32[8,4,128]{2,1,0:T(4,128)S(1)}, u32[]{:S(2)}, u32[]{:S(2)}) %all-to-all-start.6) | async-done | bytes 16416 | tf_op jit(solution)/shard_map/all_to_all | solution.py:401
  120.3 13.8 %all_to_all.45 = f32[8,18,512]{2,1,0:T(8,128)S(1)} all-to-all(f32[8,18,512]{2,1,0:T(8,128)S(1)} %broadcast_in_dim.40), channel_id=1, replica_groups=mesh['y'=4,'core'=2,'x'=4,'zh'=8,'zl'=2] {'y','core'}, dimensions={0} | all-to-all | bytes 589824 | tf_op jit(solution)/shard_map/all_to_all | solution.py:401
  134.1 0.6 copy.21
  134.7 0.1 reshape.50
  134.8 0.9 copy.16
  (22 shorter events, 0.2 us)
Async XLA Ops:
  0.6 0.7 copy-start
  0.6 46.8 %copy-start.3 = (s32[2,64]{1,0:T(2,128)S(1)}, s32[2,64]{1,0:T(2,128)}, u32[]{:S(2)}) copy-start(s32[2,64]{1,0:T(2,128)} %starts_ref.5) | copy-start | bytes 1540
  0.7 46.8 %copy-start.2 = (s32[2,64]{1,0:T(2,128)S(1)}, s32[2,64]{1,0:T(2,128)}, u32[]{:S(2)}) copy-start(s32[2,64]{1,0:T(2,128)} %labels_ref.1) | copy-start | bytes 1540
  0.7 46.8 %copy-start.1 = (bf16[2,64,512]{2,1,0:T(8,128)(2,1)S(1)}, bf16[2,64,512]{2,1,0:T(8,128)(2,1)}, u32[]{:S(2)}) copy-start(bf16[2,64,512]{2,1,0:T(8,128)(2,1)} %param.7) | copy-start | bytes 393220
  0.7 55.3 %copy-start.4 = (s32[2]{0:T(128)S(1)}, s32[2]{0:T(128)}, u32[]{:S(2)}) copy-start(s32[2]{0:T(128)} %frames_ref.3) | copy-start | bytes 28
  0.7 55.3 %copy-start.5 = (s32[2]{0:T(128)S(1)}, s32[2]{0:T(128)}, u32[]{:S(2)}) copy-start(s32[2]{0:T(128)} %labels_len_ref.3) | copy-start | bytes 28
  38.5 17.5 %all-to-all-start.2 = ((bf16[8,64,512]{2,1,0:T(8,128)(2,1)}), bf16[8,64,512]{2,1,0:T(8,128)(2,1)S(1)}, u32[]{:S(2)}, u32[]{:S(2)}) async-start(bf16[8,64,512]{2,1,0:T(8,128)(2,1)} %broadcast_in_dim.38), calls=%async_computation.2 | async-start | bytes 1048576 | tf_op jit(solution)/shard_map/all_to_all | solution.py:401
  105.5 14.7 %all-to-all-start.6 = ((f32[8,4,128]{2,1,0:T(4,128)}), f32[8,4,128]{2,1,0:T(4,128)S(1)}, u32[]{:S(2)}, u32[]{:S(2)}) async-start(f32[8,4,128]{2,1,0:T(4,128)} %reshape.48), calls=%async_computation.6 | async-start | bytes 32768 | tf_op jit(solution)/shard_map/all_to_all | solution.py:401

commit v4 on v3

--- a/solution.py
+++ b/solution.py
@@ -22,9 +22,8 @@
 
 PRED_SHARE = 17
 PRED_SLOT = 32
-TM = ("y", "core")
-NEAR = ("x", "zl")
-FAR = "zh"
+TM = "tm"
+UTT = "utt"
 
 NT_DIMS = (((1,), (1,)), ((), ()))
 
@@ -90,8 +89,7 @@
     if own_rows != 8:
         return slot
     share = width // 8
-    tm, x, zl, zh = slot // share, slot // 16 % 4, slot // 8 % 2, slot % 8
-    return (x * 16 + zh * 2 + zl) * own_rows + tm
+    return slot % share * own_rows + slot // share
 
 
 def frame_shifts(starts, half):
@@ -218,18 +216,23 @@
         levels = half.bit_length() - 1
         for level in range(levels):
             reach = 1 << level
-            latter = [pltpu.roll(tree_ref[level, m], LANES - reach, 1) for m in range(S)]
-
-            def product(i, carry, level=level, latter=latter):
-                former = tree_ref[level, i]
+            late = lanes % (2 * reach) == reach
+            back = LANES - reach
+            latter = [tree_ref[level, m] for m in range(S)]
+            latter = [jnp.where(late, one, pltpu.roll(one, back, 1)) for one in latter]
+
+            def product(i, carry, level=level, reach=reach, late=late, back=back, latter=latter):
+                former = jnp.where(late, pltpu.roll(tree_ref[level, i + S // 2], reach, 1), tree_ref[level, i])
                 row = rowwise_logsumexp([former[m : m + 1, :] + latter[m] for m in range(S)])
                 if level + 1 < levels:
                     tree_ref[level + 1, i] = row
+                    tree_ref[level + 1, i + S // 2] = pltpu.roll(row, back, 1)
                 else:
                     root[i] = row
+                    root[i + S // 2] = pltpu.roll(row, back, 1)
                 return carry
 
-            lax.fori_loop(0, S, product, 0, unroll=4)
+            lax.fori_loop(0, S // 2, product, 0, unroll=4)
         flat = jnp.transpose(root[...].reshape(S * S, LANES))
         payload_ref[...] = jnp.zeros_like(payload_ref)
         for b in range(2):
@@ -412,7 +415,7 @@
     label_rows = predictor.shape[1]
     tm_index = lax.axis_index(TM)
     tm_count = lax.axis_size(TM)
-    near, far = lax.axis_size(NEAR), lax.axis_size(FAR)
+    utt_size = lax.axis_size(UTT)
     piece = own_rows // tm_count
     padded = -(-vocab // LANES) * LANES
     fold = piece * padded // LANES
@@ -422,8 +425,7 @@
 
     mine = lax.dynamic_slice_in_dim(w_out, tm_index * piece, piece, axis=0)
     mine = jnp.pad(mine, ((0, 0), (0, padded - vocab))).reshape(fold, LANES)
-    held = share_copies(mine, FAR).reshape(far * piece, padded)
-    held = share_copies(held, NEAR).reshape(share, padded)
+    held = share_copies(mine, UTT).reshape(share, padded)
     gathered = share_copies(held, TM).reshape(width, padded)
     block = tm_index.reshape(1).astype(jnp.int32)
 
@@ -530,35 +532,28 @@
     )(starts, frame_lengths, label_lengths, block, blocks, lps, tree, label_ids, weights, hidden, exps)
 
     block_sum = jnp.sum(exchange(send, TM).astype(F32), axis=0)
-    pred_rows = block_sum[share : share + PRED_SHARE]
-    near_sum = jnp.sum(exchange(block_sum[:share].reshape(near, share // near, padded), NEAR), axis=0)
-    own_weight = jnp.sum(exchange(near_sum.reshape(far, fold, LANES), FAR), axis=0).reshape(piece, padded)
-    final = share_copies(jnp.concatenate([pred_rows, own_weight], axis=0), TM)
-    grad_predictor = final[:, :PRED_SHARE].reshape(-1, width)[: utt_count * label_rows]
+    pred_rows = share_copies(block_sum[share : share + PRED_SHARE], TM)
+    weight_rows = exchange(block_sum[:share].reshape(utt_size, fold, LANES), UTT)
+    pred_rows, weight_rows = lax.optimization_barrier((pred_rows, weight_rows))
+    grad_w_out = share_copies(jnp.sum(weight_rows, axis=0), TM).reshape(own_rows, padded)
+    grad_predictor = pred_rows.reshape(-1, width)[: utt_count * label_rows]
     grad_predictor = grad_predictor.reshape(utt_count, label_rows, width)
-    grad_w_out = final[:, PRED_SHARE:, :vocab].reshape(own_rows, vocab)
-    return (losses, grad_encoder.reshape(encoder.shape), grad_predictor, grad_w_out)
-
-
-def finer(mesh):
-    sizes = (4, 2, 4, 8, 2) if mesh.shape["utt"] == 64 else (4, 2, 1, 1, 1)
-    return jax.sharding.Mesh(mesh.devices.reshape(sizes), (*TM, "x", FAR, "zl"))
+    return (losses, grad_encoder.reshape(encoder.shape), grad_predictor, grad_w_out[:, :vocab])
 
 
 def solution(mesh):
-    utt = ("x", FAR, "zl")
     return jax.shard_map(
         per_device,
-        mesh=finer(mesh),
+        mesh=mesh,
         in_specs=(
-            P(utt, TM, None),
-            P(utt, None, None),
-            P(utt, TM),
-            P(utt),
-            P(utt),
-            P(utt, None),
-            P(utt, None),
+            P(UTT, TM, None),
+            P(UTT, None, None),
+            P(UTT, TM),
+            P(UTT),
+            P(UTT),
+            P(UTT, None),
+            P(UTT, None),
         ),
-        out_specs=(P(utt), P(utt, TM, None), P(utt, None, None), P(utt, None)),
+        out_specs=(P(UTT), P(UTT, TM, None), P(UTT, None, None), P(UTT, None)),
         check_vma=False,
     )

time: 136 us -> 136 us (level)
  blocking collectives: 81.4 us -> 73.8 us
  starting transfers between devices: 11.3 us -> 17.5 us
    all_to_all x6 -> x4, blocking collectives: 81.4 us -> 73.8 us  [exchange(): return lax.all_to_all(blocks, axes, 0, 0, tiled=True)]
    all_to_all x2 -> x3, starting transfers between devices: 11.3 us -> 17.5 us  [exchange(): return lax.all_to_all(blocks, axes, 0, 0, tiled=True)]
    broadcast_in_dim x5, local copies, waits for them, and re-layouts: 0.87 us -> 2.27 us  [share_copies(): return exchange(jnp.broadcast_to(block[None], (count, *block.shape)), axes)]
    all_to_all x2 -> x3, waiting for transfers between devices: 17.9 us -> 18.3 us  [exchange(): return lax.all_to_all(blocks, axes, 0, 0, tiled=True)]
  transfers between devices with their start and end apart: 2 -> 3, of which waited for: 2 -> 3; matrix products, arithmetic and copies ran while one was open for 1% -> 1% of each run, Pallas kernels for 1% -> 1%
where the time goes in v4:
time: 136 us
  blocking collectives  73.8 us (54%)
  Pallas kernels  19.5 us (14%)
  waiting for transfers between devices  18.3 us (13%)
  starting transfers between devices  17.5 us (13%)
  local copies, waits for them, and re-layouts  5.58 us (4%)
    all_to_all x4, blocking collectives, exchange(): return lax.all_to_all(blocks, axes, 0, 0, tiled=True)  73.8 us
    all_to_all x3, waiting for transfers between devices, exchange(): return lax.all_to_all(blocks, axes, 0, 0, tiled=True)  18.3 us
    all_to_all x3, starting transfers between devices, exchange(): return lax.all_to_all(blocks, axes, 0, 0, tiled=True)  17.5 us
    pallas_call x1, Pallas kernels, per_device(): pl.pallas_call(functools.partial(backward_kernel, own_rows, label_rows),...  9.22 us
    pallas_call x1, Pallas kernels, per_device(): pl.pallas_call(functools.partial(forward_kernel, own_rows, vocab), grid=(...  8.38 us
    unnamed x16, local copies, waits for them, and re-layouts  3.14 us
  transfers between devices with their start and end apart: 3, of which 3 were waited for; matrix products, arithmetic and copies ran while one was open for 1% of the time, Pallas kernels for 1%

profile of v4, /device:TPU:1, one launch (start us, length us, event | category | flops | bytes accessed | tf_op | source)
XLA Modules:
  0.0 135.7 jit_solution(16101291797362734963)
XLA Ops:
  0.6 0.0 copy-start
  0.7 0.7 copy-done
  1.4 32.4 %all_to_all.35 = bf16[64,4,128]{2,1,0:T(4,128)(2,1)S(1)} all-to-all(bf16[64,4,128]{2,1,0:T(4,128)(2,1)S(1)} %broadcast_in_dim.15), channel_id=1, replica_groups=mesh['tm'=8,'utt'=64] {'utt'}, dimensions={0} | all-to-all | bytes 131072 | tf_op jit(solution)/shard_map/all_to_all | solution.py:404
  33.9 0.8 broadcast_in_dim.17
  34.7 6.6 %all-to-all-start.1 = ((bf16[8,64,512]{2,1,0:T(8,128)(2,1)}), bf16[8,64,512]{2,1,0:T(8,128)(2,1)S(1)}, u32[]{:S(2)}, u32[]{:S(2)}) async-start(bf16[8,64,512]{2,1,0:T(8,128)(2,1)} %broadcast_in_dim.17), calls=%async_computation.1 | async-start | bytes 1048576 | tf_op jit(solution)/shard_map/all_to_all | solution.py:404
  41.3 0.9 copy.14.pred_ref
  42.2 1.9 %shard_map.102 = (bf16[512,2048]{1,0:T(8,128)(2,1)S(1)}, s32[16,128]{1,0:T(8,128)S(1)}) custom-call(s32[2,64]{1,0:T(2,128)S(1)} %copy-done.3, s32[2,64]{1,0:T(2,128)S(1)} %copy-done.2, bf16[128,512]{1,0:T(8,128)(2,1)S(1)} %bitcast.16, bf16[2,65,512]{2,1,0:T(8,128)(2,1)S(1)} %copy.14.pred_ref), custom_call_target="tpu_custom_call" | custom-call | flops 335544320 | bytes 3145728 | tf_op jit(solution)/shard_map/pallas_call | solution.py:432
  44.2 6.6 %all-to-all-done.1 = bf16[8,64,512]{2,1,0:T(8,128)(2,1)S(1)} async-done(((bf16[8,64,512]{2,1,0:T(8,128)(2,1)}), bf16[8,64,512]{2,1,0:T(8,128)(2,1)S(1)}, u32[]{:S(2)}, u32[]{:S(2)}) %all-to-all-start.1) | async-done | bytes 524320 | tf_op jit(solution)/shard_map/all_to_all | solution.py:404
  50.8 8.4 %shard_map.103 = (f32[512,2048]{1,0:T(8,128)S(1)}, bf16[512,512]{1,0:T(8,128)(2,1)S(1)}, f32[3,16,128]{2,1,0:T(8,128)S(1)}, f32[6,16,16,128]{3,2,1,0:T(8,128)S(1)}, f32[8,128]{1,0:T(8,128)S(1)}) custom-call(s32[2,64]{1,0:T(2,128)S(1)} %copy-done.3, s32[2]{0:T(128)S(1)} %copy-done.4, s32[2]{0:T(128)S(1)} %copy-done.5, s32[1]{0:T(128)} %bitcast.block_ref, ...), custom_call_target="tpu_custom_call" | custom-call | flops 1073741824 | bytes 8388608 | tf_op jit(solution)/shard_map/pallas_call | solution.py:455
  59.2 8.0 %all_to_all.36.blocks_ref = f32[8,8,128]{2,1,0:T(8,128)S(1)} all-to-all(f32[8,8,128]{2,1,0:T(8,128)S(1)} %broadcast_in_dim.36), channel_id=1, replica_groups=mesh['tm'=8,'utt'=64] {'tm'}, dimensions={0} | all-to-all | bytes 65536 | tf_op jit(solution)/shard_map/all_to_all | solution.py:404
  67.1 9.2 %shard_map.104 = (f32[2]{0:T(128)}, bf16[128,512]{1,0:T(8,128)(2,1)}, bf16[8,96,512]{2,1,0:T(8,128)(2,1)S(1)}) custom-call(s32[2,64]{1,0:T(2,128)S(1)} %copy-done.3, s32[2]{0:T(128)S(1)} %copy-done.4, s32[2]{0:T(128)S(1)} %copy-done.5, s32[1]{0:T(128)} %bitcast.block_ref, f32[8,8,128]{2,1,0:T(8,128)S(1)} %all_to_all.36.blocks_ref, ...), custom_call_target="tpu_custom_call" | custom-call | flops 3221225472 | bytes 8388608 | tf_op jit(solution)/shard_map/pallas_call | solution.py:493
  76.3 15.4 %all_to_all.37 = bf16[8,96,512]{2,1,0:T(8,128)(2,1)S(1)} all-to-all(bf16[8,96,512]{2,1,0:T(8,128)(2,1)S(1)} %get-tuple-element.25), channel_id=1, replica_groups=mesh['tm'=8,'utt'=64] {'tm'}, dimensions={0} | all-to-all | bytes 1572864 | tf_op jit(solution)/shard_map/all_to_all | solution.py:404
  91.7 0.1 convert_reduce_fusion
  91.8 0.8 broadcast_in_dim.37
  92.6 4.4 %all-to-all-start.4 = ((f32[8,17,512]{2,1,0:T(8,128)}), f32[8,17,512]{2,1,0:T(8,128)S(1)}, u32[]{:S(2)}, u32[]{:S(2)}) async-start(f32[8,17,512]{2,1,0:T(8,128)} %broadcast_in_dim.37), calls=%async_computation.4 | async-start | bytes 786432 | tf_op jit(solution)/shard_map/all_to_all | solution.py:404
  97.1 8.0 %all-to-all-done.4 = f32[8,17,512]{2,1,0:T(8,128)S(1)} async-done(((f32[8,17,512]{2,1,0:T(8,128)}), f32[8,17,512]{2,1,0:T(8,128)S(1)}, u32[]{:S(2)}, u32[]{:S(2)}) %all-to-all-start.4) | async-done | bytes 278560 | tf_op jit(solution)/shard_map/all_to_all | solution.py:404
  105.1 18.1 %all_to_all.38 = f32[64,4,128]{2,1,0:T(4,128)S(1)} all-to-all(f32[64,4,128]{2,1,0:T(4,128)S(1)} %reshape.41), channel_id=1, replica_groups=mesh['tm'=8,'utt'=64] {'utt'}, dimensions={0} | all-to-all | bytes 262144 | tf_op jit(solution)/shard_map/all_to_all | solution.py:404
  123.2 0.1 reduce_sum.19
  123.2 0.6 broadcast_in_dim.38
  123.9 6.5 %all-to-all-start.6 = ((f32[8,4,128]{2,1,0:T(4,128)}), f32[8,4,128]{2,1,0:T(4,128)S(1)}, u32[]{:S(2)}, u32[]{:S(2)}) async-start(f32[8,4,128]{2,1,0:T(4,128)} %broadcast_in_dim.38), calls=%async_computation.6 | async-start | bytes 32768 | tf_op jit(solution)/shard_map/all_to_all | solution.py:404
  130.4 0.1 reshape.42
  130.5 0.9 copy.15
  131.4 3.7 %all-to-all-done.6 = f32[8,4,128]{2,1,0:T(4,128)S(1)} async-done(((f32[8,4,128]{2,1,0:T(4,128)}), f32[8,4,128]{2,1,0:T(4,128)S(1)}, u32[]{:S(2)}, u32[]{:S(2)}) %all-to-all-start.6) | async-done | bytes 16416 | tf_op jit(solution)/shard_map/all_to_all | solution.py:404
  135.1 0.6 copy.21
  (19 shorter events, 0.2 us)
Async XLA Ops:
  0.6 0.7 copy-start
  0.6 41.6 %copy-start.3 = (s32[2,64]{1,0:T(2,128)S(1)}, s32[2,64]{1,0:T(2,128)}, u32[]{:S(2)}) copy-start(s32[2,64]{1,0:T(2,128)} %starts_ref.5) | copy-start | bytes 1540
  0.7 41.6 %copy-start.2 = (s32[2,64]{1,0:T(2,128)S(1)}, s32[2,64]{1,0:T(2,128)}, u32[]{:S(2)}) copy-start(s32[2,64]{1,0:T(2,128)} %labels_ref.1) | copy-start | bytes 1540
  0.7 41.6 %copy-start.1 = (bf16[2,64,512]{2,1,0:T(8,128)(2,1)S(1)}, bf16[2,64,512]{2,1,0:T(8,128)(2,1)}, u32[]{:S(2)}) copy-start(bf16[2,64,512]{2,1,0:T(8,128)(2,1)} %param.7) | copy-start | bytes 393220
  1.4 49.4 %copy-start.4 = (s32[2]{0:T(128)S(1)}, s32[2]{0:T(128)}, u32[]{:S(2)}) copy-start(s32[2]{0:T(128)} %frames_ref.3) | copy-start | bytes 28
  1.4 49.4 %copy-start.5 = (s32[2]{0:T(128)S(1)}, s32[2]{0:T(128)}, u32[]{:S(2)}) copy-start(s32[2]{0:T(128)} %labels_len_ref.3) | copy-start | bytes 28
  34.7 16.1 %all-to-all-start.1 = ((bf16[8,64,512]{2,1,0:T(8,128)(2,1)}), bf16[8,64,512]{2,1,0:T(8,128)(2,1)S(1)}, u32[]{:S(2)}, u32[]{:S(2)}) async-start(bf16[8,64,512]{2,1,0:T(8,128)(2,1)} %broadcast_in_dim.17), calls=%async_computation.1 | async-start | bytes 1048576 | tf_op jit(solution)/shard_map/all_to_all | solution.py:404
  92.6 12.5 %all-to-all-start.4 = ((f32[8,17,512]{2,1,0:T(8,128)}), f32[8,17,512]{2,1,0:T(8,128)S(1)}, u32[]{:S(2)}, u32[]{:S(2)}) async-start(f32[8,17,512]{2,1,0:T(8,128)} %broadcast_in_dim.37), calls=%async_computation.4 | async-start | bytes 786432 | tf_op jit(solution)/shard_map/all_to_all | solution.py:404
  123.9 11.2 %all-to-all-start.6 = ((f32[8,4,128]{2,1,0:T(4,128)}), f32[8,4,128]{2,1,0:T(4,128)S(1)}, u32[]{:S(2)}, u32[]{:S(2)}) async-start(f32[8,4,128]{2,1,0:T(4,128)} %broadcast_in_dim.38), calls=%async_computation.6 | async-start | bytes 32768 | tf_op jit(solution)/shard_map/all_to_all | solution.py:404

commit v5 on v4

--- a/solution.py
+++ b/solution.py
@@ -108,19 +108,27 @@
     return rows
 
 
-def hidden_kernel(starts_ref, labels_ref, enc_ref, pred_ref, hidden_ref, label_ref, enc_t, pred_t, stack):
+def reorder(own_rows, width):
+    source = slot_row(row_ids((width, width)), own_rows, width)
+    return (lane_ids((width, width)) == source).astype(BF16)
+
+
+def hidden_kernel(own_rows, starts_ref, labels_ref, enc_ref, pred_ref, hidden_ref, label_ref, enc_t, pred_t, stack):
     step = pl.program_id(0)
     half = starts_ref.shape[1]
     starts = rows_to_lanes(starts_ref[...])
 
     @pl.when(step == 0)
     def _():
-        enc_t[...] = jnp.transpose(enc_ref[...].astype(F32))
+        turn = reorder(own_rows, enc_ref.shape[1])
+        enc_t[...] = lax.dot_general(turn, enc_ref[...], NT_DIMS, preferred_element_type=F32)
         stack[...] = jnp.zeros_like(stack)
         rows = pred_ref.shape[1]
         stack[0:rows, :] = pred_ref[0].astype(F32)
         stack[PRED_PAD : PRED_PAD + rows, :] = pred_ref[1].astype(F32)
-        pred_t[...] = jnp.transpose(stack[...]).astype(BF16)
+        pred_t[...] = lax.dot_general(
+            turn, stack[...].astype(BF16), NT_DIMS, preferred_element_type=F32
+        ).astype(BF16)
         cap = labels_ref.shape[1]
         labels = labels_ref[...].astype(F32)
         table = [jnp.transpose(jnp.broadcast_to(labels[b : b + 1, :], (LANES, cap))) for b in range(2)]
@@ -142,7 +150,6 @@
 
 
 def forward_kernel(
-    own_rows,
     vocab,
     starts_ref,
     frames_ref,
@@ -152,23 +159,18 @@
     gathered_ref,
     hidden_ref,
     exps_ref,
-    weights_ref,
     lps_ref,
     tree_ref,
     payload_ref,
     weights_t,
+    former,
     root,
 ):
     step = pl.program_id(0)
-    width = gathered_ref.shape[0]
 
     @pl.when(step == 0)
     def _():
-        source = slot_row(lane_ids((width, width)), own_rows, width)
-        turn = (row_ids((width, width)) == source).astype(BF16)
-        weights = jnp.dot(turn, gathered_ref[...], preferred_element_type=F32)
-        weights_ref[...] = weights.astype(BF16)
-        weights_t[...] = jnp.transpose(weights).astype(BF16)
+        weights_t[...] = jnp.transpose(gathered_ref[...])
 
     logits = jnp.dot(weights_t[...], hidden_ref[...], preferred_element_type=F32)
     padded = logits.shape[0]
@@ -216,23 +218,27 @@
         levels = half.bit_length() - 1
         for level in range(levels):
             reach = 1 << level
+            back = LANES - reach
             late = lanes % (2 * reach) == reach
-            back = LANES - reach
-            latter = [tree_ref[level, m] for m in range(S)]
-            latter = [jnp.where(late, one, pltpu.roll(one, back, 1)) for one in latter]
-
-            def product(i, carry, level=level, reach=reach, late=late, back=back, latter=latter):
-                former = jnp.where(late, pltpu.roll(tree_ref[level, i + S // 2], reach, 1), tree_ref[level, i])
-                row = rowwise_logsumexp([former[m : m + 1, :] + latter[m] for m in range(S)])
-                if level + 1 < levels:
-                    tree_ref[level + 1, i] = row
-                    tree_ref[level + 1, i + S // 2] = pltpu.roll(row, back, 1)
-                else:
-                    root[i] = row
-                    root[i + S // 2] = pltpu.roll(row, back, 1)
-                return carry
-
-            lax.fori_loop(0, S // 2, product, 0, unroll=4)
+            for i in range(S // 2):
+                behind = pltpu.roll(tree_ref[level, i + S // 2], reach, 1)
+                former[i] = jnp.where(late, behind, tree_ref[level, i])
+            for cut in (slice(0, 8), slice(8, 16)):
+                latter = [tree_ref[level, m, cut, :] for m in range(S)]
+                latter = [jnp.where(late, one, pltpu.roll(one, back, 1)) for one in latter]
+
+                def product(i, carry, level=level, back=back, latter=latter, cut=cut):
+                    row = rowwise_logsumexp([former[i, m : m + 1, :] + latter[m] for m in range(S)])
+                    moved = pltpu.roll(row, back, 1)
+                    if level + 1 < levels:
+                        tree_ref[level + 1, i, cut, :] = row
+                        tree_ref[level + 1, i + S // 2, cut, :] = moved
+                    else:
+                        root[i, cut, :] = row
+                        root[i + S // 2, cut, :] = moved
+                    return carry
+
+                lax.fori_loop(0, S // 2, product, 0, unroll=2)
         flat = jnp.transpose(root[...].reshape(S * S, LANES))
         payload_ref[...] = jnp.zeros_like(payload_ref)
         for b in range(2):
@@ -357,7 +363,9 @@
     spread = (grad_blank + grad_emit) * wide(lps_ref, 2)
     padded = exps_ref.shape[0]
     ids = row_ids((padded, WIDE))
-    coeff = jnp.where(ids == names, grad_emit, jnp.where(ids == 0, grad_blank, 0.0))
+    coeff = jnp.where(ids == names, grad_emit, 0.0)
+    head = coeff[:8] + jnp.where(row_ids((8, WIDE)) == 0, grad_blank, 0.0)
+    coeff = jnp.concatenate([head, coeff[8:]], axis=0)
     grad_logits = (coeff - exps_ref[...] * spread).astype(BF16)
     grad_hidden = jnp.dot(weights_ref[...], grad_logits, preferred_element_type=F32)
     hidden = hidden_ref[...]
@@ -379,14 +387,14 @@
 
     @pl.when(step == STEPS - 1)
     def _():
-        grad_enc_ref[...] = jnp.transpose(enc_sum[...]).astype(BF16)
+        turn = reorder(own_rows, width)
+        enc_rows = jnp.transpose(enc_sum[...]).astype(BF16)
+        grad_enc_ref[...] = jnp.dot(enc_rows, turn, preferred_element_type=F32).astype(BF16)
+        pred_rows = jnp.dot(pred_sum[...].astype(BF16), turn, preferred_element_type=F32).astype(BF16)
         share = width // 8
-        source = slot_row(row_ids((width, width)), own_rows, width)
-        turn = (lane_ids((width, width)) == source).astype(BF16)
-        turned = jnp.dot(turn, weight_sum[...].astype(BF16), preferred_element_type=F32).astype(BF16)
         for p in range(8):
-            send_ref[p, 0:share, :] = turned[p * share : (p + 1) * share, :]
-            send_ref[p, share : share + PRED_SLOT, :] = pred_sum[p * PRED_SLOT : (p + 1) * PRED_SLOT, :].astype(BF16)
+            send_ref[p, 0:share, :] = weight_sum[p * share : (p + 1) * share, :].astype(BF16)
+            send_ref[p, share : share + PRED_SLOT, :] = pred_rows[p * PRED_SLOT : (p + 1) * PRED_SLOT, :]
 
 
 def params():
@@ -426,11 +434,10 @@
     mine = lax.dynamic_slice_in_dim(w_out, tm_index * piece, piece, axis=0)
     mine = jnp.pad(mine, ((0, 0), (0, padded - vocab))).reshape(fold, LANES)
     held = share_copies(mine, UTT).reshape(share, padded)
-    gathered = share_copies(held, TM).reshape(width, padded)
     block = tm_index.reshape(1).astype(jnp.int32)
 
     hidden, label_ids = pl.pallas_call(
-        hidden_kernel,
+        functools.partial(hidden_kernel, own_rows),
         grid=(STEPS,),
         in_specs=[
             whole(starts.shape),
@@ -451,9 +458,11 @@
         ),
     )(starts, labels, encoder.reshape(-1, width), predictor)
 
+    held, hidden = lax.optimization_barrier((held, hidden))
+    gathered = share_copies(held, TM).reshape(width, padded)
     levels = frame_count.bit_length() - 1
-    exps, weights, lps, tree, payload = pl.pallas_call(
-        functools.partial(forward_kernel, own_rows, vocab),
+    exps, lps, tree, payload = pl.pallas_call(
+        functools.partial(forward_kernel, vocab),
         grid=(STEPS,),
         in_specs=[
             whole(starts.shape),
@@ -466,20 +475,19 @@
         ],
         out_specs=[
             pl.BlockSpec((padded, WIDE), lambda i: (0, i)),
-            whole((width, padded)),
             whole((3, S, LANES)),
             whole((levels, S, S, LANES)),
             whole((8, LANES)),
         ],
         out_shape=[
             shape((padded, rows), F32),
-            shape((width, padded), BF16),
             shape((3, S, LANES), F32),
             shape((levels, S, S, LANES), F32),
             shape((8, LANES), F32),
         ],
         scratch_shapes=[
             pltpu.VMEM((padded, width), BF16),
+            pltpu.VMEM((S // 2, S, LANES), F32),
             pltpu.VMEM((S, S, LANES), F32),
         ],
         compiler_params=params(),
@@ -529,16 +537,17 @@
         cost_estimate=pl.CostEstimate(
             flops=6 * padded * width * rows, bytes_accessed=8 * 2**20, transcendentals=2**16
         ),
-    )(starts, frame_lengths, label_lengths, block, blocks, lps, tree, label_ids, weights, hidden, exps)
+    )(starts, frame_lengths, label_lengths, block, blocks, lps, tree, label_ids, gathered, hidden, exps)
 
     block_sum = jnp.sum(exchange(send, TM).astype(F32), axis=0)
-    pred_rows = share_copies(block_sum[share : share + PRED_SHARE], TM)
+    pred_rows = block_sum[share : share + PRED_SHARE]
     weight_rows = exchange(block_sum[:share].reshape(utt_size, fold, LANES), UTT)
-    pred_rows, weight_rows = lax.optimization_barrier((pred_rows, weight_rows))
-    grad_w_out = share_copies(jnp.sum(weight_rows, axis=0), TM).reshape(own_rows, padded)
-    grad_predictor = pred_rows.reshape(-1, width)[: utt_count * label_rows]
+    own_weight = jnp.sum(weight_rows, axis=0).reshape(piece, padded)
+    final = share_copies(jnp.concatenate([pred_rows, own_weight], axis=0).astype(BF16), TM).astype(F32)
+    grad_predictor = final[:, :PRED_SHARE].reshape(-1, width)[: utt_count * label_rows]
     grad_predictor = grad_predictor.reshape(utt_count, label_rows, width)
-    return (losses, grad_encoder.reshape(encoder.shape), grad_predictor, grad_w_out[:, :vocab])
+    grad_w_out = final[:, PRED_SHARE:, :vocab].reshape(own_rows, vocab)
+    return (losses, grad_encoder.reshape(encoder.shape), grad_predictor, grad_w_out)
 
 
 def solution(mesh):

time: 136 us -> 128 us (0.941)
  blocking collectives: 73.8 us -> 50.9 us
  starting transfers between devices: 17.5 us -> 24.7 us
  waiting for transfers between devices: 18.3 us -> 22.2 us
  Pallas kernels: 19.5 us -> 22.1 us
  local copies, waits for them, and re-layouts: 5.58 us -> 7 us
    all_to_all x4, blocking collectives: 73.8 us -> 50.9 us  [exchange(): return lax.all_to_all(blocks, axes, 0, 0, tiled=True)]
    all_to_all x3 -> x2, starting transfers between devices: 17.5 us -> 24.7 us  [exchange(): return lax.all_to_all(blocks, axes, 0, 0, tiled=True)]
    all_to_all x3 -> x2, waiting for transfers between devices: 18.3 us -> 22.2 us  [exchange(): return lax.all_to_all(blocks, axes, 0, 0, tiled=True)]
    pallas_call x2, Pallas kernels: 10.3 us -> 12.8 us  [the longest x1 10.7 us: per_device(): pl.pallas_call(functools.partial(forward_kernel, vocab), grid=(STEPS,), i...]
    unnamed x16 -> x19, local copies, waits for them, and re-layouts: 3.14 us -> 5.42 us
    broadcast_in_dim x5 -> x4, local copies, waits for them, and re-layouts: 2.27 us -> 0.71 us  [share_copies(): return exchange(jnp.broadcast_to(block[None], (count, *block.shape)), axes)]
  transfers between devices with their start and end apart: 3 -> 2, of which waited for: 3 -> 2; matrix products, arithmetic and copies ran while one was open for 1% -> 1% of each run, Pallas kernels for 1% -> 2%
where the time goes in v5:
time: 128 us
  blocking collectives  50.9 us (40%)
  starting transfers between devices  24.7 us (19%)
  waiting for transfers between devices  22.2 us (17%)
  Pallas kernels  22.1 us (17%)
  local copies, waits for them, and re-layouts  7 us (5%)
    all_to_all x4, blocking collectives, exchange(): return lax.all_to_all(blocks, axes, 0, 0, tiled=True)  50.9 us
    all_to_all x2, starting transfers between devices, exchange(): return lax.all_to_all(blocks, axes, 0, 0, tiled=True)  24.7 us
    all_to_all x2, waiting for transfers between devices, exchange(): return lax.all_to_all(blocks, axes, 0, 0, tiled=True)  22.2 us
    pallas_call x1, Pallas kernels, per_device(): pl.pallas_call(functools.partial(forward_kernel, vocab), grid=(STEPS,), i...  10.7 us
    pallas_call x1, Pallas kernels, per_device(): pl.pallas_call(functools.partial(backward_kernel, own_rows, label_rows),...  9.27 us
    unnamed x19, local copies, waits for them, and re-layouts  5.42 us
  transfers between devices with their start and end apart: 2, of which 2 were waited for; matrix products, arithmetic and copies ran while one was open for 1% of the time, Pallas kernels for 2%

profile of v5, /device:TPU:1, one launch (start us, length us, event | category | flops | bytes accessed | tf_op | source)
XLA Modules:
  0.0 127.9 jit_solution(7486820722904659955)
XLA Ops:
  0.6 0.0 copy-start
  0.7 0.7 copy-done
  1.4 0.6 broadcast_in_dim.11
  2.0 19.2 %all-to-all-start = ((bf16[64,4,128]{2,1,0:T(4,128)(2,1)}), bf16[64,4,128]{2,1,0:T(4,128)(2,1)S(1)}, u32[]{:S(2)}, u32[]{:S(2)}) async-start(bf16[64,4,128]{2,1,0:T(4,128)(2,1)} %broadcast_in_dim.11), calls=%async_computation | async-start | bytes 131072 | tf_op jit(solution)/shard_map/all_to_all | solution.py:412
  21.3 0.9 copy.15.pred_ref
  22.2 0.9 copy-done.1
  23.1 0.7 copy-done.2
  23.8 0.7 copy-done.3
  24.5 2.1 %shard_map.102 = (bf16[512,2048]{1,0:T(8,128)(2,1)S(1)}, s32[16,128]{1,0:T(8,128)S(1)}) custom-call(s32[2,64]{1,0:T(2,128)S(1)} %copy-done.3, s32[2,64]{1,0:T(2,128)S(1)} %copy-done.2, bf16[128,512]{1,0:T(8,128)(2,1)S(1)} %bitcast.22, bf16[2,65,512]{2,1,0:T(8,128)(2,1)S(1)} %copy.15.pred_ref), custom_call_target="tpu_custom_call" | custom-call | flops 335544320 | bytes 3145728 | tf_op jit(solution)/shard_map/pallas_call | solution.py:439
  26.6 8.2 %all-to-all-done = bf16[64,4,128]{2,1,0:T(4,128)(2,1)S(1)} async-done(((bf16[64,4,128]{2,1,0:T(4,128)(2,1)}), bf16[64,4,128]{2,1,0:T(4,128)(2,1)S(1)}, u32[]{:S(2)}, u32[]{:S(2)}) %all-to-all-start) | async-done | bytes 65568 | tf_op jit(solution)/shard_map/all_to_all | solution.py:412
  34.9 15.7 %all_to_all.30 = bf16[8,64,512]{2,1,0:T(8,128)(2,1)S(1)} all-to-all(bf16[8,64,512]{2,1,0:T(8,128)(2,1)S(1)} %broadcast_in_dim.12), channel_id=1, replica_groups=mesh['tm'=8,'utt'=64] {'tm'}, dimensions={0} | all-to-all | bytes 1048576 | tf_op jit(solution)/shard_map/all_to_all | solution.py:412
  50.6 10.7 %shard_map.103 = (f32[512,2048]{1,0:T(8,128)S(1)}, f32[3,16,128]{2,1,0:T(8,128)S(1)}, f32[6,16,16,128]{3,2,1,0:T(8,128)S(1)}, f32[8,128]{1,0:T(8,128)S(1)}) custom-call(s32[2,64]{1,0:T(2,128)S(1)} %copy-done.4, s32[2]{0:T(128)S(1)} %copy-done.5, s32[2]{0:T(128)S(1)} %copy-done.6, s32[1]{0:T(128)} %bitcast.block_ref, ...), custom_call_target="tpu_custom_call" | custom-call | flops 1073741824 | bytes 8388608 | tf_op jit(solution)/shard_map/pallas_call | solution.py:464
  61.3 8.1 %all_to_all.31.blocks_ref = f32[8,8,128]{2,1,0:T(8,128)S(1)} all-to-all(f32[8,8,128]{2,1,0:T(8,128)S(1)} %broadcast_in_dim.13), channel_id=1, replica_groups=mesh['tm'=8,'utt'=64] {'tm'}, dimensions={0} | all-to-all | bytes 65536 | tf_op jit(solution)/shard_map/all_to_all | solution.py:412
  69.5 9.3 %shard_map.104 = (f32[2]{0:T(128)}, bf16[128,512]{1,0:T(8,128)(2,1)}, bf16[8,96,512]{2,1,0:T(8,128)(2,1)S(1)}) custom-call(s32[2,64]{1,0:T(2,128)S(1)} %copy-done.4, s32[2]{0:T(128)S(1)} %copy-done.5, s32[2]{0:T(128)S(1)} %copy-done.6, s32[1]{0:T(128)} %bitcast.block_ref, f32[8,8,128]{2,1,0:T(8,128)S(1)} %all_to_all.31.blocks_ref, ...), custom_call_target="tpu_custom_call" | custom-call | flops 3221225472 | bytes 8388608 | tf_op jit(solution)/shard_map/pallas_call | solution.py:501
  78.7 15.4 %all_to_all.32 = bf16[8,96,512]{2,1,0:T(8,128)(2,1)S(1)} all-to-all(bf16[8,96,512]{2,1,0:T(8,128)(2,1)S(1)} %get-tuple-element.25), channel_id=1, replica_groups=mesh['tm'=8,'utt'=64] {'tm'}, dimensions={0} | all-to-all | bytes 1572864 | tf_op jit(solution)/shard_map/all_to_all | solution.py:412
  94.1 0.1 convert_reduce_fusion
  94.2 0.7 reshape.61
  94.9 5.5 %all-to-all-start.4 = ((f32[64,4,128]{2,1,0:T(4,128)}), f32[64,4,128]{2,1,0:T(4,128)S(1)}, u32[]{:S(2)}, u32[]{:S(2)}) async-start(f32[64,4,128]{2,1,0:T(4,128)} %reshape.61), calls=%async_computation.4 | async-start | bytes 262144 | tf_op jit(solution)/shard_map/all_to_all | solution.py:412
  100.4 13.9 %all-to-all-done.4 = f32[64,4,128]{2,1,0:T(4,128)S(1)} async-done(((f32[64,4,128]{2,1,0:T(4,128)}), f32[64,4,128]{2,1,0:T(4,128)S(1)}, u32[]{:S(2)}, u32[]{:S(2)}) %all-to-all-start.4) | async-done | bytes 131104 | tf_op jit(solution)/shard_map/all_to_all | solution.py:412
  114.4 0.1 reduce_sum.19
  114.5 11.7 %all_to_all.33 = bf16[8,18,512]{2,1,0:T(8,128)(2,1)S(1)} all-to-all(bf16[8,18,512]{2,1,0:T(8,128)(2,1)S(1)} %broadcast_in_dim.14), channel_id=1, replica_groups=mesh['tm'=8,'utt'=64] {'tm'}, dimensions={0} | all-to-all | bytes 294912 | tf_op jit(solution)/shard_map/all_to_all | solution.py:412
  126.2 0.6 copy.24
  126.8 0.1 reshape.62
  126.9 0.9 copy.16
  (22 shorter events, 0.2 us)
Async XLA Ops:
  0.6 0.7 copy-start
  2.0 48.6 %copy-start.4 = (s32[2,64]{1,0:T(2,128)S(1)}, s32[2,64]{1,0:T(2,128)}, u32[]{:S(2)}) copy-start(s32[2,64]{1,0:T(2,128)} %starts_ref.5) | copy-start | bytes 1540
  2.0 48.6 %copy-start.5 = (s32[2]{0:T(128)S(1)}, s32[2]{0:T(128)}, u32[]{:S(2)}) copy-start(s32[2]{0:T(128)} %frames_ref.3) | copy-start | bytes 28
  2.0 48.6 %copy-start.6 = (s32[2]{0:T(128)S(1)}, s32[2]{0:T(128)}, u32[]{:S(2)}) copy-start(s32[2]{0:T(128)} %labels_len_ref.3) | copy-start | bytes 28
  2.0 32.8 %all-to-all-start = ((bf16[64,4,128]{2,1,0:T(4,128)(2,1)}), bf16[64,4,128]{2,1,0:T(4,128)(2,1)S(1)}, u32[]{:S(2)}, u32[]{:S(2)}) async-start(bf16[64,4,128]{2,1,0:T(4,128)(2,1)} %broadcast_in_dim.11), calls=%async_computation | async-start | bytes 131072 | tf_op jit(solution)/shard_map/all_to_all | solution.py:412
  22.2 0.9 copy-start.1
  23.1 0.7 copy-start.2
  23.8 0.7 copy-start.3
  94.9 19.4 %all-to-all-start.4 = ((f32[64,4,128]{2,1,0:T(4,128)}), f32[64,4,128]{2,1,0:T(4,128)S(1)}, u32[]{:S(2)}, u32[]{:S(2)}) async-start(f32[64,4,128]{2,1,0:T(4,128)} %reshape.61), calls=%async_computation.4 | async-start | bytes 262144 | tf_op jit(solution)/shard_map/all_to_all | solution.py:412

commit v6 on v5

v6 whole, which is shorter than its diff:
```python
import functools

import jax
import jax.numpy as jnp
from jax import lax
from jax.experimental import pallas as pl
from jax.experimental.pallas import tpu as pltpu
from jax.sharding import PartitionSpec as P

S = 16
LANES = 128
GROUP = 4
STEPS = S // GROUP
WIDE = GROUP * LANES
PRED_PAD = 80
VMEM_BYTES = 40 * 2**20

masked_log = -1e30

F32 = jnp.float32
BF16 = jnp.bfloat16

PRED_SHARE = 17
PRED_SLOT = 32
TM = "tm"
UTT = "utt"

NT_DIMS = (((1,), (1,)), ((), ()))


def lane_ids(shape=(1, LANES)):
    return lax.broadcasted_iota(jnp.int32, shape, 1)


def row_ids(shape):
    return lax.broadcasted_iota(jnp.int32, shape, 0)


def per_lane(half, low, high):
    return jnp.where(lane_ids() < half, low, high)


def rows_to_lanes(pair):
    return jnp.concatenate([pair[0:1, :], pair[1:2, :]], axis=1)


def balanced(combine, terms):
    while len(terms) > 1:
        terms = [combine(a, b) for a, b in zip(terms[0::2], terms[1::2])]
    return terms[0]


def rowwise_logsumexp(terms):
    top = balanced(jnp.maximum, terms)
    total = balanced(jnp.add, [jnp.exp(t - top) for t in terms])
    return top + jnp.log(total)


def vector_times(vector, matrix):
    return rowwise_logsumexp([vector[i : i + 1, :] + matrix[i] for i in range(S)])


def times_vector(matrix, vector, rows_ref):
    for i in range(S):
        terms = matrix[i] + vector
        top = jnp.max(terms, axis=0, keepdims=True)
        total = jnp.sum(jnp.exp(terms - top), axis=0, keepdims=True)
        rows_ref[i : i + 1, :] = top + jnp.log(total)
    return rows_ref[...]


def window_down(vector, distance):
    places = row_ids((S, LANES))
    for bit in (1, 2, 4, 8):
        moved = jnp.where(places < S - bit, pltpu.roll(vector, S - bit, 0), masked_log)
        vector = jnp.where((distance & bit) != 0, moved, vector)
    return vector


def window_up(vector, distance):
    places = row_ids((S, LANES))
    for bit in (1, 2, 4, 8):
        moved = jnp.where(places >= bit, pltpu.roll(vector, bit, 0), masked_log)
        vector = jnp.where((distance & bit) != 0, moved, vector)
    return vector


def slot_row(slot, own_rows, width):
    if own_rows != 8:
        return slot
    share = width // 8
    return slot % share * own_rows + slot // share


def frame_shifts(starts, half):
    lanes = lane_ids()
    first = (lanes == 0) | (lanes == half)
    return jnp.where(first, 0, starts - pltpu.roll(starts, 1, 1))


def span_rows(blank, emit):
    places = row_ids((S, LANES))
    spans = jnp.zeros((S, LANES), F32)
    rows = [None] * S
    for e in reversed(range(S)):
        spans = jnp.where(places > e, spans + emit[e : e + 1, :], 0.0)
        rows[e] = jnp.where(places >= e, spans + blank, masked_log)
    return rows


def reorder(own_rows, width):
    source = slot_row(row_ids((width, width)), own_rows, width)
    return (lane_ids((width, width)) == source).astype(BF16)


def hidden_kernel(own_rows, starts_ref, labels_ref, enc_ref, pred_ref, hidden_ref, label_ref, enc_t, pred_t, stack):
    step = pl.program_id(0)
    half = starts_ref.shape[1]
    starts = rows_to_lanes(starts_ref[...])

    @pl.when(step == 0)
    def _():
        turn = reorder(own_rows, enc_ref.shape[1])
        enc_t[...] = lax.dot_general(turn, enc_ref[...], NT_DIMS, preferred_element_type=F32)
        stack[...] = jnp.zeros_like(stack)
        rows = pred_ref.shape[1]
        stack[0:rows, :] = pred_ref[0].astype(F32)
        stack[PRED_PAD : PRED_PAD + rows, :] = pred_ref[1].astype(F32)
        pred_t[...] = lax.dot_general(
            turn, stack[...].astype(BF16), NT_DIMS, preferred_element_type=F32
        ).astype(BF16)
        cap = labels_ref.shape[1]
        labels = labels_ref[...].astype(F32)
        table = [jnp.transpose(jnp.broadcast_to(labels[b : b + 1, :], (LANES, cap))) for b in range(2)]
        table = jnp.where(lane_ids((cap, LANES)) < half, table[0], table[1])
        places = row_ids((cap, LANES))
        for k in range(S):
            wanted = jnp.minimum(starts + k, cap - 1)
            label_ref[k : k + 1, :] = jnp.sum(
                jnp.where(places == wanted, table, 0.0), axis=0, keepdims=True
            ).astype(jnp.int32)

    base = starts + per_lane(half, 0, PRED_PAD) + step * GROUP
    wanted = jnp.concatenate([base + k for k in range(GROUP)], axis=1)
    match = (row_ids((2 * PRED_PAD, WIDE)) == wanted).astype(BF16)
    picked = jnp.dot(pred_t[...], match, preferred_element_type=F32)
    for k in range(GROUP):
        part = slice(k * LANES, (k + 1) * LANES)
        hidden_ref[:, part] = jnp.tanh(enc_t[...] + picked[:, part]).astype(BF16)


def forward_kernel(
    vocab,
    starts_ref,
    frames_ref,
    labels_len_ref,
    block_ref,
    label_ref,
    gathered_ref,
    hidden_ref,
    exps_ref,
    lps_ref,
    tree_ref,
    payload_ref,
    weights_t,
    root,
):
    weights_t[...] = jnp.transpose(gathered_ref[...])
    for step in range(STEPS):
        joiner_step(step, vocab, weights_t, label_ref, hidden_ref, exps_ref, lps_ref)
    lattice_products(starts_ref, frames_ref, labels_len_ref, block_ref, lps_ref, tree_ref, payload_ref, root)


def joiner_step(step, vocab, weights_t, label_ref, hidden_ref, exps_ref, lps_ref):
    here = slice(step * WIDE, (step + 1) * WIDE)
    logits = jnp.dot(weights_t[...], hidden_ref[:, here], preferred_element_type=F32)
    padded = logits.shape[0]
    edge = padded - 16
    tail = jnp.where(row_ids((16, WIDE)) < vocab - edge, logits[edge:], masked_log)
    logits = jnp.concatenate([logits[:edge], tail], axis=0)
    top = jnp.max(logits, axis=0, keepdims=True)
    exps = jnp.exp(logits - top)
    exps_ref[:, here] = exps
    total = jnp.sum(exps, axis=0, keepdims=True)
    norm = top + jnp.log(total)
    scale = 1.0 / total
    names = jnp.concatenate([label_ref[step * GROUP + k : step * GROUP + k + 1, :] for k in range(GROUP)], axis=1)
    emit = jnp.sum(jnp.where(row_ids((padded, WIDE)) == names, logits, 0.0), axis=0, keepdims=True) - norm
    blank = logits[0:1, :] - norm
    for k in range(GROUP):
        part = slice(k * LANES, (k + 1) * LANES)
        row = slice(step * GROUP + k, step * GROUP + k + 1)
        lps_ref[0, row, :] = blank[:, part]
        lps_ref[1, row, :] = emit[:, part]
        lps_ref[2, row, :] = scale[:, part]


def lattice_products(starts_ref, frames_ref, labels_len_ref, block_ref, lps_ref, tree_ref, payload_ref, root):
    half = starts_ref.shape[1]
    lanes = lane_ids()
    starts = rows_to_lanes(starts_ref[...])
    frame = block_ref[0] * half + lanes % half
    live = frame < per_lane(half, frames_ref[0], frames_ref[1])
    limit = per_lane(half, labels_len_ref[0], labels_len_ref[1])
    allowed = live & (row_ids((S, LANES)) + starts < limit)
    blank = jnp.where(live, lps_ref[0], 0.0)
    emit = jnp.where(allowed, lps_ref[1], masked_log)
    lps_ref[0] = blank
    lps_ref[1] = emit
    shift = frame_shifts(starts, half)
    rows = span_rows(blank, emit)
    for bit in (1, 2, 4, 8):
        moved = (shift & bit) != 0
        rows = [
            jnp.where(moved, rows[i - bit] if i >= bit else masked_log, rows[i]) for i in range(S)
        ]
    for i in range(S):
        tree_ref[0, i] = rows[i]
    levels = half.bit_length() - 1
    for level in range(levels):
        reach = 1 << level
        back = LANES - reach
        late = lanes % (2 * reach) == reach
        latter = [tree_ref[level, m] for m in range(S)]
        latter = [jnp.where(late, one, pltpu.roll(one, back, 1)) for one in latter]
        for i in range(S // 2):
            former = jnp.where(late, pltpu.roll(tree_ref[level, i + S // 2], reach, 1), tree_ref[level, i])
            row = rowwise_logsumexp([former[m : m + 1, :] + latter[m] for m in range(S)])
            moved = pltpu.roll(row, back, 1)
            if level + 1 < levels:
                tree_ref[level + 1, i] = row
                tree_ref[level + 1, i + S // 2] = moved
            else:
                root[i] = row
                root[i + S // 2] = moved
    flat = jnp.transpose(root[...].reshape(S * S, LANES))
    payload_ref[...] = jnp.zeros_like(payload_ref)
    for b in range(2):
        line = flat[b * half : b * half + 1, :]
        payload_ref[4 * b : 4 * b + 1, :] = line[:, :LANES]
        payload_ref[4 * b + 1 : 4 * b + 2, :] = line[:, LANES:]
        for end, at in ((2, half - 1), (3, 0)):
            edge_start = starts_ref[b : b + 1, at : at + 1].astype(F32)
            payload_ref[4 * b + end : 4 * b + end + 1, :] = jnp.broadcast_to(edge_start, (1, LANES))


def backward_kernel(
    own_rows,
    label_rows,
    starts_ref,
    frames_ref,
    labels_len_ref,
    block_ref,
    blocks_ref,
    lps_ref,
    tree_ref,
    label_ref,
    weights_ref,
    hidden_ref,
    exps_ref,
    losses_ref,
    grad_enc_ref,
    send_ref,
    chain,
    line_up,
    rows_ref,
    grads,
    enc_sum,
    pred_sum,
    weight_sum,
):
    half = starts_ref.shape[1]
    width = weights_ref.shape[0]
    count = blocks_ref.shape[0]
    lanes = lane_ids()

    places = row_ids((S, LANES))
    line_up[...] = jnp.zeros_like(line_up)
    ends = jnp.zeros((1, LANES), F32)
    begins = jnp.zeros((1, LANES), F32)
    for r in range(count):
        for b in range(2):
            at = 2 * r + b
            line_up[0, at : at + 1, :] = blocks_ref[r, 4 * b : 4 * b + 1, :]
            line_up[1, at : at + 1, :] = blocks_ref[r, 4 * b + 1 : 4 * b + 2, :]
            ends = jnp.where(lanes == at, blocks_ref[r, 4 * b + 2 : 4 * b + 3, :], ends)
            begins = jnp.where(lanes == at, blocks_ref[r, 4 * b + 3 : 4 * b + 4, :], begins)
    for h in range(2):
        chain[h * S // 2 : (h + 1) * S // 2] = jnp.transpose(line_up[h]).reshape(S // 2, S, LANES)
    odd = lanes % 2 == 1
    last_start = [blocks_ref[count - 1, 4 * b + 2 : 4 * b + 3, :].astype(jnp.int32) for b in range(2)]
    final_place = jnp.where(odd, labels_len_ref[1] - last_start[1], labels_len_ref[0] - last_start[0])
    gap = (begins - pltpu.roll(ends, 2, 1)).astype(jnp.int32)
    gap = jnp.where((lanes >= 2) & (lanes < 2 * count), gap, 0)
    forward = jnp.where(places == 0, 0.0, masked_log) + jnp.zeros((S, LANES), F32)
    closing = jnp.where(places == final_place, 0.0, masked_log)
    backward = closing
    owner = lanes // 2
    for turn in range(count - 1):
        ahead = window_down(pltpu.roll(vector_times(forward, chain), 2, 1), gap)
        forward = jnp.where(owner == turn + 1, ahead, forward)
        behind = pltpu.roll(window_up(times_vector(chain, backward, rows_ref), gap), LANES - 2, 1)
        backward = jnp.where(owner == count - 2 - turn, behind, backward)
    leaving = vector_times(forward, chain) + closing
    best = jnp.max(leaving, axis=0, keepdims=True)
    log_total = best + jnp.log(jnp.sum(jnp.exp(leaving - best), axis=0, keepdims=True))
    for b in range(2):
        own_total = jnp.sum(jnp.where(lanes == 2 * (count - 1) + b, log_total, 0.0))
        losses_ref[b] = -own_total / frames_ref[b].astype(F32)

    def own_boundary(vectors):
        columns = [
            jnp.sum(jnp.where(lanes == 2 * block_ref[0] + b, vectors, 0.0), axis=1, keepdims=True)
            for b in range(2)
        ]
        spread = jnp.where(lanes < half, columns[0], columns[1])
        return spread - jnp.max(spread, axis=0, keepdims=True)

    alpha = own_boundary(forward)
    beta = own_boundary(backward)
    levels = half.bit_length() - 1
    for level in reversed(range(levels)):
        reach = 1 << level
        later = lanes % (2 * reach) == reach
        ahead = pltpu.roll(vector_times(alpha, tree_ref.at[level]), reach, 1)
        alpha = jnp.where(later, ahead, alpha)
        beta_late = pltpu.roll(beta, reach, 1)
        behind = times_vector(tree_ref.at[level], beta_late, rows_ref)
        beta = jnp.where(later, beta_late, pltpu.roll(behind, LANES - reach, 1))
    starts = rows_to_lanes(starts_ref[...])
    alpha = window_down(alpha, frame_shifts(starts, half))
    spans = span_rows(lps_ref[0], lps_ref[1])
    scores = [spans[e] + alpha[e : e + 1, :] + beta for e in range(S)]
    best = jnp.max(functools.reduce(jnp.maximum, scores), axis=0, keepdims=True)
    weights = [jnp.exp(score - best) for score in scores]
    for e in range(1, S):
        weights[e] = weights[e] + weights[e - 1]
    total = jnp.sum(weights[S - 1], axis=0, keepdims=True)
    negative = -1.0 / total
    grads[0] = weights[S - 1] * negative
    for m in range(S):
        crossing = jnp.sum(jnp.where(places > m, weights[m], 0.0), axis=0, keepdims=True)
        grads[1, m : m + 1, :] = crossing * negative
    for step in range(STEPS):
        gradient_step(
            step, label_rows, starts_ref, lps_ref, label_ref, weights_ref, hidden_ref, exps_ref, grads,
            enc_sum, pred_sum, weight_sum,
        )
    turn = reorder(own_rows, width)
    enc_rows = jnp.transpose(enc_sum[...]).astype(BF16)
    grad_enc_ref[...] = jnp.dot(enc_rows, turn, preferred_element_type=F32).astype(BF16)
    pred_rows = jnp.dot(pred_sum[...].astype(BF16), turn, preferred_element_type=F32).astype(BF16)
    share = width // 8
    for p in range(8):
        send_ref[p, 0:share, :] = weight_sum[p * share : (p + 1) * share, :].astype(BF16)
        send_ref[p, share : share + PRED_SLOT, :] = pred_rows[p * PRED_SLOT : (p + 1) * PRED_SLOT, :]


def gradient_step(
    step, label_rows, starts_ref, lps_ref, label_ref, weights_ref, hidden_ref, exps_ref, grads,
    enc_sum, pred_sum, weight_sum,
):
    half = starts_ref.shape[1]
    here = slice(step * WIDE, (step + 1) * WIDE)

    def wide(ref, *lead):
        return jnp.concatenate(
            [ref[(*lead, slice(step * GROUP + k, step * GROUP + k + 1))] for k in range(GROUP)], axis=1
        )

    names = wide(label_ref)
    grad_blank = wide(grads, 0)
    grad_emit = wide(grads, 1)
    spread = (grad_blank + grad_emit) * wide(lps_ref, 2)
    padded = exps_ref.shape[0]
    ids = row_ids((padded, WIDE))
    coeff = jnp.where(ids == names, grad_emit, 0.0)
    head = coeff[:8] + jnp.where(row_ids((8, WIDE)) == 0, grad_blank, 0.0)
    coeff = jnp.concatenate([head, coeff[8:]], axis=0)
    grad_logits = (coeff - exps_ref[:, here] * spread).astype(BF16)
    grad_hidden = jnp.dot(weights_ref[...], grad_logits, preferred_element_type=F32)
    hidden = hidden_ref[:, here]
    hidden_wide = hidden.astype(F32)
    grad_summed = grad_hidden * (1.0 - hidden_wide * hidden_wide)
    enc_term = balanced(jnp.add, [grad_summed[:, k * LANES : (k + 1) * LANES] for k in range(GROUP)])
    enc_sum[...] = enc_term if step == 0 else enc_sum[...] + enc_term
    starts = rows_to_lanes(starts_ref[...])
    base = starts + step * GROUP
    rows = jnp.concatenate([base + k for k in range(GROUP)], axis=1)
    wanted = rows + jnp.concatenate([per_lane(half, 0, label_rows)] * GROUP, axis=1)
    slot = row_ids((8 * PRED_SLOT, WIDE))
    match = (slot // PRED_SLOT * PRED_SHARE + slot % PRED_SLOT == wanted) & (slot % PRED_SLOT < PRED_SHARE)
    pred_term = lax.dot_general(
        match.astype(BF16), grad_summed.astype(BF16), NT_DIMS, preferred_element_type=F32
    )
    pred_sum[...] = pred_term if step == 0 else pred_sum[...] + pred_term
    weight_term = lax.dot_general(hidden, grad_logits, NT_DIMS, preferred_element_type=F32)
    weight_sum[...] = weight_term if step == 0 else weight_sum[...] + weight_term


def params():
    return pltpu.CompilerParams(dimension_semantics=("arbitrary",), vmem_limit_bytes=VMEM_BYTES)


def whole(shape):
    return pl.BlockSpec(shape, lambda i: (0,) * len(shape))


smem = pl.BlockSpec(memory_space=pltpu.SMEM)
vmem = pl.BlockSpec(memory_space=pltpu.VMEM)


def exchange(blocks, axes):
    return lax.all_to_all(blocks, axes, 0, 0, tiled=True)


def share_copies(block, axes):
    count = lax.axis_size(axes)
    return exchange(jnp.broadcast_to(block[None], (count, *block.shape)), axes)


def per_device(encoder, predictor, starts, frame_lengths, label_lengths, labels, w_out):
    utt_count, frame_count, width = encoder.shape
    own_rows, vocab = w_out.shape
    label_rows = predictor.shape[1]
    tm_index = lax.axis_index(TM)
    tm_count = lax.axis_size(TM)
    utt_size = lax.axis_size(UTT)
    piece = own_rows // tm_count
    padded = -(-vocab // LANES) * LANES
    fold = piece * padded // LANES
    share = width // tm_count
    rows = S * utt_count * frame_count
    shape = jax.ShapeDtypeStruct

    mine = lax.dynamic_slice_in_dim(w_out, tm_index * piece, piece, axis=0)
    mine = jnp.pad(mine, ((0, 0), (0, padded - vocab))).reshape(fold, LANES)
    held = share_copies(mine, UTT).reshape(share, padded)
    block = tm_index.reshape(1).astype(jnp.int32)

    hidden, label_ids = pl.pallas_call(
        functools.partial(hidden_kernel, own_rows),
        grid=(STEPS,),
        in_specs=[
            whole(starts.shape),
            whole(labels.shape),
            whole((utt_count * frame_count, width)),
            whole(predictor.shape),
        ],
        out_specs=[pl.BlockSpec((width, WIDE), lambda i: (0, i)), whole((S, LANES))],
        out_shape=[shape((width, rows), BF16), shape((S, LANES), jnp.int32)],
        scratch_shapes=[
            pltpu.VMEM((width, LANES), F32),
            pltpu.VMEM((width, 2 * PRED_PAD), BF16),
            pltpu.VMEM((2 * PRED_PAD, width), F32),
        ],
        compiler_params=params(),
        cost_estimate=pl.CostEstimate(
            flops=2 * 2 * PRED_PAD * width * rows, bytes_accessed=3 * 2**20, transcendentals=width * rows
        ),
    )(starts, labels, encoder.reshape(-1, width), predictor)

    held, hidden = lax.optimization_barrier((held, hidden))
    gathered = share_copies(held, TM).reshape(width, padded)
    levels = frame_count.bit_length() - 1
    exps, lps, tree, payload = pl.pallas_call(
        functools.partial(forward_kernel, vocab),
        in_specs=[vmem, smem, smem, smem] + [vmem] * 3,
        out_specs=[vmem] * 4,
        out_shape=[
            shape((padded, rows), F32),
            shape((3, S, LANES), F32),
            shape((levels, S, S, LANES), F32),
            shape((8, LANES), F32),
        ],
        scratch_shapes=[
            pltpu.VMEM((padded, width), BF16),
            pltpu.VMEM((S, S, LANES), F32),
        ],
        compiler_params=pltpu.CompilerParams(vmem_limit_bytes=VMEM_BYTES),
        cost_estimate=pl.CostEstimate(
            flops=2 * padded * width * rows, bytes_accessed=8 * 2**20, transcendentals=padded * rows
        ),
    )(starts, frame_lengths, label_lengths, block, label_ids, gathered, hidden)

    blocks = share_copies(payload, TM)

    losses, grad_encoder, send = pl.pallas_call(
        functools.partial(backward_kernel, own_rows, label_rows),
        in_specs=[vmem, smem, smem, smem] + [vmem] * 7,
        out_specs=[smem, vmem, vmem],
        out_shape=[
            shape((utt_count,), F32),
            shape((utt_count * frame_count, width), BF16),
            shape((tm_count, share + PRED_SLOT, padded), BF16),
        ],
        scratch_shapes=[
            pltpu.VMEM((S, S, LANES), F32),
            pltpu.VMEM((2, LANES, LANES), F32),
            pltpu.VMEM((S, LANES), F32),
            pltpu.VMEM((2, S, LANES), F32),
            pltpu.VMEM((width, LANES), F32),
            pltpu.VMEM((8 * PRED_SLOT, width), F32),
            pltpu.VMEM((width, padded), F32),
        ],
        compiler_params=pltpu.CompilerParams(vmem_limit_bytes=VMEM_BYTES),
        cost_estimate=pl.CostEstimate(
            flops=6 * padded * width * rows, bytes_accessed=8 * 2**20, transcendentals=2**16
        ),
    )(starts, frame_lengths, label_lengths, block, blocks, lps, tree, label_ids, gathered, hidden, exps)

    block_sum = jnp.sum(exchange(send, TM).astype(F32), axis=0)
    pred_rows = block_sum[share : share + PRED_SHARE]
    weight_rows = exchange(block_sum[:share].reshape(utt_size, fold, LANES), UTT)
    own_weight = jnp.sum(weight_rows, axis=0).reshape(piece, padded)
    final = share_copies(jnp.concatenate([pred_rows, own_weight], axis=0).astype(BF16), TM).astype(F32)
    grad_predictor = final[:, :PRED_SHARE].reshape(-1, width)[: utt_count * label_rows]
    grad_predictor = grad_predictor.reshape(utt_count, label_rows, width)
    grad_w_out = final[:, PRED_SHARE:, :vocab].reshape(own_rows, vocab)
    return (losses, grad_encoder.reshape(encoder.shape), grad_predictor, grad_w_out)


def solution(mesh):
    return jax.shard_map(
        per_device,
        mesh=mesh,
        in_specs=(
            P(UTT, TM, None),
            P(UTT, None, None),
            P(UTT, TM),
            P(UTT),
            P(UTT),
            P(UTT, None),
            P(UTT, None),
        ),
        out_specs=(P(UTT), P(UTT, TM, None), P(UTT, None, None), P(UTT, None)),
        check_vma=False,
    )
```

time: 128 us -> 121 us (0.945)
  Pallas kernels: 22.1 us -> 14.7 us
    pallas_call x1, Pallas kernels: 10.7 us -> 5 us  [per_device(): pl.pallas_call(functools.partial(forward_kernel, vocab), in_specs=[vmem,...]
    pallas_call x1, Pallas kernels: 9.27 us -> 7.6 us  [per_device(): pl.pallas_call(functools.partial(backward_kernel, own_rows, label_rows),...]
where the time goes in v6:
time: 121 us; the launch traced here: 120 us
  blocking collectives  50.9 us (42%)
  starting transfers between devices  24.7 us (20%)
  waiting for transfers between devices  22.2 us (18%)
  Pallas kernels  14.7 us (12%)
  local copies, waits for them, and re-layouts  7.01 us (6%)
    all_to_all x4, blocking collectives, exchange(): return lax.all_to_all(blocks, axes, 0, 0, tiled=True)  50.9 us
    all_to_all x2, starting transfers between devices, exchange(): return lax.all_to_all(blocks, axes, 0, 0, tiled=True)  24.7 us
    all_to_all x2, waiting for transfers between devices, exchange(): return lax.all_to_all(blocks, axes, 0, 0, tiled=True)  22.2 us
    pallas_call x1, Pallas kernels, per_device(): pl.pallas_call(functools.partial(backward_kernel, own_rows, label_rows),...  7.6 us
    unnamed x19, local copies, waits for them, and re-layouts  5.42 us
    pallas_call x1, Pallas kernels, per_device(): pl.pallas_call(functools.partial(forward_kernel, vocab), in_specs=[vmem,...  5 us
  transfers between devices with their start and end apart: 2, of which 2 were waited for; matrix products, arithmetic and copies ran while one was open for 1% of the time, Pallas kernels for 2%

profile of v6, /device:TPU:1, one launch (start us, length us, event | category | flops | bytes accessed | tf_op | source)
XLA Modules:
  0.0 120.5 jit_solution(11229605104300818836)
XLA Ops:
  0.6 0.0 copy-start
  0.7 0.7 copy-done
  1.4 0.6 broadcast_in_dim.11
  2.0 19.2 %all-to-all-start = ((bf16[64,4,128]{2,1,0:T(4,128)(2,1)}), bf16[64,4,128]{2,1,0:T(4,128)(2,1)S(1)}, u32[]{:S(2)}, u32[]{:S(2)}) async-start(bf16[64,4,128]{2,1,0:T(4,128)(2,1)} %broadcast_in_dim.11), calls=%async_computation | async-start | bytes 131072 | tf_op jit(solution)/shard_map/all_to_all | solution.py:414
  21.3 0.9 copy.15.pred_ref
  22.2 0.9 copy-done.1
  23.1 0.7 copy-done.2
  23.8 0.7 copy-done.3
  24.5 2.1 %shard_map.102 = (bf16[512,2048]{1,0:T(8,128)(2,1)S(1)}, s32[16,128]{1,0:T(8,128)S(1)}) custom-call(s32[2,64]{1,0:T(2,128)S(1)} %copy-done.3, s32[2,64]{1,0:T(2,128)S(1)} %copy-done.2, bf16[128,512]{1,0:T(8,128)(2,1)S(1)} %bitcast.22, bf16[2,65,512]{2,1,0:T(8,128)(2,1)S(1)} %copy.15.pred_ref), custom_call_target="tpu_custom_call" | custom-call | flops 335544320 | bytes 3145728 | tf_op jit(solution)/shard_map/pallas_call | solution.py:441
  26.6 8.2 %all-to-all-done = bf16[64,4,128]{2,1,0:T(4,128)(2,1)S(1)} async-done(((bf16[64,4,128]{2,1,0:T(4,128)(2,1)}), bf16[64,4,128]{2,1,0:T(4,128)(2,1)S(1)}, u32[]{:S(2)}, u32[]{:S(2)}) %all-to-all-start) | async-done | bytes 65568 | tf_op jit(solution)/shard_map/all_to_all | solution.py:414
  34.9 15.7 %all_to_all.30 = bf16[8,64,512]{2,1,0:T(8,128)(2,1)S(1)} all-to-all(bf16[8,64,512]{2,1,0:T(8,128)(2,1)S(1)} %broadcast_in_dim.12), channel_id=1, replica_groups=mesh['tm'=8,'utt'=64] {'tm'}, dimensions={0} | all-to-all | bytes 1048576 | tf_op jit(solution)/shard_map/all_to_all | solution.py:414
  50.6 5.0 %shard_map.103 = (f32[512,2048]{1,0:T(8,128)S(1)}, f32[3,16,128]{2,1,0:T(8,128)S(1)}, f32[6,16,16,128]{3,2,1,0:T(8,128)S(1)}, f32[8,128]{1,0:T(8,128)S(1)}) custom-call(s32[2,64]{1,0:T(2,128)S(1)} %copy-done.4, s32[2]{0:T(128)S(1)} %copy-done.5, s32[2]{0:T(128)S(1)} %copy-done.6, s32[1]{0:T(128)} %bitcast.block_ref, ...), custom_call_target="tpu_custom_call" | custom-call | flops 1073741824 | bytes 8388608 | tf_op jit(solution)/shard_map/pallas_call | solution.py:466
  55.6 8.1 %all_to_all.31.blocks_ref = f32[8,8,128]{2,1,0:T(8,128)S(1)} all-to-all(f32[8,8,128]{2,1,0:T(8,128)S(1)} %broadcast_in_dim.13), channel_id=1, replica_groups=mesh['tm'=8,'utt'=64] {'tm'}, dimensions={0} | all-to-all | bytes 65536 | tf_op jit(solution)/shard_map/all_to_all | solution.py:414
  63.8 7.6 %shard_map.104 = (f32[2]{0:T(128)}, bf16[128,512]{1,0:T(8,128)(2,1)}, bf16[8,96,512]{2,1,0:T(8,128)(2,1)S(1)}) custom-call(s32[2,64]{1,0:T(2,128)S(1)} %copy-done.4, s32[2]{0:T(128)S(1)} %copy-done.5, s32[2]{0:T(128)S(1)} %copy-done.6, s32[1]{0:T(128)} %bitcast.block_ref, f32[8,8,128]{2,1,0:T(8,128)S(1)} %all_to_all.31.blocks_ref, ...), custom_call_target="tpu_custom_call" | custom-call | flops 3221225472 | bytes 8388608 | tf_op jit(solution)/shard_map/pallas_call | solution.py:488
  71.4 15.4 %all_to_all.32 = bf16[8,96,512]{2,1,0:T(8,128)(2,1)S(1)} all-to-all(bf16[8,96,512]{2,1,0:T(8,128)(2,1)S(1)} %get-tuple-element.25), channel_id=1, replica_groups=mesh['tm'=8,'utt'=64] {'tm'}, dimensions={0} | all-to-all | bytes 1572864 | tf_op jit(solution)/shard_map/all_to_all | solution.py:414
  86.7 0.1 convert_reduce_fusion
  86.8 0.7 reshape.61
  87.5 5.5 %all-to-all-start.4 = ((f32[64,4,128]{2,1,0:T(4,128)}), f32[64,4,128]{2,1,0:T(4,128)S(1)}, u32[]{:S(2)}, u32[]{:S(2)}) async-start(f32[64,4,128]{2,1,0:T(4,128)} %reshape.61), calls=%async_computation.4 | async-start | bytes 262144 | tf_op jit(solution)/shard_map/all_to_all | solution.py:414
  93.0 13.9 %all-to-all-done.4 = f32[64,4,128]{2,1,0:T(4,128)S(1)} async-done(((f32[64,4,128]{2,1,0:T(4,128)}), f32[64,4,128]{2,1,0:T(4,128)S(1)}, u32[]{:S(2)}, u32[]{:S(2)}) %all-to-all-start.4) | async-done | bytes 131104 | tf_op jit(solution)/shard_map/all_to_all | solution.py:414
  107.0 0.1 reduce_sum.19
  107.1 11.7 %all_to_all.33 = bf16[8,18,512]{2,1,0:T(8,128)(2,1)S(1)} all-to-all(bf16[8,18,512]{2,1,0:T(8,128)(2,1)S(1)} %broadcast_in_dim.14), channel_id=1, replica_groups=mesh['tm'=8,'utt'=64] {'tm'}, dimensions={0} | all-to-all | bytes 294912 | tf_op jit(solution)/shard_map/all_to_all | solution.py:414
  118.8 0.6 copy.24
  119.5 0.1 reshape.62
  119.6 0.9 copy.16
  (22 shorter events, 0.2 us)
Async XLA Ops:
  0.6 0.7 copy-start
  2.0 48.6 %copy-start.4 = (s32[2,64]{1,0:T(2,128)S(1)}, s32[2,64]{1,0:T(2,128)}, u32[]{:S(2)}) copy-start(s32[2,64]{1,0:T(2,128)} %starts_ref.5) | copy-start | bytes 1540
  2.0 48.6 %copy-start.5 = (s32[2]{0:T(128)S(1)}, s32[2]{0:T(128)}, u32[]{:S(2)}) copy-start(s32[2]{0:T(128)} %frames_ref.3) | copy-start | bytes 28
  2.0 48.6 %copy-start.6 = (s32[2]{0:T(128)S(1)}, s32[2]{0:T(128)}, u32[]{:S(2)}) copy-start(s32[2]{0:T(128)} %labels_len_ref.3) | copy-start | bytes 28
  2.0 32.8 %all-to-all-start = ((bf16[64,4,128]{2,1,0:T(4,128)(2,1)}), bf16[64,4,128]{2,1,0:T(4,128)(2,1)S(1)}, u32[]{:S(2)}, u32[]{:S(2)}) async-start(bf16[64,4,128]{2,1,0:T(4,128)(2,1)} %broadcast_in_dim.11), calls=%async_computation | async-start | bytes 131072 | tf_op jit(solution)/shard_map/all_to_all | solution.py:414
  22.2 0.9 copy-start.1
  23.1 0.7 copy-start.2
  23.8 0.7 copy-start.3
  87.5 19.4 %all-to-all-start.4 = ((f32[64,4,128]{2,1,0:T(4,128)}), f32[64,4,128]{2,1,0:T(4,128)S(1)}, u32[]{:S(2)}, u32[]{:S(2)}) async-start(f32[64,4,128]{2,1,0:T(4,128)} %reshape.61), calls=%async_computation.4 | async-start | bytes 262144 | tf_op jit(solution)/shard_map/all_to_all | solution.py:414

commit v7 on v6

--- a/solution.py
+++ b/solution.py
@@ -20,8 +20,6 @@
 F32 = jnp.float32
 BF16 = jnp.bfloat16
 
-PRED_SHARE = 17
-PRED_SLOT = 32
 TM = "tm"
 UTT = "utt"
 
@@ -85,11 +83,10 @@
     return vector
 
 
-def slot_row(slot, own_rows, width):
-    if own_rows != 8:
-        return slot
-    share = width // 8
-    return slot % share * own_rows + slot // share
+def slot_row(slot, core, own_rows, width):
+    half, owned = width // 2, own_rows // 2
+    inner = slot % half
+    return inner // owned * own_rows + (slot // half + core) % 2 * owned + inner % owned
 
 
 def frame_shifts(starts, half):
@@ -108,19 +105,21 @@
     return rows
 
 
-def reorder(own_rows, width):
-    source = slot_row(row_ids((width, width)), own_rows, width)
+def reorder(core, own_rows, width):
+    source = slot_row(row_ids((width, width)), core, own_rows, width)
     return (lane_ids((width, width)) == source).astype(BF16)
 
 
-def hidden_kernel(own_rows, starts_ref, labels_ref, enc_ref, pred_ref, hidden_ref, label_ref, enc_t, pred_t, stack):
+def hidden_kernel(
+    own_rows, block_ref, starts_ref, labels_ref, enc_ref, pred_ref, hidden_ref, label_ref, enc_t, pred_t, stack
+):
     step = pl.program_id(0)
     half = starts_ref.shape[1]
     starts = rows_to_lanes(starts_ref[...])
 
     @pl.when(step == 0)
     def _():
-        turn = reorder(own_rows, enc_ref.shape[1])
+        turn = reorder(block_ref[0] % 2, own_rows, enc_ref.shape[1])
         enc_t[...] = lax.dot_general(turn, enc_ref[...], NT_DIMS, preferred_element_type=F32)
         stack[...] = jnp.zeros_like(stack)
         rows = pred_ref.shape[1]
@@ -156,7 +155,8 @@
     labels_len_ref,
     block_ref,
     label_ref,
-    gathered_ref,
+    own_half_ref,
+    far_half_ref,
     hidden_ref,
     exps_ref,
     lps_ref,
@@ -165,7 +165,9 @@
     weights_t,
     root,
 ):
-    weights_t[...] = jnp.transpose(gathered_ref[...])
+    split = own_half_ref.shape[0]
+    weights_t[:, :split] = jnp.transpose(own_half_ref[...])
+    weights_t[:, split:] = jnp.transpose(far_half_ref[...])
     for step in range(STEPS):
         joiner_step(step, vocab, weights_t, label_ref, hidden_ref, exps_ref, lps_ref)
     lattice_products(starts_ref, frames_ref, labels_len_ref, block_ref, lps_ref, tree_ref, payload_ref, root)
@@ -246,7 +248,6 @@
 
 def backward_kernel(
     own_rows,
-    label_rows,
     starts_ref,
     frames_ref,
     labels_len_ref,
@@ -255,11 +256,14 @@
     lps_ref,
     tree_ref,
     label_ref,
-    weights_ref,
+    own_half_ref,
+    far_half_ref,
     hidden_ref,
     exps_ref,
     losses_ref,
     grad_enc_ref,
+    weight_ref,
+    pred_ref,
     send_ref,
     chain,
     line_up,
@@ -270,7 +274,8 @@
     weight_sum,
 ):
     half = starts_ref.shape[1]
-    width = weights_ref.shape[0]
+    width = hidden_ref.shape[0]
+    core = block_ref[0] % 2
     count = blocks_ref.shape[0]
     lanes = lane_ids()
 
@@ -343,21 +348,24 @@
         grads[1, m : m + 1, :] = crossing * negative
     for step in range(STEPS):
         gradient_step(
-            step, label_rows, starts_ref, lps_ref, label_ref, weights_ref, hidden_ref, exps_ref, grads,
+            step, core, starts_ref, lps_ref, label_ref, own_half_ref, far_half_ref, hidden_ref, exps_ref, grads,
             enc_sum, pred_sum, weight_sum,
         )
-    turn = reorder(own_rows, width)
+    turn = reorder(core, own_rows, width)
     enc_rows = jnp.transpose(enc_sum[...]).astype(BF16)
     grad_enc_ref[...] = jnp.dot(enc_rows, turn, preferred_element_type=F32).astype(BF16)
-    pred_rows = jnp.dot(pred_sum[...].astype(BF16), turn, preferred_element_type=F32).astype(BF16)
-    share = width // 8
-    for p in range(8):
-        send_ref[p, 0:share, :] = weight_sum[p * share : (p + 1) * share, :].astype(BF16)
-        send_ref[p, share : share + PRED_SLOT, :] = pred_rows[p * PRED_SLOT : (p + 1) * PRED_SLOT, :]
+    split = width // 2
+    weight_ref[...] = weight_sum[:split, :]
+    send_ref[:split, :] = weight_sum[split:, :].astype(BF16)
+    upper = pred_sum[...].astype(BF16)
+    lower = (pred_sum[:PRED_PAD, :] - upper[:PRED_PAD].astype(F32)).astype(BF16)
+    turned = jnp.dot(upper, turn, preferred_element_type=F32)
+    pred_ref[...] = turned[:PRED_PAD] + jnp.dot(lower, turn, preferred_element_type=F32)
+    send_ref[split:, :] = turned[PRED_PAD:].astype(BF16)
 
 
 def gradient_step(
-    step, label_rows, starts_ref, lps_ref, label_ref, weights_ref, hidden_ref, exps_ref, grads,
+    step, core, starts_ref, lps_ref, label_ref, own_half_ref, far_half_ref, hidden_ref, exps_ref, grads,
     enc_sum, pred_sum, weight_sum,
 ):
     half = starts_ref.shape[1]
@@ -378,7 +386,9 @@
     head = coeff[:8] + jnp.where(row_ids((8, WIDE)) == 0, grad_blank, 0.0)
     coeff = jnp.concatenate([head, coeff[8:]], axis=0)
     grad_logits = (coeff - exps_ref[:, here] * spread).astype(BF16)
-    grad_hidden = jnp.dot(weights_ref[...], grad_logits, preferred_element_type=F32)
+    grad_hidden = jnp.concatenate(
+        [jnp.dot(ref[...], grad_logits, preferred_element_type=F32) for ref in (own_half_ref, far_half_ref)], axis=0
+    )
     hidden = hidden_ref[:, here]
     hidden_wide = hidden.astype(F32)
     grad_summed = grad_hidden * (1.0 - hidden_wide * hidden_wide)
@@ -387,9 +397,9 @@
     starts = rows_to_lanes(starts_ref[...])
     base = starts + step * GROUP
     rows = jnp.concatenate([base + k for k in range(GROUP)], axis=1)
-    wanted = rows + jnp.concatenate([per_lane(half, 0, label_rows)] * GROUP, axis=1)
-    slot = row_ids((8 * PRED_SLOT, WIDE))
-    match = (slot // PRED_SLOT * PRED_SHARE + slot % PRED_SLOT == wanted) & (slot % PRED_SLOT < PRED_SHARE)
+    second = jnp.concatenate([per_lane(half, 0, 1)] * GROUP, axis=1)
+    slot = row_ids((2 * PRED_PAD, WIDE))
+    match = (slot % PRED_PAD == rows) & ((slot // PRED_PAD + core) % 2 == second)
     pred_term = lax.dot_general(
         match.astype(BF16), grad_summed.astype(BF16), NT_DIMS, preferred_element_type=F32
     )
@@ -417,6 +427,10 @@
 def share_copies(block, axes):
     count = lax.axis_size(axes)
     return exchange(jnp.broadcast_to(block[None], (count, *block.shape)), axes)
+
+
+def tm_flip(block, turn):
+    return lax.ppermute(block, TM, [(i ^ turn, i) for i in range(lax.axis_size(TM))])
 
 
 def per_device(encoder, predictor, starts, frame_lengths, label_lengths, labels, w_out):
@@ -426,22 +440,23 @@
     tm_index = lax.axis_index(TM)
     tm_count = lax.axis_size(TM)
     utt_size = lax.axis_size(UTT)
-    piece = own_rows // tm_count
+    core = tm_index & 1
+    owned = own_rows // 2
+    split = width // 2
     padded = -(-vocab // LANES) * LANES
-    fold = piece * padded // LANES
-    share = width // tm_count
     rows = S * utt_count * frame_count
     shape = jax.ShapeDtypeStruct
 
-    mine = lax.dynamic_slice_in_dim(w_out, tm_index * piece, piece, axis=0)
-    mine = jnp.pad(mine, ((0, 0), (0, padded - vocab))).reshape(fold, LANES)
-    held = share_copies(mine, UTT).reshape(share, padded)
+    mine = lax.dynamic_slice_in_dim(w_out, core * owned, owned, axis=0)
+    mine = jnp.pad(mine, ((0, 0), (0, padded - vocab)))
+    own_half = share_copies(mine, UTT).reshape(split, padded)
     block = tm_index.reshape(1).astype(jnp.int32)
 
     hidden, label_ids = pl.pallas_call(
         functools.partial(hidden_kernel, own_rows),
         grid=(STEPS,),
         in_specs=[
+            smem,
             whole(starts.shape),
             whole(labels.shape),
             whole((utt_count * frame_count, width)),
@@ -458,14 +473,14 @@
         cost_estimate=pl.CostEstimate(
             flops=2 * 2 * PRED_PAD * width * rows, bytes_accessed=3 * 2**20, transcendentals=width * rows
         ),
-    )(starts, labels, encoder.reshape(-1, width), predictor)
-
-    held, hidden = lax.optimization_barrier((held, hidden))
-    gathered = share_copies(held, TM).reshape(width, padded)
+    )(block, starts, labels, encoder.reshape(-1, width), predictor)
+
+    own_half, hidden = lax.optimization_barrier((own_half, hidden))
+    far_half = tm_flip(own_half, 1)
     levels = frame_count.bit_length() - 1
     exps, lps, tree, payload = pl.pallas_call(
         functools.partial(forward_kernel, vocab),
-        in_specs=[vmem, smem, smem, smem] + [vmem] * 3,
+        in_specs=[vmem, smem, smem, smem] + [vmem] * 4,
         out_specs=[vmem] * 4,
         out_shape=[
             shape((padded, rows), F32),
@@ -481,18 +496,20 @@
         cost_estimate=pl.CostEstimate(
             flops=2 * padded * width * rows, bytes_accessed=8 * 2**20, transcendentals=padded * rows
         ),
-    )(starts, frame_lengths, label_lengths, block, label_ids, gathered, hidden)
+    )(starts, frame_lengths, label_lengths, block, label_ids, own_half, far_half, hidden)
 
     blocks = share_copies(payload, TM)
 
-    losses, grad_encoder, send = pl.pallas_call(
-        functools.partial(backward_kernel, own_rows, label_rows),
-        in_specs=[vmem, smem, smem, smem] + [vmem] * 7,
-        out_specs=[smem, vmem, vmem],
+    losses, grad_encoder, weight_own, pred_own, send = pl.pallas_call(
+        functools.partial(backward_kernel, own_rows),
+        in_specs=[vmem, smem, smem, smem] + [vmem] * 8,
+        out_specs=[smem] + [vmem] * 4,
         out_shape=[
             shape((utt_count,), F32),
             shape((utt_count * frame_count, width), BF16),
-            shape((tm_count, share + PRED_SLOT, padded), BF16),
+            shape((split, padded), F32),
+            shape((PRED_PAD, width), F32),
+            shape((split + PRED_PAD, padded), BF16),
         ],
         scratch_shapes=[
             pltpu.VMEM((S, S, LANES), F32),
@@ -500,23 +517,26 @@
             pltpu.VMEM((S, LANES), F32),
             pltpu.VMEM((2, S, LANES), F32),
             pltpu.VMEM((width, LANES), F32),
-            pltpu.VMEM((8 * PRED_SLOT, width), F32),
+            pltpu.VMEM((2 * PRED_PAD, width), F32),
             pltpu.VMEM((width, padded), F32),
         ],
         compiler_params=pltpu.CompilerParams(vmem_limit_bytes=VMEM_BYTES),
         cost_estimate=pl.CostEstimate(
             flops=6 * padded * width * rows, bytes_accessed=8 * 2**20, transcendentals=2**16
         ),
-    )(starts, frame_lengths, label_lengths, block, blocks, lps, tree, label_ids, gathered, hidden, exps)
-
-    block_sum = jnp.sum(exchange(send, TM).astype(F32), axis=0)
-    pred_rows = block_sum[share : share + PRED_SHARE]
-    weight_rows = exchange(block_sum[:share].reshape(utt_size, fold, LANES), UTT)
-    own_weight = jnp.sum(weight_rows, axis=0).reshape(piece, padded)
-    final = share_copies(jnp.concatenate([pred_rows, own_weight], axis=0).astype(BF16), TM).astype(F32)
-    grad_predictor = final[:, :PRED_SHARE].reshape(-1, width)[: utt_count * label_rows]
-    grad_predictor = grad_predictor.reshape(utt_count, label_rows, width)
-    grad_w_out = final[:, PRED_SHARE:, :vocab].reshape(own_rows, vocab)
+    )(starts, frame_lengths, label_lengths, block, blocks, lps, tree, label_ids, own_half, far_half, hidden, exps)
+
+    came = tm_flip(send, 1)
+    weight_half = (weight_own + came[:split].astype(F32)).astype(BF16).reshape(utt_size, owned, padded)
+    weight_rows = jnp.sum(exchange(weight_half, UTT).astype(F32), axis=0)
+    pred_own = pred_own + came[split:].astype(F32)
+    for turn in (2, 4):
+        pred_own = pred_own + tm_flip(pred_own.astype(BF16), turn).astype(F32)
+    pred_own = pred_own[:label_rows]
+    pred_far = tm_flip(pred_own, 1)
+    grad_predictor = jnp.stack([jnp.where(core == 1, pred_far, pred_own), jnp.where(core == 1, pred_own, pred_far)])
+    final = share_copies(weight_rows, TM).reshape(tm_count // 2, own_rows, padded)
+    grad_w_out = jnp.sum(final, axis=0)[:, :vocab]
     return (losses, grad_encoder.reshape(encoder.shape), grad_predictor, grad_w_out)
 
 

time: 121 us -> 113 us (0.934)
  blocking collectives: 50.9 us -> 9.36 us
  starting transfers between devices: 24.7 us -> 47.3 us
  waiting for transfers between devices: 22.2 us -> 30.5 us
  local copies, waits for them, and re-layouts: 7.01 us -> 9.07 us
    all_to_all x4 -> x1, blocking collectives: 50.9 us -> 9.36 us  [exchange(): return lax.all_to_all(blocks, axes, 0, 0, tiled=True)]
    ppermute x0 -> x5, starting transfers between devices: none -> 16.6 us  [tm_flip(): lax.ppermute(block, TM, [(i ^ turn, i) for i in range(lax.axis_size(TM))])]
    ppermute x0 -> x5, waiting for transfers between devices: none -> 10.9 us  [tm_flip(): lax.ppermute(block, TM, [(i ^ turn, i) for i in range(lax.axis_size(TM))])]
    all_to_all x2 -> x3, starting transfers between devices: 24.7 us -> 30.7 us  [exchange(): return lax.all_to_all(blocks, axes, 0, 0, tiled=True)]
    all_to_all x2 -> x3, waiting for transfers between devices: 22.2 us -> 19.6 us  [exchange(): return lax.all_to_all(blocks, axes, 0, 0, tiled=True)]
    unnamed x19 -> x16, local copies, waits for them, and re-layouts: 5.42 us -> 6.77 us
  transfers between devices with their start and end apart: 2 -> 8, of which waited for: 2 -> 8; matrix products, arithmetic and copies ran while one was open for 1% -> 2% of each run, Pallas kernels for 2% -> 2%
where the time goes in v7:
time: 113 us
  starting transfers between devices  47.3 us (42%)
  waiting for transfers between devices  30.5 us (27%)
  Pallas kernels  14.7 us (13%)
  blocking collectives  9.36 us (8%)
  local copies, waits for them, and re-layouts  9.07 us (8%)
    all_to_all x3, starting transfers between devices, exchange(): return lax.all_to_all(blocks, axes, 0, 0, tiled=True)  30.7 us
    all_to_all x3, waiting for transfers between devices, exchange(): return lax.all_to_all(blocks, axes, 0, 0, tiled=True)  19.6 us
    ppermute x5, starting transfers between devices, tm_flip(): lax.ppermute(block, TM, [(i ^ turn, i) for i in range(lax.axis_size(TM))])  16.6 us
    ppermute x5, waiting for transfers between devices, tm_flip(): lax.ppermute(block, TM, [(i ^ turn, i) for i in range(lax.axis_size(TM))])  10.9 us
    all_to_all x1, blocking collectives, exchange(): return lax.all_to_all(blocks, axes, 0, 0, tiled=True)  9.36 us
    pallas_call x1, Pallas kernels, per_device(): pl.pallas_call(functools.partial(backward_kernel, own_rows), in_specs=[vm...  7.56 us
    unnamed x16, local copies, waits for them, and re-layouts  6.77 us
    pallas_call x1, Pallas kernels, per_device(): pl.pallas_call(functools.partial(forward_kernel, vocab), in_specs=[vmem,...  4.99 us
  transfers between devices with their start and end apart: 8, of which 8 were waited for; matrix products, arithmetic and copies ran while one was open for 2% of the time, Pallas kernels for 2%

profile of v7, /device:TPU:1, one launch (start us, length us, event | category | flops | bytes accessed | tf_op | source)
XLA Modules:
  0.0 112.7 jit_solution(15648707416114563727)
XLA Ops:
  1.4 0.8 broadcast_in_dim.6
  2.1 19.1 %all-to-all-start = ((bf16[64,4,512]{2,1,0:T(4,128)(2,1)}), bf16[64,4,512]{2,1,0:T(4,128)(2,1)S(1)}, u32[]{:S(2)}, u32[]{:S(2)}) async-start(bf16[64,4,512]{2,1,0:T(4,128)(2,1)} %broadcast_in_dim.6), calls=%async_computation | async-start | bytes 524288 | tf_op jit(solution)/shard_map/all_to_all | solution.py:424
  21.2 0.9 copy.13.pred_ref
  22.2 0.9 copy-done.1
  24.4 2.1 %shard_map.102 = (bf16[512,2048]{1,0:T(8,128)(2,1)S(1)}, s32[16,128]{1,0:T(8,128)S(1)}) custom-call(s32[1]{0:T(128)} %bitcast.block_ref, s32[2,64]{1,0:T(2,128)S(1)} %copy-done.3, s32[2,64]{1,0:T(2,128)S(1)} %copy-done.2, bf16[128,512]{1,0:T(8,128)(2,1)S(1)} %bitcast.8, bf16[2,65,512]{2,1,0:T(8,128)(2,1)S(1)} %copy.13.pred_ref), custom_call_target="tpu_custom_call" | custom-call | flops 335544320 | bytes 3145728 | tf_op jit(solution)/shard_map/pallas_call | solution.py:455
  26.6 13.7 %all-to-all-done = bf16[64,4,512]{2,1,0:T(4,128)(2,1)S(1)} async-done(((bf16[64,4,512]{2,1,0:T(4,128)(2,1)}), bf16[64,4,512]{2,1,0:T(4,128)(2,1)S(1)}, u32[]{:S(2)}, u32[]{:S(2)}) %all-to-all-start) | async-done | bytes 262176 | tf_op jit(solution)/shard_map/all_to_all | solution.py:424
  40.4 4.8 %collective-permute-start = (bf16[256,512]{1,0:T(8,128)(2,1)S(1)}, bf16[256,512]{1,0:T(8,128)(2,1)S(1)}, u32[]{:S(2)}, u32[]{:S(2)}) collective-permute-start(bf16[256,512]{1,0:T(8,128)(2,1)S(1)} %reshape.31.own_half_ref), channel_id=1, source_target_pairs={{64,0},{0,64},{192,128},{128,192},{320,256},{256,320},{448,384},{3... | collective-permute-start | bytes 786440 | tf_op jit(solution)/shard_map/ppermute | solution.py:433
  45.2 1.1 %collective-permute-done.far_half_ref = bf16[256,512]{1,0:T(8,128)(2,1)S(1)} collective-permute-done((bf16[256,512]{1,0:T(8,128)(2,1)S(1)}, bf16[256,512]{1,0:T(8,128)(2,1)S(1)}, u32[]{:S(2)}, u32[]{:S(2)}) %collective-permute-start) | collective-permute-done | bytes 262176 | tf_op jit(solution)/shard_map/ppermute | solution.py:433
  48.3 5.0 %shard_map.103 = (f32[512,2048]{1,0:T(8,128)S(1)}, f32[3,16,128]{2,1,0:T(8,128)S(1)}, f32[6,16,16,128]{3,2,1,0:T(8,128)S(1)}, f32[8,128]{1,0:T(8,128)S(1)}) custom-call(s32[2,64]{1,0:T(2,128)S(1)} %copy-done.4, s32[2]{0:T(128)S(1)} %copy-done.5, s32[2]{0:T(128)S(1)} %copy-done.6, s32[1]{0:T(128)} %bitcast.block_ref, ...), custom_call_target="tpu_custom_call" | custom-call | flops 1073741824 | bytes 8388608 | tf_op jit(solution)/shard_map/pallas_call | solution.py:481
  53.3 9.4 %all_to_all.20.blocks_ref = f32[8,8,128]{2,1,0:T(8,128)S(1)} all-to-all(f32[8,8,128]{2,1,0:T(8,128)S(1)} %broadcast_in_dim.7), channel_id=1, replica_groups=mesh['tm'=8,'utt'=64] {'tm'}, dimensions={0} | all-to-all | bytes 65536 | tf_op jit(solution)/shard_map/all_to_all | solution.py:424
  62.7 7.6 %shard_map.104 = (f32[2]{0:T(128)}, bf16[128,512]{1,0:T(8,128)(2,1)}, f32[256,512]{1,0:T(8,128)S(1)}, f32[80,512]{1,0:T(8,128)S(1)}, bf16[336,512]{1,0:T(8,128)(2,1)S(1)}) custom-call(s32[2,64]{1,0:T(2,128)S(1)} %copy-done.4, s32[2]{0:T(128)S(1)} %copy-done.5, s32[2]{0:T(128)S(1)} %copy-done.6, s32[1]{0:T(128)} %bitcast.block_ref, ...), custom_call_target="tpu_custom_call" | custom-call | flops 3221225472 | bytes 8388608 | tf_op jit(solution)/shard_map/pallas_call | solution.py:503
  70.2 2.6 %collective-permute-start.1 = (bf16[336,512]{1,0:T(8,128)(2,1)S(1)}, bf16[336,512]{1,0:T(8,128)(2,1)S(1)}, u32[]{:S(2)}, u32[]{:S(2)}) collective-permute-start(bf16[336,512]{1,0:T(8,128)(2,1)S(1)} %get-tuple-element.28), channel_id=1, source_target_pairs={{64,0},{0,64},{192,128},{128,192},{320,256},{256,320},{448,384},{3... | collective-permute-start | bytes 1032200 | tf_op jit(solution)/shard_map/ppermute | solution.py:433
  72.9 1.3 %collective-permute-done.1 = bf16[336,512]{1,0:T(8,128)(2,1)S(1)} collective-permute-done((bf16[336,512]{1,0:T(8,128)(2,1)S(1)}, bf16[336,512]{1,0:T(8,128)(2,1)S(1)}, u32[]{:S(2)}, u32[]{:S(2)}) %collective-permute-start.1) | collective-permute-done | bytes 344096 | tf_op jit(solution)/shard_map/ppermute | solution.py:433
  75.0 6.2 %all-to-all-start.2 = ((bf16[64,4,512]{2,1,0:T(4,128)(2,1)}), bf16[64,4,512]{2,1,0:T(4,128)(2,1)S(1)}, u32[]{:S(2)}, u32[]{:S(2)}) async-start(bf16[64,4,512]{2,1,0:T(4,128)(2,1)} %reshape.33), calls=%async_computation.2 | async-start | bytes 524288 | tf_op jit(solution)/shard_map/all_to_all | solution.py:424
  81.2 2.2 %collective-permute-start.2 = (bf16[80,512]{1,0:T(8,128)(2,1)S(1)}, bf16[80,512]{1,0:T(8,128)(2,1)S(1)}, u32[]{:S(2)}, u32[]{:S(2)}) collective-permute-start(bf16[80,512]{1,0:T(8,128)(2,1)S(1)} %fusion), channel_id=1, source_target_pairs={{128,0},{192,64},{0,128},{64,192},{384,256},{448,320},{256,384},{3... | collective-permute-start | bytes 245768 | tf_op jit(solution)/shard_map/ppermute | solution.py:433
  83.4 3.3 %collective-permute-done.2 = bf16[80,512]{1,0:T(8,128)(2,1)S(1)} collective-permute-done((bf16[80,512]{1,0:T(8,128)(2,1)S(1)}, bf16[80,512]{1,0:T(8,128)(2,1)S(1)}, u32[]{:S(2)}, u32[]{:S(2)}) %collective-permute-start.2) | collective-permute-done | bytes 81952 | tf_op jit(solution)/shard_map/ppermute | solution.py:433
  86.7 2.7 %collective-permute-start.3 = (bf16[80,512]{1,0:T(8,128)(2,1)S(1)}, bf16[80,512]{1,0:T(8,128)(2,1)S(1)}, u32[]{:S(2)}, u32[]{:S(2)}) collective-permute-start(bf16[80,512]{1,0:T(8,128)(2,1)S(1)} %get-tuple-element.38), channel_id=1, source_target_pairs={{256,0},{320,64},{384,128},{448,192},{0,256},{64,320},{128,384},{1... | collective-permute-start | bytes 245768 | tf_op jit(solution)/shard_map/ppermute | solution.py:433
  89.4 4.3 %collective-permute-done.3 = bf16[80,512]{1,0:T(8,128)(2,1)S(1)} collective-permute-done((bf16[80,512]{1,0:T(8,128)(2,1)S(1)}, bf16[80,512]{1,0:T(8,128)(2,1)S(1)}, u32[]{:S(2)}, u32[]{:S(2)}) %collective-permute-start.3) | collective-permute-done | bytes 81952 | tf_op jit(solution)/shard_map/ppermute | solution.py:433
  93.7 4.3 %collective-permute-start.4 = (f32[65,512]{1,0:T(8,128)S(1)}, f32[65,512]{1,0:T(8,128)S(1)}, u32[]{:S(2)}, u32[]{:S(2)}) collective-permute-start(f32[65,512]{1,0:T(8,128)S(1)} %slice_add_fusion), channel_id=1, source_target_pairs={{64,0},{0,64},{192,128},{128,192},{320,256},{256,320},{448,384},{3... | collective-permute-start | bytes 399368 | tf_op jit(solution)/shard_map/ppermute | solution.py:433
  98.0 1.0 collective-permute-done.4
  99.0 2.0 %all-to-all-done.2 = bf16[64,4,512]{2,1,0:T(4,128)(2,1)S(1)} async-done(((bf16[64,4,512]{2,1,0:T(4,128)(2,1)}), bf16[64,4,512]{2,1,0:T(4,128)(2,1)S(1)}, u32[]{:S(2)}, u32[]{:S(2)}) %all-to-all-start.2) | async-done | bytes 262176 | tf_op jit(solution)/shard_map/all_to_all | solution.py:424
  101.8 5.4 %all-to-all-start.3 = ((f32[8,4,512]{2,1,0:T(4,128)}), f32[8,4,512]{2,1,0:T(4,128)S(1)}, u32[]{:S(2)}, u32[]{:S(2)}) async-start(f32[8,4,512]{2,1,0:T(4,128)} %broadcast_in_dim.8), calls=%async_computation.3 | async-start | bytes 131072 | tf_op jit(solution)/shard_map/all_to_all | solution.py:424
  107.2 0.9 copy.14
  108.1 3.9 %all-to-all-done.3 = f32[8,4,512]{2,1,0:T(4,128)S(1)} async-done(((f32[8,4,512]{2,1,0:T(4,128)}), f32[8,4,512]{2,1,0:T(4,128)S(1)}, u32[]{:S(2)}, u32[]{:S(2)}) %all-to-all-start.3) | async-done | bytes 65568 | tf_op jit(solution)/shard_map/all_to_all | solution.py:424
  (28 shorter events, 6.5 us)
Async XLA Ops:
  0.6 0.7 copy-start
  2.1 38.2 %all-to-all-start = ((bf16[64,4,512]{2,1,0:T(4,128)(2,1)}), bf16[64,4,512]{2,1,0:T(4,128)(2,1)S(1)}, u32[]{:S(2)}, u32[]{:S(2)}) async-start(bf16[64,4,512]{2,1,0:T(4,128)(2,1)} %broadcast_in_dim.6), calls=%async_computation | async-start | bytes 524288 | tf_op jit(solution)/shard_map/all_to_all | solution.py:424
  22.2 0.9 copy-start.1
  23.1 0.7 copy-start.2
  23.8 0.7 copy-start.3
  40.4 5.9 %collective-permute-start = (bf16[256,512]{1,0:T(8,128)(2,1)S(1)}, bf16[256,512]{1,0:T(8,128)(2,1)S(1)}, u32[]{:S(2)}, u32[]{:S(2)}) collective-permute-start(bf16[256,512]{1,0:T(8,128)(2,1)S(1)} %reshape.31.own_half_ref), channel_id=1, source_target_pairs={{64,0},{0,64},{192,128},{128,192},{320,256},{256,320},{448,384},{3... | collective-permute-start | bytes 786440 | tf_op jit(solution)/shard_map/ppermute | solution.py:433
  46.3 0.7 copy-start.4
  47.0 0.7 copy-start.5
  47.6 0.7 copy-start.6
  70.2 3.9 %collective-permute-start.1 = (bf16[336,512]{1,0:T(8,128)(2,1)S(1)}, bf16[336,512]{1,0:T(8,128)(2,1)S(1)}, u32[]{:S(2)}, u32[]{:S(2)}) collective-permute-start(bf16[336,512]{1,0:T(8,128)(2,1)S(1)} %get-tuple-element.28), channel_id=1, source_target_pairs={{64,0},{0,64},{192,128},{128,192},{320,256},{256,320},{448,384},{3... | collective-permute-start | bytes 1032200 | tf_op jit(solution)/shard_map/ppermute | solution.py:433
  75.0 26.0 %all-to-all-start.2 = ((bf16[64,4,512]{2,1,0:T(4,128)(2,1)}), bf16[64,4,512]{2,1,0:T(4,128)(2,1)S(1)}, u32[]{:S(2)}, u32[]{:S(2)}) async-start(bf16[64,4,512]{2,1,0:T(4,128)(2,1)} %reshape.33), calls=%async_computation.2 | async-start | bytes 524288 | tf_op jit(solution)/shard_map/all_to_all | solution.py:424
  81.2 5.5 %collective-permute-start.2 = (bf16[80,512]{1,0:T(8,128)(2,1)S(1)}, bf16[80,512]{1,0:T(8,128)(2,1)S(1)}, u32[]{:S(2)}, u32[]{:S(2)}) collective-permute-start(bf16[80,512]{1,0:T(8,128)(2,1)S(1)} %fusion), channel_id=1, source_target_pairs={{128,0},{192,64},{0,128},{64,192},{384,256},{448,320},{256,384},{3... | collective-permute-start | bytes 245768 | tf_op jit(solution)/shard_map/ppermute | solution.py:433
  86.7 7.0 %collective-permute-start.3 = (bf16[80,512]{1,0:T(8,128)(2,1)S(1)}, bf16[80,512]{1,0:T(8,128)(2,1)S(1)}, u32[]{:S(2)}, u32[]{:S(2)}) collective-permute-start(bf16[80,512]{1,0:T(8,128)(2,1)S(1)} %get-tuple-element.38), channel_id=1, source_target_pairs={{256,0},{320,64},{384,128},{448,192},{0,256},{64,320},{128,384},{1... | collective-permute-start | bytes 245768 | tf_op jit(solution)/shard_map/ppermute | solution.py:433
  93.7 5.3 %collective-permute-start.4 = (f32[65,512]{1,0:T(8,128)S(1)}, f32[65,512]{1,0:T(8,128)S(1)}, u32[]{:S(2)}, u32[]{:S(2)}) collective-permute-start(f32[65,512]{1,0:T(8,128)S(1)} %slice_add_fusion), channel_id=1, source_target_pairs={{64,0},{0,64},{192,128},{128,192},{320,256},{256,320},{448,384},{3... | collective-permute-start | bytes 399368 | tf_op jit(solution)/shard_map/ppermute | solution.py:433
  101.8 10.3 %all-to-all-start.3 = ((f32[8,4,512]{2,1,0:T(4,128)}), f32[8,4,512]{2,1,0:T(4,128)S(1)}, u32[]{:S(2)}, u32[]{:S(2)}) async-start(f32[8,4,512]{2,1,0:T(4,128)} %broadcast_in_dim.8), calls=%async_computation.3 | async-start | bytes 131072 | tf_op jit(solution)/shard_map/all_to_all | solution.py:424

commit v8 on v7

--- a/solution.py
+++ b/solution.py
@@ -81,12 +81,6 @@
         moved = jnp.where(places >= bit, pltpu.roll(vector, bit, 0), masked_log)
         vector = jnp.where((distance & bit) != 0, moved, vector)
     return vector
-
-
-def slot_row(slot, core, own_rows, width):
-    half, owned = width // 2, own_rows // 2
-    inner = slot % half
-    return inner // owned * own_rows + (slot // half + core) % 2 * owned + inner % owned
 
 
 def frame_shifts(starts, half):
@@ -105,29 +99,19 @@
     return rows
 
 
-def reorder(core, own_rows, width):
-    source = slot_row(row_ids((width, width)), core, own_rows, width)
-    return (lane_ids((width, width)) == source).astype(BF16)
-
-
-def hidden_kernel(
-    own_rows, block_ref, starts_ref, labels_ref, enc_ref, pred_ref, hidden_ref, label_ref, enc_t, pred_t, stack
-):
+def hidden_kernel(starts_ref, labels_ref, enc_ref, pred_ref, hidden_ref, label_ref, enc_t, pred_t, stack):
     step = pl.program_id(0)
     half = starts_ref.shape[1]
     starts = rows_to_lanes(starts_ref[...])
 
     @pl.when(step == 0)
     def _():
-        turn = reorder(block_ref[0] % 2, own_rows, enc_ref.shape[1])
-        enc_t[...] = lax.dot_general(turn, enc_ref[...], NT_DIMS, preferred_element_type=F32)
+        enc_t[...] = jnp.transpose(enc_ref[...].astype(F32))
         stack[...] = jnp.zeros_like(stack)
         rows = pred_ref.shape[1]
         stack[0:rows, :] = pred_ref[0].astype(F32)
         stack[PRED_PAD : PRED_PAD + rows, :] = pred_ref[1].astype(F32)
-        pred_t[...] = lax.dot_general(
-            turn, stack[...].astype(BF16), NT_DIMS, preferred_element_type=F32
-        ).astype(BF16)
+        pred_t[...] = jnp.transpose(stack[...]).astype(BF16)
         cap = labels_ref.shape[1]
         labels = labels_ref[...].astype(F32)
         table = [jnp.transpose(jnp.broadcast_to(labels[b : b + 1, :], (LANES, cap))) for b in range(2)]
@@ -151,9 +135,7 @@
 def forward_kernel(
     vocab,
     starts_ref,
-    frames_ref,
-    labels_len_ref,
-    block_ref,
+    meta_ref,
     label_ref,
     own_half_ref,
     far_half_ref,
@@ -165,12 +147,13 @@
     weights_t,
     root,
 ):
-    split = own_half_ref.shape[0]
-    weights_t[:, :split] = jnp.transpose(own_half_ref[...])
-    weights_t[:, split:] = jnp.transpose(far_half_ref[...])
+    split = own_half_ref.shape[1]
+    core = meta_ref[0] % 2
+    weights_t[pl.ds(pl.multiple_of(core * split, split), split), :] = jnp.transpose(own_half_ref[...])
+    weights_t[pl.ds(pl.multiple_of((1 - core) * split, split), split), :] = jnp.transpose(far_half_ref[...])
     for step in range(STEPS):
         joiner_step(step, vocab, weights_t, label_ref, hidden_ref, exps_ref, lps_ref)
-    lattice_products(starts_ref, frames_ref, labels_len_ref, block_ref, lps_ref, tree_ref, payload_ref, root)
+    lattice_products(starts_ref, meta_ref, lps_ref, tree_ref, payload_ref, root)
 
 
 def joiner_step(step, vocab, weights_t, label_ref, hidden_ref, exps_ref, lps_ref):
@@ -197,13 +180,13 @@
         lps_ref[2, row, :] = scale[:, part]
 
 
-def lattice_products(starts_ref, frames_ref, labels_len_ref, block_ref, lps_ref, tree_ref, payload_ref, root):
+def lattice_products(starts_ref, meta_ref, lps_ref, tree_ref, payload_ref, root):
     half = starts_ref.shape[1]
     lanes = lane_ids()
     starts = rows_to_lanes(starts_ref[...])
-    frame = block_ref[0] * half + lanes % half
-    live = frame < per_lane(half, frames_ref[0], frames_ref[1])
-    limit = per_lane(half, labels_len_ref[0], labels_len_ref[1])
+    frame = meta_ref[0] * half + lanes % half
+    live = frame < per_lane(half, meta_ref[1], meta_ref[2])
+    limit = per_lane(half, meta_ref[3], meta_ref[4])
     allowed = live & (row_ids((S, LANES)) + starts < limit)
     blank = jnp.where(live, lps_ref[0], 0.0)
     emit = jnp.where(allowed, lps_ref[1], masked_log)
@@ -247,11 +230,8 @@
 
 
 def backward_kernel(
-    own_rows,
     starts_ref,
-    frames_ref,
-    labels_len_ref,
-    block_ref,
+    meta_ref,
     blocks_ref,
     lps_ref,
     tree_ref,
@@ -272,10 +252,11 @@
     enc_sum,
     pred_sum,
     weight_sum,
+    joined,
 ):
     half = starts_ref.shape[1]
     width = hidden_ref.shape[0]
-    core = block_ref[0] % 2
+    core = meta_ref[0] % 2
     count = blocks_ref.shape[0]
     lanes = lane_ids()
 
@@ -294,7 +275,7 @@
         chain[h * S // 2 : (h + 1) * S // 2] = jnp.transpose(line_up[h]).reshape(S // 2, S, LANES)
     odd = lanes % 2 == 1
     last_start = [blocks_ref[count - 1, 4 * b + 2 : 4 * b + 3, :].astype(jnp.int32) for b in range(2)]
-    final_place = jnp.where(odd, labels_len_ref[1] - last_start[1], labels_len_ref[0] - last_start[0])
+    final_place = jnp.where(odd, meta_ref[4] - last_start[1], meta_ref[3] - last_start[0])
     gap = (begins - pltpu.roll(ends, 2, 1)).astype(jnp.int32)
     gap = jnp.where((lanes >= 2) & (lanes < 2 * count), gap, 0)
     forward = jnp.where(places == 0, 0.0, masked_log) + jnp.zeros((S, LANES), F32)
@@ -311,11 +292,11 @@
     log_total = best + jnp.log(jnp.sum(jnp.exp(leaving - best), axis=0, keepdims=True))
     for b in range(2):
         own_total = jnp.sum(jnp.where(lanes == 2 * (count - 1) + b, log_total, 0.0))
-        losses_ref[b] = -own_total / frames_ref[b].astype(F32)
+        losses_ref[b] = -own_total / meta_ref[1 + b].astype(F32)
 
     def own_boundary(vectors):
         columns = [
-            jnp.sum(jnp.where(lanes == 2 * block_ref[0] + b, vectors, 0.0), axis=1, keepdims=True)
+            jnp.sum(jnp.where(lanes == 2 * meta_ref[0] + b, vectors, 0.0), axis=1, keepdims=True)
             for b in range(2)
         ]
         spread = jnp.where(lanes < half, columns[0], columns[1])
@@ -346,26 +327,27 @@
     for m in range(S):
         crossing = jnp.sum(jnp.where(places > m, weights[m], 0.0), axis=0, keepdims=True)
         grads[1, m : m + 1, :] = crossing * negative
+    split = own_half_ref.shape[1]
+    own_columns = pl.ds(pl.multiple_of(core * split, split), split)
+    far_columns = pl.ds(pl.multiple_of((1 - core) * split, split), split)
+    joined[:, own_columns] = own_half_ref[...]
+    joined[:, far_columns] = far_half_ref[...]
     for step in range(STEPS):
         gradient_step(
-            step, core, starts_ref, lps_ref, label_ref, own_half_ref, far_half_ref, hidden_ref, exps_ref, grads,
+            step, core, starts_ref, lps_ref, label_ref, joined, hidden_ref, exps_ref, grads,
             enc_sum, pred_sum, weight_sum,
         )
-    turn = reorder(core, own_rows, width)
-    enc_rows = jnp.transpose(enc_sum[...]).astype(BF16)
-    grad_enc_ref[...] = jnp.dot(enc_rows, turn, preferred_element_type=F32).astype(BF16)
-    split = width // 2
-    weight_ref[...] = weight_sum[:split, :]
-    send_ref[:split, :] = weight_sum[split:, :].astype(BF16)
-    upper = pred_sum[...].astype(BF16)
-    lower = (pred_sum[:PRED_PAD, :] - upper[:PRED_PAD].astype(F32)).astype(BF16)
-    turned = jnp.dot(upper, turn, preferred_element_type=F32)
-    pred_ref[...] = turned[:PRED_PAD] + jnp.dot(lower, turn, preferred_element_type=F32)
-    send_ref[split:, :] = turned[PRED_PAD:].astype(BF16)
+    grad_enc_ref[...] = jnp.transpose(enc_sum[...]).astype(BF16)
+    weight_ref[...] = weight_sum[:, own_columns]
+    send_ref[:width, :] = weight_sum[:, far_columns].astype(BF16)
+    for i in range(2):
+        rows, columns = slice(i * PRED_PAD, (i + 1) * PRED_PAD), slice(i * split, (i + 1) * split)
+        pred_ref[rows, :] = pred_sum[:PRED_PAD, columns]
+        send_ref[width + i * PRED_PAD : width + (i + 1) * PRED_PAD, :] = pred_sum[PRED_PAD:, columns].astype(BF16)
 
 
 def gradient_step(
-    step, core, starts_ref, lps_ref, label_ref, own_half_ref, far_half_ref, hidden_ref, exps_ref, grads,
+    step, core, starts_ref, lps_ref, label_ref, joined, hidden_ref, exps_ref, grads,
     enc_sum, pred_sum, weight_sum,
 ):
     half = starts_ref.shape[1]
@@ -386,9 +368,7 @@
     head = coeff[:8] + jnp.where(row_ids((8, WIDE)) == 0, grad_blank, 0.0)
     coeff = jnp.concatenate([head, coeff[8:]], axis=0)
     grad_logits = (coeff - exps_ref[:, here] * spread).astype(BF16)
-    grad_hidden = jnp.concatenate(
-        [jnp.dot(ref[...], grad_logits, preferred_element_type=F32) for ref in (own_half_ref, far_half_ref)], axis=0
-    )
+    grad_hidden = jnp.dot(joined[...], grad_logits, preferred_element_type=F32)
     hidden = hidden_ref[:, here]
     hidden_wide = hidden.astype(F32)
     grad_summed = grad_hidden * (1.0 - hidden_wide * hidden_wide)
@@ -441,22 +421,19 @@
     tm_count = lax.axis_size(TM)
     utt_size = lax.axis_size(UTT)
     core = tm_index & 1
-    owned = own_rows // 2
-    split = width // 2
-    padded = -(-vocab // LANES) * LANES
+    padded = -(-vocab // 256) * 256
+    split = padded // 2
     rows = S * utt_count * frame_count
     shape = jax.ShapeDtypeStruct
 
-    mine = lax.dynamic_slice_in_dim(w_out, core * owned, owned, axis=0)
-    mine = jnp.pad(mine, ((0, 0), (0, padded - vocab)))
-    own_half = share_copies(mine, UTT).reshape(split, padded)
-    block = tm_index.reshape(1).astype(jnp.int32)
+    mine = lax.dynamic_slice_in_dim(jnp.pad(w_out, ((0, 0), (0, padded - vocab))), core * split, split, axis=1)
+    own_half = share_copies(mine, UTT).reshape(width, split)
+    meta = jnp.concatenate([tm_index.reshape(1).astype(jnp.int32), frame_lengths, label_lengths])
 
     hidden, label_ids = pl.pallas_call(
-        functools.partial(hidden_kernel, own_rows),
+        hidden_kernel,
         grid=(STEPS,),
         in_specs=[
-            smem,
             whole(starts.shape),
             whole(labels.shape),
             whole((utt_count * frame_count, width)),
@@ -473,14 +450,14 @@
         cost_estimate=pl.CostEstimate(
             flops=2 * 2 * PRED_PAD * width * rows, bytes_accessed=3 * 2**20, transcendentals=width * rows
         ),
-    )(block, starts, labels, encoder.reshape(-1, width), predictor)
+    )(starts, labels, encoder.reshape(-1, width), predictor)
 
     own_half, hidden = lax.optimization_barrier((own_half, hidden))
     far_half = tm_flip(own_half, 1)
     levels = frame_count.bit_length() - 1
     exps, lps, tree, payload = pl.pallas_call(
         functools.partial(forward_kernel, vocab),
-        in_specs=[vmem, smem, smem, smem] + [vmem] * 4,
+        in_specs=[vmem, smem] + [vmem] * 4,
         out_specs=[vmem] * 4,
         out_shape=[
             shape((padded, rows), F32),
@@ -496,20 +473,20 @@
         cost_estimate=pl.CostEstimate(
             flops=2 * padded * width * rows, bytes_accessed=8 * 2**20, transcendentals=padded * rows
         ),
-    )(starts, frame_lengths, label_lengths, block, label_ids, own_half, far_half, hidden)
+    )(starts, meta, label_ids, own_half, far_half, hidden)
 
     blocks = share_copies(payload, TM)
 
     losses, grad_encoder, weight_own, pred_own, send = pl.pallas_call(
-        functools.partial(backward_kernel, own_rows),
-        in_specs=[vmem, smem, smem, smem] + [vmem] * 8,
+        backward_kernel,
+        in_specs=[vmem, smem] + [vmem] * 8,
         out_specs=[smem] + [vmem] * 4,
         out_shape=[
             shape((utt_count,), F32),
             shape((utt_count * frame_count, width), BF16),
-            shape((split, padded), F32),
-            shape((PRED_PAD, width), F32),
-            shape((split + PRED_PAD, padded), BF16),
+            shape((width, split), F32),
+            shape((2 * PRED_PAD, split), F32),
+            shape((width + 2 * PRED_PAD, split), BF16),
         ],
         scratch_shapes=[
             pltpu.VMEM((S, S, LANES), F32),
@@ -519,24 +496,27 @@
             pltpu.VMEM((width, LANES), F32),
             pltpu.VMEM((2 * PRED_PAD, width), F32),
             pltpu.VMEM((width, padded), F32),
+            pltpu.VMEM((width, padded), BF16),
         ],
         compiler_params=pltpu.CompilerParams(vmem_limit_bytes=VMEM_BYTES),
         cost_estimate=pl.CostEstimate(
             flops=6 * padded * width * rows, bytes_accessed=8 * 2**20, transcendentals=2**16
         ),
-    )(starts, frame_lengths, label_lengths, block, blocks, lps, tree, label_ids, own_half, far_half, hidden, exps)
+    )(starts, meta, blocks, lps, tree, label_ids, own_half, far_half, hidden, exps)
 
     came = tm_flip(send, 1)
-    weight_half = (weight_own + came[:split].astype(F32)).astype(BF16).reshape(utt_size, owned, padded)
+    weight_half = (weight_own + came[:width].astype(F32)).astype(BF16).reshape(utt_size, own_rows, split)
     weight_rows = jnp.sum(exchange(weight_half, UTT).astype(F32), axis=0)
-    pred_own = pred_own + came[split:].astype(F32)
+    pred_own = pred_own + came[width:].astype(F32)
     for turn in (2, 4):
         pred_own = pred_own + tm_flip(pred_own.astype(BF16), turn).astype(F32)
-    pred_own = pred_own[:label_rows]
     pred_far = tm_flip(pred_own, 1)
-    grad_predictor = jnp.stack([jnp.where(core == 1, pred_far, pred_own), jnp.where(core == 1, pred_own, pred_far)])
-    final = share_copies(weight_rows, TM).reshape(tm_count // 2, own_rows, padded)
-    grad_w_out = jnp.sum(final, axis=0)[:, :vocab]
+    pred_pair = jnp.stack([jnp.where(core == 1, pred_far, pred_own), jnp.where(core == 1, pred_own, pred_far)])
+    pred_pair = pred_pair.reshape(utt_count, 2, PRED_PAD, split)[:, :, :label_rows]
+    grad_predictor = jnp.concatenate([pred_pair[:, 0], pred_pair[:, 1]], axis=-1)
+    final = share_copies(weight_rows, TM).reshape(tm_count // 2, 2, own_rows, split)
+    final = jnp.sum(final, axis=0)
+    grad_w_out = jnp.concatenate([final[0], final[1]], axis=-1)[:, :vocab]
     return (losses, grad_encoder.reshape(encoder.shape), grad_predictor, grad_w_out)
 
 

time: 113 us -> 114 us (level)
  local copies, waits for them, and re-layouts: 9.07 us -> 6.25 us
  other arithmetic: 0.95 us -> 3.38 us
  starting transfers between devices: 47.3 us -> 48.6 us
    ppermute x5, waiting for transfers between devices: 10.9 us -> 5.65 us  [tm_flip(): lax.ppermute(block, TM, [(i ^ turn, i) for i in range(lax.axis_size(TM))])]
    all_to_all x3, waiting for transfers between devices: 19.6 us -> 24.8 us  [exchange(): return lax.all_to_all(blocks, axes, 0, 0, tiled=True)]
    unnamed x16 -> x9, local copies, waits for them, and re-layouts: 6.77 us -> 3.86 us
    concatenate x0 -> x3, other arithmetic: none -> 2.18 us  [the longest x1 0.82 us: per_device(): jnp.concatenate([pred_pair[:, 0], pred_pair[:, 1]], axis=-1)]
  transfers between devices with their start and end apart: 8 -> 8, of which waited for: 8 -> 7; matrix products, arithmetic and copies ran while one was open for 2% -> 3% of each run, Pallas kernels for 2% -> 2%
where the time goes in v8:
time: 114 us; the launch traced here: 113 us
  starting transfers between devices  48.6 us (43%)
  waiting for transfers between devices  30.4 us (27%)
  Pallas kernels  14.5 us (13%)
  blocking collectives  9.35 us (8%)
  local copies, waits for them, and re-layouts  6.25 us (5%)
  other arithmetic  3.38 us (3%)
    all_to_all x3, starting transfers between devices, exchange(): return lax.all_to_all(blocks, axes, 0, 0, tiled=True)  31.4 us
    all_to_all x3, waiting for transfers between devices, exchange(): return lax.all_to_all(blocks, axes, 0, 0, tiled=True)  24.8 us
    ppermute x5, starting transfers between devices, tm_flip(): lax.ppermute(block, TM, [(i ^ turn, i) for i in range(lax.axis_size(TM))])  17.3 us
    all_to_all x1, blocking collectives, exchange(): return lax.all_to_all(blocks, axes, 0, 0, tiled=True)  9.35 us
    pallas_call x1, Pallas kernels, per_device(): pl.pallas_call(backward_kernel, in_specs=[vmem, smem] + [vmem] * 8, out_s...  7.64 us
    ppermute x5, waiting for transfers between devices, tm_flip(): lax.ppermute(block, TM, [(i ^ turn, i) for i in range(lax.axis_size(TM))])  5.65 us
    pallas_call x1, Pallas kernels, per_device(): pl.pallas_call(functools.partial(forward_kernel, vocab), in_specs=[vmem,...  5 us
    unnamed x9, local copies, waits for them, and re-layouts  3.86 us
  transfers between devices with their start and end apart: 8, of which 7 were waited for; matrix products, arithmetic and copies ran while one was open for 3% of the time, Pallas kernels for 2%

profile of v8, /device:TPU:1, one launch (start us, length us, event | category | flops | bytes accessed | tf_op | source)
XLA Modules:
  0.0 113.4 jit_solution(5213683615286594313)
XLA Ops:
  1.3 0.7 broadcast_in_dim.6
  2.1 19.1 %all-to-all-start = ((bf16[64,8,256]{2,1,0:T(8,128)(2,1)}), bf16[64,8,256]{2,1,0:T(8,128)(2,1)S(1)}, u32[]{:S(2)}, u32[]{:S(2)}) async-start(bf16[64,8,256]{2,1,0:T(8,128)(2,1)} %broadcast_in_dim.6), calls=%async_computation | async-start | bytes 524288 | tf_op jit(solution)/shard_map/all_to_all | solution.py:404
  21.2 0.9 copy.14.pred_ref
  22.1 0.9 copy-done
  24.4 1.9 %shard_map.102 = (bf16[512,2048]{1,0:T(8,128)(2,1)S(1)}, s32[16,128]{1,0:T(8,128)S(1)}) custom-call(s32[2,64]{1,0:T(2,128)S(1)} %copy-done.2, s32[2,64]{1,0:T(2,128)S(1)} %copy-done.1, bf16[128,512]{1,0:T(8,128)(2,1)S(1)} %bitcast.20, bf16[2,65,512]{2,1,0:T(8,128)(2,1)S(1)} %copy.14.pred_ref), custom_call_target="tpu_custom_call" | custom-call | flops 335544320 | bytes 3145728 | tf_op jit(solution)/shard_map/pallas_call | solution.py:433
  26.3 14.0 %all-to-all-done = bf16[64,8,256]{2,1,0:T(8,128)(2,1)S(1)} async-done(((bf16[64,8,256]{2,1,0:T(8,128)(2,1)}), bf16[64,8,256]{2,1,0:T(8,128)(2,1)S(1)}, u32[]{:S(2)}, u32[]{:S(2)}) %all-to-all-start) | async-done | bytes 262176 | tf_op jit(solution)/shard_map/all_to_all | solution.py:404
  40.2 4.8 %collective-permute-start = (bf16[512,256]{1,0:T(8,128)(2,1)S(1)}, bf16[512,256]{1,0:T(8,128)(2,1)S(1)}, u32[]{:S(2)}, u32[]{:S(2)}) collective-permute-start(bf16[512,256]{1,0:T(8,128)(2,1)S(1)} %bitcast.17), channel_id=1, source_target_pairs={{64,0},{0,64},{192,128},{128,192},{320,256},{256,320},{448,384},{3... | collective-permute-start | bytes 786440 | tf_op jit(solution)/shard_map/ppermute | solution.py:413
  45.0 0.8 pad_add_fusion.meta_ref
  46.8 5.0 %shard_map.103 = (f32[512,2048]{1,0:T(8,128)S(1)}, f32[3,16,128]{2,1,0:T(8,128)S(1)}, f32[6,16,16,128]{3,2,1,0:T(8,128)S(1)}, f32[8,128]{1,0:T(8,128)S(1)}) custom-call(s32[2,64]{1,0:T(2,128)S(1)} %copy-done.3, s32[5]{0:T(128)S(1)} %pad_add_fusion.meta_ref, s32[16,128]{1,0:T(8,128)S(1)} %get-tuple-element.17.label_ref, bf16[512,256]{1,0:T(8,128)(2,1)S(1)} %bitcast.18, ...), custom_call_target="tpu_custom_call" | custom-call | flops 1073741824 | bytes 8388608 | tf_op jit(solution)/shard_map/pallas_call | solution.py:458
  51.9 9.4 %all_to_all.20.blocks_ref = f32[8,8,128]{2,1,0:T(8,128)S(1)} all-to-all(f32[8,8,128]{2,1,0:T(8,128)S(1)} %broadcast_in_dim.7), channel_id=1, replica_groups=mesh['tm'=8,'utt'=64] {'tm'}, dimensions={0} | all-to-all | bytes 65536 | tf_op jit(solution)/shard_map/all_to_all | solution.py:404
  61.2 7.6 %shard_map.104 = (f32[2]{0:T(128)}, bf16[128,512]{1,0:T(8,128)(2,1)}, f32[512,256]{1,0:T(8,128)S(1)}, f32[160,256]{1,0:T(8,128)S(1)}, bf16[672,256]{1,0:T(8,128)(2,1)S(1)}) custom-call(s32[2,64]{1,0:T(2,128)S(1)} %copy-done.3, s32[5]{0:T(128)S(1)} %pad_add_fusion.meta_ref, f32[8,8,128]{2,1,0:T(8,128)S(1)} %all_to_all.20.blocks_ref, ...), custom_call_target="tpu_custom_call" | custom-call | flops 3221225472 | bytes 8388608 | tf_op jit(solution)/shard_map/pallas_call | solution.py:480
  68.9 2.6 %collective-permute-start.1 = (bf16[672,256]{1,0:T(8,128)(2,1)S(1)}, bf16[672,256]{1,0:T(8,128)(2,1)S(1)}, u32[]{:S(2)}, u32[]{:S(2)}) collective-permute-start(bf16[672,256]{1,0:T(8,128)(2,1)S(1)} %get-tuple-element.28), channel_id=1, source_target_pairs={{64,0},{0,64},{192,128},{128,192},{320,256},{256,320},{448,384},{3... | collective-permute-start | bytes 1032200 | tf_op jit(solution)/shard_map/ppermute | solution.py:413
  71.5 1.3 %collective-permute-done.1 = bf16[672,256]{1,0:T(8,128)(2,1)S(1)} collective-permute-done((bf16[672,256]{1,0:T(8,128)(2,1)S(1)}, bf16[672,256]{1,0:T(8,128)(2,1)S(1)}, u32[]{:S(2)}, u32[]{:S(2)}) %collective-permute-start.1) | collective-permute-done | bytes 344096 | tf_op jit(solution)/shard_map/ppermute | solution.py:413
  72.8 2.2 %collective-permute-start.2 = (bf16[160,256]{1,0:T(8,128)(2,1)S(1)}, bf16[160,256]{1,0:T(8,128)(2,1)S(1)}, u32[]{:S(2)}, u32[]{:S(2)}) collective-permute-start(bf16[160,256]{1,0:T(8,128)(2,1)S(1)} %fusion.2), channel_id=1, source_target_pairs={{128,0},{192,64},{0,128},{64,192},{384,256},{448,320},{256,384},{3... | collective-permute-start | bytes 245768 | tf_op jit(solution)/shard_map/ppermute | solution.py:413
  75.0 0.8 fusion
  75.8 6.2 %all-to-all-start.2 = ((bf16[64,8,256]{2,1,0:T(8,128)(2,1)}), bf16[64,8,256]{2,1,0:T(8,128)(2,1)S(1)}, u32[]{:S(2)}, u32[]{:S(2)}) async-start(bf16[64,8,256]{2,1,0:T(8,128)(2,1)} %fusion), calls=%async_computation.2 | async-start | bytes 524288 | tf_op jit(solution)/shard_map/all_to_all | solution.py:404
  82.0 3.7 %collective-permute-start.3 = (bf16[160,256]{1,0:T(8,128)(2,1)S(1)}, bf16[160,256]{1,0:T(8,128)(2,1)S(1)}, u32[]{:S(2)}, u32[]{:S(2)}) collective-permute-start(bf16[160,256]{1,0:T(8,128)(2,1)S(1)} %fusion.3), channel_id=1, source_target_pairs={{256,0},{320,64},{384,128},{448,192},{0,256},{64,320},{128,384},{1... | collective-permute-start | bytes 245768 | tf_op jit(solution)/shard_map/ppermute | solution.py:413
  85.7 3.0 %collective-permute-done.3 = bf16[160,256]{1,0:T(8,128)(2,1)S(1)} collective-permute-done((bf16[160,256]{1,0:T(8,128)(2,1)S(1)}, bf16[160,256]{1,0:T(8,128)(2,1)S(1)}, u32[]{:S(2)}, u32[]{:S(2)}) %collective-permute-start.3) | collective-permute-done | bytes 81952 | tf_op jit(solution)/shard_map/ppermute | solution.py:413
  88.7 4.0 %collective-permute-start.4 = (f32[160,256]{1,0:T(8,128)S(1)}, f32[160,256]{1,0:T(8,128)S(1)}, u32[]{:S(2)}, u32[]{:S(2)}) collective-permute-start(f32[160,256]{1,0:T(8,128)S(1)} %convert_add_fusion), channel_id=1, source_target_pairs={{64,0},{0,64},{192,128},{128,192},{320,256},{256,320},{448,384},{3... | collective-permute-start | bytes 491528 | tf_op jit(solution)/shard_map/ppermute | solution.py:413
  92.7 1.0 collective-permute-done.4
  94.4 6.8 %all-to-all-done.2 = bf16[64,8,256]{2,1,0:T(8,128)(2,1)S(1)} async-done(((bf16[64,8,256]{2,1,0:T(8,128)(2,1)}), bf16[64,8,256]{2,1,0:T(8,128)(2,1)S(1)}, u32[]{:S(2)}, u32[]{:S(2)}) %all-to-all-start.2) | async-done | bytes 262176 | tf_op jit(solution)/shard_map/all_to_all | solution.py:404
  101.8 6.1 %all-to-all-start.3 = ((f32[8,8,256]{2,1,0:T(8,128)}), f32[8,8,256]{2,1,0:T(8,128)S(1)}, u32[]{:S(2)}, u32[]{:S(2)}) async-start(f32[8,8,256]{2,1,0:T(8,128)} %broadcast_in_dim.8), calls=%async_computation.3 | async-start | bytes 131072 | tf_op jit(solution)/shard_map/all_to_all | solution.py:404
  107.9 0.8 pad_maximum_fusion
  108.7 4.0 %all-to-all-done.3 = f32[8,8,256]{2,1,0:T(8,128)S(1)} async-done(((f32[8,8,256]{2,1,0:T(8,128)}), f32[8,8,256]{2,1,0:T(8,128)S(1)}, u32[]{:S(2)}, u32[]{:S(2)}) %all-to-all-start.3) | async-done | bytes 65568 | tf_op jit(solution)/shard_map/all_to_all | solution.py:404
  (23 shorter events, 5.1 us)
Async XLA Ops:
  2.1 38.2 %all-to-all-start = ((bf16[64,8,256]{2,1,0:T(8,128)(2,1)}), bf16[64,8,256]{2,1,0:T(8,128)(2,1)S(1)}, u32[]{:S(2)}, u32[]{:S(2)}) async-start(bf16[64,8,256]{2,1,0:T(8,128)(2,1)} %broadcast_in_dim.6), calls=%async_computation | async-start | bytes 524288 | tf_op jit(solution)/shard_map/all_to_all | solution.py:404
  22.1 0.9 copy-start
  23.0 0.7 copy-start.1
  23.7 0.7 copy-start.2
  40.2 5.9 %collective-permute-start = (bf16[512,256]{1,0:T(8,128)(2,1)S(1)}, bf16[512,256]{1,0:T(8,128)(2,1)S(1)}, u32[]{:S(2)}, u32[]{:S(2)}) collective-permute-start(bf16[512,256]{1,0:T(8,128)(2,1)S(1)} %bitcast.17), channel_id=1, source_target_pairs={{64,0},{0,64},{192,128},{128,192},{320,256},{256,320},{448,384},{3... | collective-permute-start | bytes 786440 | tf_op jit(solution)/shard_map/ppermute | solution.py:413
  46.2 0.7 copy-start.3
  68.9 3.9 %collective-permute-start.1 = (bf16[672,256]{1,0:T(8,128)(2,1)S(1)}, bf16[672,256]{1,0:T(8,128)(2,1)S(1)}, u32[]{:S(2)}, u32[]{:S(2)}) collective-permute-start(bf16[672,256]{1,0:T(8,128)(2,1)S(1)} %get-tuple-element.28), channel_id=1, source_target_pairs={{64,0},{0,64},{192,128},{128,192},{320,256},{256,320},{448,384},{3... | collective-permute-start | bytes 1032200 | tf_op jit(solution)/shard_map/ppermute | solution.py:413
  72.8 9.2 %collective-permute-start.2 = (bf16[160,256]{1,0:T(8,128)(2,1)S(1)}, bf16[160,256]{1,0:T(8,128)(2,1)S(1)}, u32[]{:S(2)}, u32[]{:S(2)}) collective-permute-start(bf16[160,256]{1,0:T(8,128)(2,1)S(1)} %fusion.2), channel_id=1, source_target_pairs={{128,0},{192,64},{0,128},{64,192},{384,256},{448,320},{256,384},{3... | collective-permute-start | bytes 245768 | tf_op jit(solution)/shard_map/ppermute | solution.py:413
  75.8 25.4 %all-to-all-start.2 = ((bf16[64,8,256]{2,1,0:T(8,128)(2,1)}), bf16[64,8,256]{2,1,0:T(8,128)(2,1)S(1)}, u32[]{:S(2)}, u32[]{:S(2)}) async-start(bf16[64,8,256]{2,1,0:T(8,128)(2,1)} %fusion), calls=%async_computation.2 | async-start | bytes 524288 | tf_op jit(solution)/shard_map/all_to_all | solution.py:404
  82.0 6.7 %collective-permute-start.3 = (bf16[160,256]{1,0:T(8,128)(2,1)S(1)}, bf16[160,256]{1,0:T(8,128)(2,1)S(1)}, u32[]{:S(2)}, u32[]{:S(2)}) collective-permute-start(bf16[160,256]{1,0:T(8,128)(2,1)S(1)} %fusion.3), channel_id=1, source_target_pairs={{256,0},{320,64},{384,128},{448,192},{0,256},{64,320},{128,384},{1... | collective-permute-start | bytes 245768 | tf_op jit(solution)/shard_map/ppermute | solution.py:413
  88.7 5.0 %collective-permute-start.4 = (f32[160,256]{1,0:T(8,128)S(1)}, f32[160,256]{1,0:T(8,128)S(1)}, u32[]{:S(2)}, u32[]{:S(2)}) collective-permute-start(f32[160,256]{1,0:T(8,128)S(1)} %convert_add_fusion), channel_id=1, source_target_pairs={{64,0},{0,64},{192,128},{128,192},{320,256},{256,320},{448,384},{3... | collective-permute-start | bytes 491528 | tf_op jit(solution)/shard_map/ppermute | solution.py:413
  101.8 10.9 %all-to-all-start.3 = ((f32[8,8,256]{2,1,0:T(8,128)}), f32[8,8,256]{2,1,0:T(8,128)S(1)}, u32[]{:S(2)}, u32[]{:S(2)}) async-start(f32[8,8,256]{2,1,0:T(8,128)} %broadcast_in_dim.8), calls=%async_computation.3 | async-start | bytes 131072 | tf_op jit(solution)/shard_map/all_to_all | solution.py:404

commit v9 on v8

--- a/solution.py
+++ b/solution.py
@@ -99,7 +99,7 @@
     return rows
 
 
-def hidden_kernel(starts_ref, labels_ref, enc_ref, pred_ref, hidden_ref, label_ref, enc_t, pred_t, stack):
+def hidden_kernel(meta_ref, starts_ref, labels_ref, enc_ref, pred_ref, hidden_ref, label_ref, enc_t, pred_t, stack):
     step = pl.program_id(0)
     half = starts_ref.shape[1]
     starts = rows_to_lanes(starts_ref[...])
@@ -434,6 +434,7 @@
         hidden_kernel,
         grid=(STEPS,),
         in_specs=[
+            smem,
             whole(starts.shape),
             whole(labels.shape),
             whole((utt_count * frame_count, width)),
@@ -450,7 +451,7 @@
         cost_estimate=pl.CostEstimate(
             flops=2 * 2 * PRED_PAD * width * rows, bytes_accessed=3 * 2**20, transcendentals=width * rows
         ),
-    )(starts, labels, encoder.reshape(-1, width), predictor)
+    )(meta, starts, labels, encoder.reshape(-1, width), predictor)
 
     own_half, hidden = lax.optimization_barrier((own_half, hidden))
     far_half = tm_flip(own_half, 1)
@@ -506,8 +507,9 @@
 
     came = tm_flip(send, 1)
     weight_half = (weight_own + came[:width].astype(F32)).astype(BF16).reshape(utt_size, own_rows, split)
+    pred_own = pred_own + came[width:].astype(F32)
+    weight_half, pred_own = lax.optimization_barrier((weight_half, pred_own))
     weight_rows = jnp.sum(exchange(weight_half, UTT).astype(F32), axis=0)
-    pred_own = pred_own + came[width:].astype(F32)
     for turn in (2, 4):
         pred_own = pred_own + tm_flip(pred_own.astype(BF16), turn).astype(F32)
     pred_far = tm_flip(pred_own, 1)

time: 114 us -> 114 us (level)
    all_to_all x3, waiting for transfers between devices: 24.8 us -> 23.5 us  [exchange(): return lax.all_to_all(blocks, axes, 0, 0, tiled=True)]
where the time goes in v9:
time: 114 us
  starting transfers between devices  48.7 us (43%)
  waiting for transfers between devices  29.9 us (26%)
  Pallas kernels  15.2 us (13%)
  blocking collectives  9.36 us (8%)
  local copies, waits for them, and re-layouts  6.26 us (5%)
  other arithmetic  3.36 us (3%)
    all_to_all x3, starting transfers between devices, exchange(): return lax.all_to_all(blocks, axes, 0, 0, tiled=True)  31.4 us
    all_to_all x3, waiting for transfers between devices, exchange(): return lax.all_to_all(blocks, axes, 0, 0, tiled=True)  23.5 us
    ppermute x5, starting transfers between devices, tm_flip(): lax.ppermute(block, TM, [(i ^ turn, i) for i in range(lax.axis_size(TM))])  17.3 us
    all_to_all x1, blocking collectives, exchange(): return lax.all_to_all(blocks, axes, 0, 0, tiled=True)  9.36 us
    pallas_call x1, Pallas kernels, per_device(): pl.pallas_call(backward_kernel, in_specs=[vmem, smem] + [vmem] * 8, out_s...  7.68 us
    ppermute x5, waiting for transfers between devices, tm_flip(): lax.ppermute(block, TM, [(i ^ turn, i) for i in range(lax.axis_size(TM))])  6.39 us
    pallas_call x1, Pallas kernels, per_device(): pl.pallas_call(functools.partial(forward_kernel, vocab), in_specs=[vmem,...  5.04 us
    unnamed x9, local copies, waits for them, and re-layouts  3.86 us
  transfers between devices with their start and end apart: 8, of which 7 were waited for; matrix products, arithmetic and copies ran while one was open for 3% of the time, Pallas kernels for 2%

profile of v9, /device:TPU:1, one launch (start us, length us, event | category | flops | bytes accessed | tf_op | source)
XLA Modules:
  0.0 113.5 jit_solution(2229305767587931951)
XLA Ops:
  2.1 19.1 %all-to-all-start = ((bf16[64,8,256]{2,1,0:T(8,128)(2,1)}), bf16[64,8,256]{2,1,0:T(8,128)(2,1)S(1)}, u32[]{:S(2)}, u32[]{:S(2)}) async-start(bf16[64,8,256]{2,1,0:T(8,128)(2,1)} %broadcast_in_dim.6), calls=%async_computation | async-start | bytes 524288 | tf_op jit(solution)/shard_map/all_to_all | solution.py:404
  21.2 0.9 copy.14.pred_ref
  22.1 0.8 pad_add_fusion.meta_ref
  22.9 0.9 copy-done
  25.1 2.5 %shard_map.102 = (bf16[512,2048]{1,0:T(8,128)(2,1)S(1)}, s32[16,128]{1,0:T(8,128)S(1)}) custom-call(s32[5]{0:T(128)S(1)} %pad_add_fusion.meta_ref, s32[2,64]{1,0:T(2,128)S(1)} %copy-done.2, s32[2,64]{1,0:T(2,128)S(1)} %copy-done.1, bf16[128,512]{1,0:T(8,128)(2,1)S(1)} %bitcast.20, bf16[2,65,512]{2,1,0:T(8,128)(2,1)S(1)} %copy.14.pred_ref), custom_call_target="tpu_custom_call" | custom-call | flops 335544320 | bytes 3145728 | tf_op jit(solution)/shard_map/pallas_call | solution.py:433
  27.6 12.6 %all-to-all-done = bf16[64,8,256]{2,1,0:T(8,128)(2,1)S(1)} async-done(((bf16[64,8,256]{2,1,0:T(8,128)(2,1)}), bf16[64,8,256]{2,1,0:T(8,128)(2,1)S(1)}, u32[]{:S(2)}, u32[]{:S(2)}) %all-to-all-start) | async-done | bytes 262176 | tf_op jit(solution)/shard_map/all_to_all | solution.py:404
  40.2 4.8 %collective-permute-start = (bf16[512,256]{1,0:T(8,128)(2,1)S(1)}, bf16[512,256]{1,0:T(8,128)(2,1)S(1)}, u32[]{:S(2)}, u32[]{:S(2)}) collective-permute-start(bf16[512,256]{1,0:T(8,128)(2,1)S(1)} %bitcast.17), channel_id=1, source_target_pairs={{64,0},{0,64},{192,128},{128,192},{320,256},{256,320},{448,384},{3... | collective-permute-start | bytes 786440 | tf_op jit(solution)/shard_map/ppermute | solution.py:413
  45.0 1.1 %collective-permute-done.far_half_ref = bf16[512,256]{1,0:T(8,128)(2,1)S(1)} collective-permute-done((bf16[512,256]{1,0:T(8,128)(2,1)S(1)}, bf16[512,256]{1,0:T(8,128)(2,1)S(1)}, u32[]{:S(2)}, u32[]{:S(2)}) %collective-permute-start) | collective-permute-done | bytes 262176 | tf_op jit(solution)/shard_map/ppermute | solution.py:413
  46.8 5.0 %shard_map.103 = (f32[512,2048]{1,0:T(8,128)S(1)}, f32[3,16,128]{2,1,0:T(8,128)S(1)}, f32[6,16,16,128]{3,2,1,0:T(8,128)S(1)}, f32[8,128]{1,0:T(8,128)S(1)}) custom-call(s32[2,64]{1,0:T(2,128)S(1)} %copy-done.3, s32[5]{0:T(128)S(1)} %pad_add_fusion.meta_ref, s32[16,128]{1,0:T(8,128)S(1)} %get-tuple-element.19.label_ref, bf16[512,256]{1,0:T(8,128)(2,1)S(1)} %bitcast.18, ...), custom_call_target="tpu_custom_call" | custom-call | flops 1073741824 | bytes 8388608 | tf_op jit(solution)/shard_map/pallas_call | solution.py:459
  51.9 9.4 %all_to_all.20.blocks_ref = f32[8,8,128]{2,1,0:T(8,128)S(1)} all-to-all(f32[8,8,128]{2,1,0:T(8,128)S(1)} %broadcast_in_dim.7), channel_id=1, replica_groups=mesh['tm'=8,'utt'=64] {'tm'}, dimensions={0} | all-to-all | bytes 65536 | tf_op jit(solution)/shard_map/all_to_all | solution.py:404
  61.3 7.7 %shard_map.104 = (f32[2]{0:T(128)}, bf16[128,512]{1,0:T(8,128)(2,1)}, f32[512,256]{1,0:T(8,128)S(1)}, f32[160,256]{1,0:T(8,128)S(1)}, bf16[672,256]{1,0:T(8,128)(2,1)S(1)}) custom-call(s32[2,64]{1,0:T(2,128)S(1)} %copy-done.3, s32[5]{0:T(128)S(1)} %pad_add_fusion.meta_ref, f32[8,8,128]{2,1,0:T(8,128)S(1)} %all_to_all.20.blocks_ref, ...), custom_call_target="tpu_custom_call" | custom-call | flops 3221225472 | bytes 8388608 | tf_op jit(solution)/shard_map/pallas_call | solution.py:481
  69.0 2.6 %collective-permute-start.1 = (bf16[672,256]{1,0:T(8,128)(2,1)S(1)}, bf16[672,256]{1,0:T(8,128)(2,1)S(1)}, u32[]{:S(2)}, u32[]{:S(2)}) collective-permute-start(bf16[672,256]{1,0:T(8,128)(2,1)S(1)} %get-tuple-element.30), channel_id=1, source_target_pairs={{64,0},{0,64},{192,128},{128,192},{320,256},{256,320},{448,384},{3... | collective-permute-start | bytes 1032200 | tf_op jit(solution)/shard_map/ppermute | solution.py:413
  71.6 1.3 %collective-permute-done.1 = bf16[672,256]{1,0:T(8,128)(2,1)S(1)} collective-permute-done((bf16[672,256]{1,0:T(8,128)(2,1)S(1)}, bf16[672,256]{1,0:T(8,128)(2,1)S(1)}, u32[]{:S(2)}, u32[]{:S(2)}) %collective-permute-start.1) | collective-permute-done | bytes 344096 | tf_op jit(solution)/shard_map/ppermute | solution.py:413
  72.9 0.8 fusion
  73.7 2.2 %collective-permute-start.2 = (bf16[160,256]{1,0:T(8,128)(2,1)S(1)}, bf16[160,256]{1,0:T(8,128)(2,1)S(1)}, u32[]{:S(2)}, u32[]{:S(2)}) collective-permute-start(bf16[160,256]{1,0:T(8,128)(2,1)S(1)} %convert_element_type.29), channel_id=1, source_target_pairs={{128,0},{192,64},{0,128},{64,192},{384,256},{448,320},{256,384},{3... | collective-permute-start | bytes 245768 | tf_op jit(solution)/shard_map/ppermute | solution.py:413
  75.9 6.2 %all-to-all-start.2 = ((bf16[64,8,256]{2,1,0:T(8,128)(2,1)}), bf16[64,8,256]{2,1,0:T(8,128)(2,1)S(1)}, u32[]{:S(2)}, u32[]{:S(2)}) async-start(bf16[64,8,256]{2,1,0:T(8,128)(2,1)} %fusion), calls=%async_computation.2 | async-start | bytes 524288 | tf_op jit(solution)/shard_map/all_to_all | solution.py:404
  82.1 3.7 %collective-permute-start.3 = (bf16[160,256]{1,0:T(8,128)(2,1)S(1)}, bf16[160,256]{1,0:T(8,128)(2,1)S(1)}, u32[]{:S(2)}, u32[]{:S(2)}) collective-permute-start(bf16[160,256]{1,0:T(8,128)(2,1)S(1)} %fusion.2), channel_id=1, source_target_pairs={{256,0},{320,64},{384,128},{448,192},{0,256},{64,320},{128,384},{1... | collective-permute-start | bytes 245768 | tf_op jit(solution)/shard_map/ppermute | solution.py:413
  85.8 3.0 %collective-permute-done.3 = bf16[160,256]{1,0:T(8,128)(2,1)S(1)} collective-permute-done((bf16[160,256]{1,0:T(8,128)(2,1)S(1)}, bf16[160,256]{1,0:T(8,128)(2,1)S(1)}, u32[]{:S(2)}, u32[]{:S(2)}) %collective-permute-start.3) | collective-permute-done | bytes 81952 | tf_op jit(solution)/shard_map/ppermute | solution.py:413
  88.8 4.0 %collective-permute-start.4 = (f32[160,256]{1,0:T(8,128)S(1)}, f32[160,256]{1,0:T(8,128)S(1)}, u32[]{:S(2)}, u32[]{:S(2)}) collective-permute-start(f32[160,256]{1,0:T(8,128)S(1)} %convert_add_fusion), channel_id=1, source_target_pairs={{64,0},{0,64},{192,128},{128,192},{320,256},{256,320},{448,384},{3... | collective-permute-start | bytes 491528 | tf_op jit(solution)/shard_map/ppermute | solution.py:413
  92.8 1.0 collective-permute-done.4
  94.4 6.8 %all-to-all-done.2 = bf16[64,8,256]{2,1,0:T(8,128)(2,1)S(1)} async-done(((bf16[64,8,256]{2,1,0:T(8,128)(2,1)}), bf16[64,8,256]{2,1,0:T(8,128)(2,1)S(1)}, u32[]{:S(2)}, u32[]{:S(2)}) %all-to-all-start.2) | async-done | bytes 262176 | tf_op jit(solution)/shard_map/all_to_all | solution.py:404
  101.9 6.1 %all-to-all-start.3 = ((f32[8,8,256]{2,1,0:T(8,128)}), f32[8,8,256]{2,1,0:T(8,128)S(1)}, u32[]{:S(2)}, u32[]{:S(2)}) async-start(f32[8,8,256]{2,1,0:T(8,128)} %broadcast_in_dim.8), calls=%async_computation.3 | async-start | bytes 131072 | tf_op jit(solution)/shard_map/all_to_all | solution.py:404
  108.0 0.8 pad_maximum_fusion
  108.8 4.0 %all-to-all-done.3 = f32[8,8,256]{2,1,0:T(8,128)S(1)} async-done(((f32[8,8,256]{2,1,0:T(8,128)}), f32[8,8,256]{2,1,0:T(8,128)S(1)}, u32[]{:S(2)}, u32[]{:S(2)}) %all-to-all-start.3) | async-done | bytes 65568 | tf_op jit(solution)/shard_map/all_to_all | solution.py:404
  (24 shorter events, 5.5 us)
Async XLA Ops:
  2.1 38.2 %all-to-all-start = ((bf16[64,8,256]{2,1,0:T(8,128)(2,1)}), bf16[64,8,256]{2,1,0:T(8,128)(2,1)S(1)}, u32[]{:S(2)}, u32[]{:S(2)}) async-start(bf16[64,8,256]{2,1,0:T(8,128)(2,1)} %broadcast_in_dim.6), calls=%async_computation | async-start | bytes 524288 | tf_op jit(solution)/shard_map/all_to_all | solution.py:404
  22.9 0.9 copy-start
  23.8 0.7 copy-start.1
  24.4 0.7 copy-start.2
  40.2 5.9 %collective-permute-start = (bf16[512,256]{1,0:T(8,128)(2,1)S(1)}, bf16[512,256]{1,0:T(8,128)(2,1)S(1)}, u32[]{:S(2)}, u32[]{:S(2)}) collective-permute-start(bf16[512,256]{1,0:T(8,128)(2,1)S(1)} %bitcast.17), channel_id=1, source_target_pairs={{64,0},{0,64},{192,128},{128,192},{320,256},{256,320},{448,384},{3... | collective-permute-start | bytes 786440 | tf_op jit(solution)/shard_map/ppermute | solution.py:413
  46.2 0.7 copy-start.3
  69.0 3.9 %collective-permute-start.1 = (bf16[672,256]{1,0:T(8,128)(2,1)S(1)}, bf16[672,256]{1,0:T(8,128)(2,1)S(1)}, u32[]{:S(2)}, u32[]{:S(2)}) collective-permute-start(bf16[672,256]{1,0:T(8,128)(2,1)S(1)} %get-tuple-element.30), channel_id=1, source_target_pairs={{64,0},{0,64},{192,128},{128,192},{320,256},{256,320},{448,384},{3... | collective-permute-start | bytes 1032200 | tf_op jit(solution)/shard_map/ppermute | solution.py:413
  73.7 8.4 %collective-permute-start.2 = (bf16[160,256]{1,0:T(8,128)(2,1)S(1)}, bf16[160,256]{1,0:T(8,128)(2,1)S(1)}, u32[]{:S(2)}, u32[]{:S(2)}) collective-permute-start(bf16[160,256]{1,0:T(8,128)(2,1)S(1)} %convert_element_type.29), channel_id=1, source_target_pairs={{128,0},{192,64},{0,128},{64,192},{384,256},{448,320},{256,384},{3... | collective-permute-start | bytes 245768 | tf_op jit(solution)/shard_map/ppermute | solution.py:413
  75.9 25.4 %all-to-all-start.2 = ((bf16[64,8,256]{2,1,0:T(8,128)(2,1)}), bf16[64,8,256]{2,1,0:T(8,128)(2,1)S(1)}, u32[]{:S(2)}, u32[]{:S(2)}) async-start(bf16[64,8,256]{2,1,0:T(8,128)(2,1)} %fusion), calls=%async_computation.2 | async-start | bytes 524288 | tf_op jit(solution)/shard_map/all_to_all | solution.py:404
  82.1 6.7 %collective-permute-start.3 = (bf16[160,256]{1,0:T(8,128)(2,1)S(1)}, bf16[160,256]{1,0:T(8,128)(2,1)S(1)}, u32[]{:S(2)}, u32[]{:S(2)}) collective-permute-start(bf16[160,256]{1,0:T(8,128)(2,1)S(1)} %fusion.2), channel_id=1, source_target_pairs={{256,0},{320,64},{384,128},{448,192},{0,256},{64,320},{128,384},{1... | collective-permute-start | bytes 245768 | tf_op jit(solution)/shard_map/ppermute | solution.py:413
  88.8 5.0 %collective-permute-start.4 = (f32[160,256]{1,0:T(8,128)S(1)}, f32[160,256]{1,0:T(8,128)S(1)}, u32[]{:S(2)}, u32[]{:S(2)}) collective-permute-start(f32[160,256]{1,0:T(8,128)S(1)} %convert_add_fusion), channel_id=1, source_target_pairs={{64,0},{0,64},{192,128},{128,192},{320,256},{256,320},{448,384},{3... | collective-permute-start | bytes 491528 | tf_op jit(solution)/shard_map/ppermute | solution.py:413
  101.9 10.9 %all-to-all-start.3 = ((f32[8,8,256]{2,1,0:T(8,128)}), f32[8,8,256]{2,1,0:T(8,128)S(1)}, u32[]{:S(2)}, u32[]{:S(2)}) async-start(f32[8,8,256]{2,1,0:T(8,128)} %broadcast_in_dim.8), calls=%async_computation.3 | async-start | bytes 131072 | tf_op jit(solution)/shard_map/all_to_all | solution.py:404
